TPU v7x, 32 devices: a whole 2x2x4 slice. The times are simulated.
32 devices in a mesh: vol: 8 (over z, y), rep: 4 (over x, core).
Axes of the slice: x: 2, y: 2, z: 4, core: 2. Of those that a mesh axis runs over, the one named last changes fastest.
Arguments:
- surface_state: float32 [896, 32, 128], P('vol', 'rep'), may hold values from -6 to 6
- direction: float32 [896, 32, 128], P('vol', 'rep'), may hold values from -6 to 6
- stiffness: float32 [896, 128], P('vol'), may hold values from 0.5 to 5
- partners: int32 [896, 4], P('vol'), may hold values from 0 to 895, as said below
- contact_owner: int32 [896], P('vol'), may hold values from 0 to 7, as said below
- projection: float32 [32, 32], replicated, may hold values from -1 to 1
- mortar: float32 [4, 128, 128], replicated, may hold values from -0.5 to 0.5
Outputs:
- hessian_product: float32 [896, 32, 128], P('vol', 'rep')
Inputs may be any that keep to these rules, and one draw needn't show every extreme that they name: `contact_owner`: in the 112 blocks of one volume owner (aligned blocks of rows) no contact owner is named more than 28 times; 1 contact owners are named exactly 28 times in every such block. `partners`: partners may repeat, may be the block itself, and may have another contact owner than their block.
All inputs are finite; a program needn't handle non-finite values.
Results may differ from a plain program's by a relative error of at most 0.0001.
Values sent between devices are 32-bit elements; how exact they have to be, the bound alone decides.
No kernel may reach another device: no remote copies, remote signals or barrier semaphores. Data moves between devices by JAX's collectives and lax.ppermute only.
A program may use at most 64 MiB of HBM per device.

v0:
```python
import jax
import jax.numpy as jnp
from jax import lax
from jax.sharding import PartitionSpec as P

sharpness = 1.5


def local(surface_state, direction, stiffness, partners, contact_owner, projection, mortar):
    highest = lax.Precision.HIGHEST
    vol_count = lax.axis_size("vol")
    rep_index = lax.axis_index("rep")
    vol_index = lax.axis_index("vol")
    blocks, channel_share, face_count = surface_state.shape
    partner_count = partners.shape[1]
    capacity = max(2, (2 * blocks + vol_count - 1) // vol_count)
    slot_count = vol_count * capacity
    my_columns = lax.dynamic_slice_in_dim(projection, rep_index * channel_share, channel_share, 1)
    my_rows = lax.dynamic_slice_in_dim(projection, rep_index * channel_share, channel_share, 0)

    def fold_one(piece):
        return jnp.einsum("ij,bjf->bif", my_rows, piece, precision=highest)

    counter = jnp.arange(blocks, dtype=jnp.int32)
    same_owner = contact_owner[:, None] == contact_owner[None, :]
    earlier = counter[:, None] < counter[None, :]
    bucket_rank = jnp.sum((same_owner & earlier).astype(jnp.int32), axis=0)
    slot_of = contact_owner * capacity + bucket_rank
    slot_iota = jnp.arange(slot_count, dtype=jnp.int32)
    matches = slot_iota[:, None] == slot_of[None, :]
    occupied = jnp.any(matches, axis=1).astype(jnp.float32)
    source_row = jnp.sum(jnp.where(matches, counter[None, :], 0), axis=1)
    global_ids = vol_index * blocks + counter
    labels = jnp.concatenate([(global_ids + 1)[:, None], partners], axis=1).astype(jnp.float32)
    send_stiff = (stiffness[source_row] * occupied[:, None]).reshape(
        vol_count, capacity, face_count
    )
    send_labels = (labels[source_row] * occupied[:, None]).reshape(
        vol_count, capacity, partner_count + 1
    )

    def pack(values):
        return (values[source_row] * occupied[:, None, None]).reshape(
            vol_count, capacity, channel_share, face_count
        )

    projected = fold_one(lax.all_gather(surface_state, "rep", axis=1, tiled=True))
    moving = fold_one(lax.all_gather(direction, "rep", axis=1, tiled=True))
    received = (
        lax.all_to_all(pack(projected), "vol", split_axis=0, concat_axis=0, tiled=True),
        lax.all_to_all(pack(moving), "vol", split_axis=0, concat_axis=0, tiled=True),
        lax.all_to_all(send_stiff, "vol", split_axis=0, concat_axis=0, tiled=True),
        lax.all_to_all(send_labels, "vol", split_axis=0, concat_axis=0, tiled=True),
    )
    got_state = received[0].reshape(slot_count, channel_share, face_count)
    got_move = received[1].reshape(slot_count, channel_share, face_count)
    got_stiff = received[2].reshape(slot_count, face_count)
    got_labels = received[3].reshape(slot_count, partner_count + 1).astype(jnp.int32)
    slot_ids = got_labels[:, 0] - 1
    partner_ids = got_labels[:, 1:]
    partner_source = partner_ids // blocks
    candidates = slot_ids.reshape(vol_count, capacity)[partner_source]
    offsets = jnp.arange(capacity, dtype=jnp.int32)
    matched = candidates == partner_ids[..., None]
    found = jnp.any(matched, axis=2).astype(jnp.float32)
    partner_offset = jnp.sum(jnp.where(matched, offsets, 0), axis=2)
    partner_slot = partner_source * capacity + partner_offset
    mapped_state = jnp.einsum("rcf,kfg->krcg", got_state, mortar, precision=highest)
    weights = []
    for column in range(partner_count):
        target = partner_slot[:, column]
        contact_gap = got_state - mapped_state[column][target]
        squashed = jax.nn.sigmoid(sharpness * contact_gap)
        weights.append(
            found[:, column][:, None, None]
            * got_stiff[:, None, :]
            * sharpness
            * squashed
            * (1.0 - squashed)
        )
    partner_slot, weights = (partner_slot, weights)
    mapped_move = jnp.einsum("rcf,kfg->krcg", got_move, mortar, precision=highest)
    tangent = jnp.zeros_like(got_move)
    returns = []
    for column in range(partner_count):
        target = partner_slot[:, column]
        traction = weights[column] * (got_move - mapped_move[column][target])
        tangent = tangent + traction
        returns.append(jax.ops.segment_sum(traction, target, num_segments=slot_count))
    returned = jnp.einsum("krcg,kfg->rcf", jnp.stack(returns), mortar, precision=highest)
    summed = (tangent - returned).reshape(vol_count, capacity, channel_share, face_count)
    returned_tiles = lax.all_to_all(summed, "vol", split_axis=0, concat_axis=0, tiled=True)
    own_tangent = returned_tiles.reshape(slot_count, channel_share, face_count)[slot_of]
    return jnp.einsum(
        "ji,bjf->bif",
        my_columns,
        lax.all_gather(own_tangent, "rep", axis=1, tiled=True),
        precision=highest,
    )


def solution(mesh):
    placed = (
        P("vol", "rep", None),
        P("vol", "rep", None),
        P("vol", None),
        P("vol", None),
        P("vol"),
        P(),
        P(),
    )
    return jax.shard_map(
        local, mesh=mesh, in_specs=placed, out_specs=P("vol", "rep", None), check_vma=False
    )
```

profile of v0, /device:TPU:0, one launch (start us, length us, event | category | flops | bytes accessed | tf_op | source)
XLA Modules:
  0.0 330.8 jit_solution(8900276318329445976)
XLA Ops:
  12.5 7.3 %all-to-all-start = ((f32[8,1,140]{2,1,0:T(1,128)}), f32[8,1,140]{2,1,0:T(1,128)S(1)}, u32[]{:S(2)}, u32[]{:S(2)}) async-start(f32[8,1,140]{2,1,0:T(1,128)} %reshape.352), calls=%async_computation | async-start | bytes 16384 | tf_op jit(solution)/shard_map/all_to_all | solution.py:53
  22.1 10.9 %all-gather.7.cloned.1.call-done = f32[112,32,128]{2,1,0:T(8,128)} async-done(((f32[112,8,128]{2,1,0:T(8,128)}), f32[112,32,128]{2,1,0:T(8,128)}) %all-gather.7.cloned.1.call-update) | async-done | bytes 1835024 | tf_op jit(solution)/shard_map/all_gather | solution.py:48
  33.0 2.5 convolution_bitcast_fusion.3
  35.5 20.4 %all-gather.5.cloned.1.call-done = f32[112,32,128]{2,1,0:T(8,128)} async-done(((f32[112,8,128]{2,1,0:T(8,128)}), f32[112,32,128]{2,1,0:T(8,128)}) %all-gather.5.cloned.1.call-update) | async-done | bytes 1835024 | tf_op jit(solution)/shard_map/all_gather | solution.py:47
  55.9 2.5 convolution_bitcast_fusion.4
  60.3 5.5 %all-to-all-start.1 = ((f32[8,28,128]{2,1,0:T(8,128)}), f32[8,28,128]{2,1,0:T(8,128)S(1)}, u32[]{:S(2)}, u32[]{:S(2)}) async-start(f32[8,28,128]{2,1,0:T(8,128)} %broadcast_multiply_fusion.2), calls=%async_computation.1 | async-start | bytes 262144 | tf_op jit(solution)/shard_map/all_to_all | solution.py:52
  67.4 5.8 %all-to-all-done.1 = f32[8,28,128]{2,1,0:T(8,128)S(1)} async-done(((f32[8,28,128]{2,1,0:T(8,128)}), f32[8,28,128]{2,1,0:T(8,128)S(1)}, u32[]{:S(2)}, u32[]{:S(2)}) %all-to-all-start.1) | async-done | bytes 114720 | tf_op jit(solution)/shard_map/all_to_all | solution.py:52
  73.3 3.6 %all-to-all-start.3 = ((f32[8,28,8,128]{3,2,1,0:T(8,128)}), f32[8,28,8,128]{3,2,1,0:T(8,128)S(1)}, u32[]{:S(2)}, u32[]{:S(2)}) async-start(f32[8,28,8,128]{3,2,1,0:T(8,128)} %get-tuple-element.38), calls=%async_computation.3 | async-start | bytes 1835008 | tf_op jit(solution)/shard_map/all_to_all | solution.py:51
  80.6 4.2 %fusion.60 = (pred[224,4]{1,0:T(8,128)(4,1)S(1)}, pred[224,4,28]{2,1,0:T(4,128)(4,1)S(1)}) fusion(s32[224,4,28]{2,1,0:T(4,128)S(1)} %bitcast.160, s32[224,4]{1,0:T(8,128)S(1)} %copy.61), kind=kLoop, calls=%fused_computation.140 | loop fusion | flops 49280 | bytes 129920 | tf_op jit(solution)/shard_map/reduce_or | solution.py:65
  84.8 3.8 %select_reduce_fusion = s32[224,4]{1,0:T(8,128)S(1)} fusion(pred[224,4,28]{2,1,0:T(4,128)(4,1)S(1)} %get-tuple-element.20), kind=kLoop, calls=%fused_computation.73 | loop fusion | flops 49280 | bytes 28672 | tf_op jit(solution)/shard_map/reduce_sum | solution.py:66
  88.6 10.5 %all-to-all-done.3 = f32[8,28,8,128]{3,2,1,0:T(8,128)S(1)} async-done(((f32[8,28,8,128]{3,2,1,0:T(8,128)}), f32[8,28,8,128]{3,2,1,0:T(8,128)S(1)}, u32[]{:S(2)}, u32[]{:S(2)}) %all-to-all-start.3) | async-done | bytes 917536 | tf_op jit(solution)/shard_map/all_to_all | solution.py:51
  99.1 3.7 %all-to-all-start.2 = ((f32[8,28,8,128]{3,2,1,0:T(8,128)}), f32[8,28,8,128]{3,2,1,0:T(8,128)S(1)}, u32[]{:S(2)}, u32[]{:S(2)}) async-start(f32[8,28,8,128]{3,2,1,0:T(8,128)} %get-tuple-element.37), calls=%async_computation.2 | async-start | bytes 1835008 | tf_op jit(solution)/shard_map/all_to_all | solution.py:50
  104.0 3.1 convolution_bitcast_fusion
  108.8 17.0 %all-to-all-done.2 = f32[8,28,8,128]{3,2,1,0:T(8,128)S(1)} async-done(((f32[8,28,8,128]{3,2,1,0:T(8,128)}), f32[8,28,8,128]{3,2,1,0:T(8,128)S(1)}, u32[]{:S(2)}, u32[]{:S(2)}) %all-to-all-start.2) | async-done | bytes 917536 | tf_op jit(solution)/shard_map/all_to_all | solution.py:50
  125.8 3.1 convolution_bitcast_fusion.1
  128.9 2.0 slice_bitcast_fusion.7
  130.9 3.0 gather_fusion.11
  133.8 2.9 gather_fusion.12
  136.7 2.8 gather_fusion.7
  139.5 1.9 gather_fusion.8
  143.3 2.9 gather_fusion.9
  148.1 1.9 gather_fusion.6
  150.0 5.1 %fusion.15 = (f32[224,8,128]{2,1,0:T(8,128)S(1)}, f32[224,8,128]{2,1,0:T(8,128)S(1)}, f32[224,8,128]{2,1,0:T(8,128)S(1)}, f32[224,8,128]{2,1,0:T(8,128)}) fusion(f32[224,8,128]{2,1,0:T(8,128)} %gather_fusion.6, f32[8,28,8,128]{3,2,1,0:T(8,128)} %copy-done.1, f32[224,8,128]{2,1,0:T(8,128)} %gather_fusion.4, f32[8,28,8,128]{3,2,1,0:T(8,128)} %copy-done.2, ...), kind=kLoop, calls=%fused_computation.46 | loop fusion | flops 9175040 | bytes 13303808 | tf_op jit(solution)/shard_map/mul | solution.py:87
  156.2 26.4 %scatter_fusion = f32[224,8,128]{2,1,0:T(8,128)} fusion(f32[224,8,128]{2,1,0:T(8,128)} %broadcast.140.clone.3, s32[224]{0:T(256)S(1)} %get-tuple-element.16, f32[224,8,128]{2,1,0:T(8,128)S(1)} %get-tuple-element.29), kind=kCustom, calls=%fused_computation.14 | custom fusion | flops 229376 | bytes 2753408 | tf_op jit(solution)/shard_map/scatter-add | solution.py:89
  183.6 26.5 %scatter_fusion.1 = f32[224,8,128]{2,1,0:T(8,128)} fusion(f32[224,8,128]{2,1,0:T(8,128)} %broadcast.140.clone.2, s32[224]{0:T(256)S(1)} %get-tuple-element.15, f32[224,8,128]{2,1,0:T(8,128)S(1)} %get-tuple-element.30), kind=kCustom, calls=%fused_computation.15 | custom fusion | flops 229376 | bytes 2753408 | tf_op jit(solution)/shard_map/scatter-add | solution.py:89
  211.0 26.9 %scatter_fusion.2 = f32[224,8,128]{2,1,0:T(8,128)} fusion(f32[224,8,128]{2,1,0:T(8,128)} %broadcast.140.clone.1, s32[224]{0:T(256)S(1)} %get-tuple-element.14, f32[224,8,128]{2,1,0:T(8,128)S(1)} %get-tuple-element.31), kind=kCustom, calls=%fused_computation.16 | custom fusion | flops 229376 | bytes 2753408 | tf_op jit(solution)/shard_map/scatter-add | solution.py:89
  238.9 27.1 %scatter_fusion.3 = f32[224,8,128]{2,1,0:T(8,128)} fusion(f32[224,8,128]{2,1,0:T(8,128)} %broadcast.140.clone, s32[224]{0:T(256)S(1)} %get-tuple-element.13, f32[224,8,128]{2,1,0:T(8,128)} %get-tuple-element.32), kind=kCustom, calls=%fused_computation.17 | custom fusion | flops 229376 | bytes 2753408 | tf_op jit(solution)/shard_map/scatter-add | solution.py:89
  266.0 6.2 %fusion.11 = f32[224,8,128]{2,1,0:T(8,128)} fusion(f32[1,224,8,128]{3,2,0,1:T(8,128)} %bitcast.152, f32[1,224,8,128]{3,2,0,1:T(8,128)} %bitcast.155, f32[1,224,8,128]{3,2,0,1:T(8,128)} %bitcast.154, f32[1,224,8,128]{3,2,0,1:T(8,128)} %bitcast.153, f32[224,8,128]{2,1,0:T(8,128)} %get-tuple-element.32, f32[224,8,128]{2,1,0:T(8,128)S(1)} %get-tuple-element.31, ...), kind=kOutput, calls=%fused_computation.29 | convolution fusion | flops 1412956160 | bytes 8519680 | tf_op jit(solution)/shard_map/krcg,kfg->rcf/dot_general | solution.py:90
  272.3 6.0 %all-to-all-start.4 = ((f32[8,28,8,128]{3,2,1,0:T(8,128)}), f32[8,28,8,128]{3,2,1,0:T(8,128)S(1)}, u32[]{:S(2)}, u32[]{:S(2)}) async-start(f32[8,28,8,128]{3,2,1,0:T(8,128)} %bitcast.156), calls=%async_computation.4 | async-start | bytes 1835008 | tf_op jit(solution)/shard_map/all_to_all | solution.py:92
  278.3 21.7 %all-to-all-done.4 = f32[8,28,8,128]{3,2,1,0:T(8,128)S(1)} async-done(((f32[8,28,8,128]{3,2,1,0:T(8,128)}), f32[8,28,8,128]{3,2,1,0:T(8,128)S(1)}, u32[]{:S(2)}, u32[]{:S(2)}) %all-to-all-start.4) | async-done | bytes 917536 | tf_op jit(solution)/shard_map/all_to_all | solution.py:92
  301.5 19.4 %all-gather.9.cloned.1.call-done = f32[112,32,128]{2,1,0:T(8,128)} async-done(((f32[112,8,128]{2,1,0:T(8,128)}), f32[112,32,128]{2,1,0:T(8,128)}) %all-gather.9.cloned.1.call-update) | async-done | bytes 1835024 | tf_op jit(solution)/shard_map/all_gather | solution.py:97
  320.9 3.4 %convolution_bitcast_fusion.2 = f32[112,8,128]{2,1,0:T(8,128)} fusion(f32[112,32,128]{2,1,0:T(8,128)} %all-gather.9.cloned.1.call-done, f32[32,32]{1,0:T(8,128)S(1)} %copy-done.6, s32[]{:T(128)S(6)} %select_n.60), kind=kOutput, calls=%fused_computation.30 | convolution fusion | flops 44040192 | bytes 2297860 | tf_op jit(solution)/shard_map/ji,bjf->bif/dot_general | solution.py:94
  (75 shorter events, 27.5 us)
Async XLA Ops:
  6.5 97.5 %copy-start = (f32[4,128,128]{2,1,0:T(8,128)S(1)}, f32[4,128,128]{2,1,0:T(8,128)}, u32[]{:S(2)}) copy-start(f32[4,128,128]{2,1,0:T(8,128)} %param.13) | copy-start | bytes 786436
  6.5 26.4 %copy-start.6 = (f32[32,32]{1,0:T(8,128)S(1)}, f32[32,32]{1,0:T(8,128)}, u32[]{:S(2)}) copy-start(f32[32,32]{1,0:T(8,128)} %param.12) | copy-start | bytes 12292
  6.5 26.4 %all-gather.7.cloned.1.call-start = ((), (), s32[]{:S(2)}) async-start(), calls=%async_computation.6 | async-start | bytes 2293760 | tf_op jit(solution)/shard_map/all_gather | solution.py:48
  7.3 48.6 %all-gather.5.cloned.1.call-start = ((), (), s32[]{:S(2)}) async-start(), calls=%async_computation.5 | async-start | bytes 2293760 | tf_op jit(solution)/shard_map/all_gather | solution.py:47
  12.5 47.8 %all-to-all-start = ((f32[8,1,140]{2,1,0:T(1,128)}), f32[8,1,140]{2,1,0:T(1,128)S(1)}, u32[]{:S(2)}, u32[]{:S(2)}) async-start(f32[8,1,140]{2,1,0:T(1,128)} %reshape.352), calls=%async_computation | async-start | bytes 16384 | tf_op jit(solution)/shard_map/all_to_all | solution.py:53
  60.3 12.9 %all-to-all-start.1 = ((f32[8,28,128]{2,1,0:T(8,128)}), f32[8,28,128]{2,1,0:T(8,128)S(1)}, u32[]{:S(2)}, u32[]{:S(2)}) async-start(f32[8,28,128]{2,1,0:T(8,128)} %broadcast_multiply_fusion.2), calls=%async_computation.1 | async-start | bytes 262144 | tf_op jit(solution)/shard_map/all_to_all | solution.py:52
  73.3 25.8 %all-to-all-start.3 = ((f32[8,28,8,128]{3,2,1,0:T(8,128)}), f32[8,28,8,128]{3,2,1,0:T(8,128)S(1)}, u32[]{:S(2)}, u32[]{:S(2)}) async-start(f32[8,28,8,128]{3,2,1,0:T(8,128)} %get-tuple-element.38), calls=%async_computation.3 | async-start | bytes 1835008 | tf_op jit(solution)/shard_map/all_to_all | solution.py:51
  99.1 8.0 %copy-start.1 = (f32[8,28,8,128]{3,2,1,0:T(8,128)}, f32[8,28,8,128]{3,2,1,0:T(8,128)S(1)}, u32[]{:S(2)}) copy-start(f32[8,28,8,128]{3,2,1,0:T(8,128)S(1)} %all-to-all-done.3) | copy-start | bytes 2752516
  99.1 26.7 %all-to-all-start.2 = ((f32[8,28,8,128]{3,2,1,0:T(8,128)}), f32[8,28,8,128]{3,2,1,0:T(8,128)S(1)}, u32[]{:S(2)}, u32[]{:S(2)}) async-start(f32[8,28,8,128]{3,2,1,0:T(8,128)} %get-tuple-element.37), calls=%async_computation.2 | async-start | bytes 1835008 | tf_op jit(solution)/shard_map/all_to_all | solution.py:50
  125.8 5.1 %copy-start.2 = (f32[8,28,8,128]{3,2,1,0:T(8,128)}, f32[8,28,8,128]{3,2,1,0:T(8,128)S(1)}, u32[]{:S(2)}) copy-start(f32[8,28,8,128]{3,2,1,0:T(8,128)S(1)} %all-to-all-done.2) | copy-start | bytes 2752516
  130.9 8.7 %copy-start.4 = (f32[224,8,128]{2,1,0:T(8,128)S(1)}, f32[224,8,128]{2,1,0:T(8,128)}, u32[]{:S(2)}) copy-start(f32[224,8,128]{2,1,0:T(8,128)} %get-tuple-element.28) | copy-start | bytes 2752516
  130.9 10.6 %copy-start.3 = (f32[224,8,128]{2,1,0:T(8,128)S(1)}, f32[224,8,128]{2,1,0:T(8,128)}, u32[]{:S(2)}) copy-start(f32[224,8,128]{2,1,0:T(8,128)} %get-tuple-element.27) | copy-start | bytes 2752516
  141.4 4.8 %copy-start.5 = (f32[224,8,128]{2,1,0:T(8,128)S(1)}, f32[224,8,128]{2,1,0:T(8,128)}, u32[]{:S(2)}) copy-start(f32[224,8,128]{2,1,0:T(8,128)} %get-tuple-element.21) | copy-start | bytes 2752516
  272.3 27.7 %all-to-all-start.4 = ((f32[8,28,8,128]{3,2,1,0:T(8,128)}), f32[8,28,8,128]{3,2,1,0:T(8,128)S(1)}, u32[]{:S(2)}, u32[]{:S(2)}) async-start(f32[8,28,8,128]{3,2,1,0:T(8,128)} %bitcast.156), calls=%async_computation.4 | async-start | bytes 1835008 | tf_op jit(solution)/shard_map/all_to_all | solution.py:92
  278.2 42.6 %all-gather.9.cloned.1.call-start = ((), (), s32[]{:S(2)}) async-start(), calls=%async_computation.7 | async-start | bytes 2293760 | tf_op jit(solution)/shard_map/all_gather | solution.py:97
Sparse Core Ops, SparseCore 0:
  8.9 24.0 all-gather.6
  34.5 21.3 all-gather.4
  301.6 19.2 all-gather.8
where the time goes:
time: 336 us; the launch traced here: 331 us
  other arithmetic  127 us (38%)
  waiting for transfers between devices  107 us (32%)
  local copies, waits for them, and re-layouts  36.9 us (11%)
  starting transfers between devices  26.1 us (8%)
  matrix products  20.7 us (6%)
  between operations  13.4 us (4%)
    scatter-add x4, other arithmetic, local(): jax.ops.segment_sum(traction, target, num_segments=slot_count)  107 us
    all_to_all x1, waiting for transfers between devices, local(): lax.all_to_all(summed, 'vol', split_axis=0, concat_axis=0, tiled=True)  21.7 us
    all_gather x1, waiting for transfers between devices, local(): lax.all_gather(surface_state, 'rep', axis=1, tiled=True)  20.4 us
    all_gather x1, waiting for transfers between devices, local(): lax.all_gather(own_tangent, 'rep', axis=1, tiled=True)  19.4 us
    all_to_all x1, waiting for transfers between devices, local(): lax.all_to_all(pack(projected), 'vol', split_axis=0, concat_axis=0, tiled...  17 us
    all_gather x1, waiting for transfers between devices, local(): moving = fold_one(lax.all_gather(direction, 'rep', axis=1, tiled=True))  10.9 us
    gather x4, local copies, waits for them, and re-layouts, local(): contact_gap = got_state - mapped_state[column][target]  10.5 us
    all_to_all x1, waiting for transfers between devices, local(): lax.all_to_all(pack(moving), 'vol', split_axis=0, concat_axis=0, tiled=True)  10.5 us
  transfers between devices with their start and end apart: 8, of which 7 were waited for; matrix products, arithmetic and copies ran while one was open for 10% of the time, Pallas kernels for 0%

commit v1 on v0

--- a/solution.py
+++ b/solution.py
@@ -1,12 +1,233 @@
+import functools
+
 import jax
 import jax.numpy as jnp
 from jax import lax
+from jax.experimental import pallas as pl
+from jax.experimental.pallas import tpu as pltpu
 from jax.sharding import PartitionSpec as P
 
 sharpness = 1.5
-
-
-def local(surface_state, direction, stiffness, partners, contact_owner, projection, mortar):
+LANES = 128
+ROWS = 8
+
+
+def halves(value):
+    high = value.astype(jnp.bfloat16)
+    low = (value - high.astype(jnp.float32)).astype(jnp.bfloat16)
+    return high, low
+
+
+def product(a, b):
+    return jnp.dot(a, b, preferred_element_type=jnp.float32)
+
+
+def product3(a, b):
+    return product(a[0], b[0]) + product(a[1], b[0]) + product(a[0], b[1])
+
+
+def iota(shape, dim):
+    return lax.broadcasted_iota(jnp.int32, shape, dim)
+
+
+def one_where(cond):
+    return jnp.where(cond, 1.0, 0.0).astype(jnp.bfloat16)
+
+
+def mixer(projection, rep_index, rep_count, share, group, pack):
+    channels = projection.shape[0]
+    inner = group // pack
+    size = channels * group
+    row = iota((size, channels), 0)
+    spread = one_where(row // group == iota((size, channels), 1))
+    col = iota((channels, size), 1)
+    d = col // (group * share)
+    j = (rep_index ^ d) * share + col % share
+    pick = one_where(iota((channels, size), 0) == j)
+    r = iota((size, size), 0)
+    c = iota((size, size), 1)
+    row_slot = r % group
+    col_slot = ((c // share) % inner) * pack + (c // (share * inner)) % pack
+    keep = row_slot == col_slot
+    out = []
+    for part in halves(projection):
+        wide = product(product(spread, part).astype(jnp.bfloat16), pick)
+        out.append(jnp.where(keep, wide, 0.0).astype(jnp.bfloat16))
+    return out
+
+
+def project_kernel(rep_count, share, place_ref, projection_ref, *refs):
+    out_ref = refs[-1]
+    state_refs, move_refs = refs[:rep_count], refs[rep_count : 2 * rep_count]
+    channels, rows, faces = out_ref.shape
+    group = ROWS
+    per = group // 2 * share
+    mix = mixer(projection_ref[...], place_ref[0], rep_count, share, group, 2)
+    for g in range(rows // group):
+        span = pl.ds(g * per, per)
+        pieces = []
+        for d in range(rep_count):
+            pieces += [state_refs[d][span, :], move_refs[d][span, :]]
+        values = halves(jnp.concatenate(pieces, axis=0))
+        out = product3(mix, values)
+        out_ref[:, pl.ds(g * group, group), :] = out.reshape(channels, group, faces)
+
+
+def back_kernel(rep_count, share, place_ref, projection_ref, summed_ref, out_ref):
+    channels, padded, faces = summed_ref.shape
+    group = ROWS
+    size = channels * group
+    mix = mixer(projection_ref[...], place_ref[0], rep_count, share, group, 1)
+    mix = [m.T for m in mix]
+    rows = out_ref.shape[1]
+    for g in range(padded // group):
+        values = halves(summed_ref[:, pl.ds(g * group, group), :].reshape(size, faces))
+        out = product3(mix, values).reshape(rep_count, group * share, faces)
+        count = min(group * share, rows - g * group * share)
+        out_ref[:, pl.ds(g * group * share, count), :] = out[:, :count]
+
+
+def contact_kernel(
+    order, blocks, partner_count, place_ref, packed_ref, notes_ref, mortar_ref, out_ref,
+    stiff_ref, columns_ref, rows_ref, mapped_ref, hot_ref, back_ref, acc_ref, tangent_ref,
+):
+    total, faces = stiff_ref.shape
+    me = place_ref[0]
+    for at, d in enumerate(order):
+        start = pl.multiple_of((me ^ d) * blocks, ROWS)
+        stiff_ref[pl.ds(start, blocks), :] = notes_ref[at, 0:blocks, :]
+        small = notes_ref[at, blocks : blocks + ROWS, :]
+        square = jnp.concatenate([small, jnp.zeros((LANES - ROWS, LANES), jnp.float32)], axis=0)
+        columns_ref[pl.ds(start, blocks), :] = square.T[:blocks]
+    for t in range(total // LANES):
+        rows_ref[:, t * LANES : (t + 1) * LANES] = columns_ref[t * LANES : (t + 1) * LANES, :].T[:ROWS]
+
+    state = packed_ref[pl.ds(0, total, stride=2), :]
+    move = packed_ref[pl.ds(1, total, stride=2), :]
+    state_parts, move_parts = halves(state), halves(move)
+    tangent_ref[...] = jnp.zeros_like(tangent_ref)
+    acc_ref[...] = jnp.zeros_like(acc_ref)
+    owner_row = rows_ref[partner_count : partner_count + 1, :]
+    owner_column = columns_ref[:, partner_count : partner_count + 1]
+
+    for k in range(partner_count):
+        mortar = halves(mortar_ref[k])
+        for part, parts in enumerate((state_parts, move_parts)):
+            high, low = halves(product3(parts, mortar))
+            mapped_ref[0, :, part * faces : (part + 1) * faces] = high
+            mapped_ref[1, :, part * faces : (part + 1) * faces] = low
+        target = columns_ref[:, k : k + 1]
+        named = iota((total, total), 1).astype(jnp.float32) == target
+        hot_ref[...] = one_where(named)
+        partner_owner = jnp.sum(jnp.where(named, owner_row, 0.0), axis=1, keepdims=True)
+        agree = (partner_owner == owner_column).astype(jnp.float32)
+        gathered = product(hot_ref[...], mapped_ref[0]) + product(hot_ref[...], mapped_ref[1])
+        gap = packed_ref[pl.ds(0, total, stride=2), :] - gathered[:, :faces]
+        change = packed_ref[pl.ds(1, total, stride=2), :] - gathered[:, faces:]
+        small = jnp.exp(-sharpness * jnp.abs(gap))
+        slope = small / ((1.0 + small) * (1.0 + small))
+        traction = stiff_ref[...] * (agree * sharpness) * slope * change
+        tangent_ref[...] += traction
+        back = product3(halves(traction), halves(mortar_ref[k].T))
+        high, low = halves(back)
+        back_ref[:, :faces] = high
+        back_ref[:, faces:] = low
+        hot_ref[...] = one_where(iota((total, total), 0).astype(jnp.float32) == rows_ref[k : k + 1, :])
+        acc_ref[...] += product(hot_ref[...], back_ref[...])
+
+    tangent_ref[...] = tangent_ref[...] - acc_ref[:, :faces] - acc_ref[:, faces:]
+    devices, padded, _ = out_ref.shape
+    slab = total // devices
+    for device in range(devices):
+        out_ref[device, 0:slab, :] = tangent_ref[device * slab : (device + 1) * slab, :]
+        if padded > slab:
+            out_ref[device, slab:padded, :] = jnp.zeros((padded - slab, faces), jnp.float32)
+
+
+def spread_local(surface_state, direction, stiffness, partners, contact_owner, projection, mortar):
+    vol_count, rep_count = lax.axis_size("vol"), lax.axis_size("rep")
+    devices = vol_count * rep_count
+    vol_index, rep_index = lax.axis_index("vol"), lax.axis_index("rep")
+    blocks, share, faces = surface_state.shape
+    channels = projection.shape[0]
+    partner_count = partners.shape[1]
+    slab = blocks // rep_count
+    padded = -(-slab // ROWS) * ROWS
+    total = blocks * vol_count
+    vmem = pl.BlockSpec(memory_space=pltpu.VMEM)
+    smem = pl.BlockSpec(memory_space=pltpu.SMEM)
+    rep_place = rep_index.astype(jnp.int32)[None]
+    vol_place = vol_index.astype(jnp.int32)[None]
+    params = pltpu.CompilerParams(vmem_limit_bytes=48 * 1024 * 1024)
+
+    small = jnp.concatenate([partners.T, contact_owner[None, :]], axis=0).astype(jnp.float32)
+    small = jnp.pad(small, ((0, ROWS - partner_count - 1), (0, faces - blocks)))
+    notes = jnp.concatenate([stiffness, small], axis=0)[None]
+    order = [0]
+    step = vol_count // 2
+    while step:
+        other = lax.ppermute(notes, "vol", [(i, i ^ step) for i in range(vol_count)])
+        notes = jnp.concatenate([notes, other], axis=0)
+        order += [d ^ step for d in order]
+        step //= 2
+
+    def slabs(values):
+        return [
+            lax.dynamic_slice_in_dim(values, (rep_index ^ d) * slab, slab, 0).reshape(slab * share, faces)
+            for d in range(rep_count)
+        ]
+
+    def exchange(pieces):
+        return pieces[:1] + [
+            lax.ppermute(pieces[d], "rep", [(i, i ^ d) for i in range(rep_count)])
+            for d in range(1, rep_count)
+        ]
+
+    both = [jnp.stack(pair) for pair in zip(slabs(surface_state), slabs(direction))]
+    both = exchange(both)
+    sent = pl.pallas_call(
+        functools.partial(project_kernel, rep_count, share),
+        out_shape=jax.ShapeDtypeStruct((channels, 2 * slab, faces), jnp.float32),
+        in_specs=[smem] + [vmem] * (1 + 2 * rep_count),
+        out_specs=vmem,
+        compiler_params=params,
+    )(rep_place, projection, *[b[0] for b in both], *[b[1] for b in both])
+    packed = lax.all_to_all(sent, ("vol", "rep"), 0, 0, tiled=True).reshape(2 * total, faces)
+
+    summed = pl.pallas_call(
+        functools.partial(contact_kernel, tuple(order), blocks, partner_count),
+        out_shape=jax.ShapeDtypeStruct((devices, padded, faces), jnp.float32),
+        in_specs=[smem, vmem, vmem, vmem],
+        out_specs=vmem,
+        scratch_shapes=[
+            pltpu.VMEM((total, faces), jnp.float32),
+            pltpu.VMEM((total, LANES), jnp.float32),
+            pltpu.VMEM((ROWS, total), jnp.float32),
+            pltpu.VMEM((2, total, 2 * faces), jnp.bfloat16),
+            pltpu.VMEM((total, total), jnp.bfloat16),
+            pltpu.VMEM((total, 2 * faces), jnp.bfloat16),
+            pltpu.VMEM((total, 2 * faces), jnp.float32),
+            pltpu.VMEM((total, faces), jnp.float32),
+        ],
+        compiler_params=params,
+    )(vol_place, packed, notes, mortar)
+    returned = lax.all_to_all(summed, ("vol", "rep"), 0, 0, tiled=True)
+
+    pieces = pl.pallas_call(
+        functools.partial(back_kernel, rep_count, share),
+        out_shape=jax.ShapeDtypeStruct((rep_count, slab * share, faces), jnp.float32),
+        in_specs=[smem, vmem, vmem],
+        out_specs=vmem,
+        compiler_params=params,
+    )(rep_place, projection, returned)
+    pieces = exchange([pieces[d] for d in range(rep_count)])
+    out = jnp.zeros((blocks * share, faces), jnp.float32)
+    for d in range(rep_count):
+        out = lax.dynamic_update_slice_in_dim(out, pieces[d], (rep_index ^ d) * slab * share, 0)
+    return out.reshape(blocks, share, faces)
+
+
+def routed_local(surface_state, direction, stiffness, partners, contact_owner, projection, mortar):
     highest = lax.Precision.HIGHEST
     vol_count = lax.axis_size("vol")
     rep_index = lax.axis_index("rep")
@@ -99,6 +320,23 @@
     )
 
 
+def one_channel_each(mesh, state_shape, partner_shape):
+    vol_count, rep_count = mesh.shape["vol"], mesh.shape["rep"]
+    total, channels, faces = state_shape
+    blocks = total // vol_count
+    powers = all(n & (n - 1) == 0 for n in (vol_count, rep_count))
+    return (
+        powers
+        and channels == vol_count * rep_count
+        and channels // rep_count == ROWS
+        and faces == LANES
+        and blocks <= faces
+        and blocks % (ROWS // 2 * rep_count) == 0
+        and total % LANES == 0
+        and partner_shape[1] < ROWS
+    )
+
+
 def solution(mesh):
     placed = (
         P("vol", "rep", None),
@@ -109,6 +347,12 @@
         P(),
         P(),
     )
-    return jax.shard_map(
-        local, mesh=mesh, in_specs=placed, out_specs=P("vol", "rep", None), check_vma=False
-    )
+
+    def program(surface_state, direction, stiffness, partners, *rest):
+        fits = one_channel_each(mesh, surface_state.shape, partners.shape)
+        plan = spread_local if fits else routed_local
+        return jax.shard_map(
+            plan, mesh=mesh, in_specs=placed, out_specs=P("vol", "rep", None), check_vma=False
+        )(surface_state, direction, stiffness, partners, *rest)
+
+    return program

time: 336 us -> 110 us (0.33); the launches traced: 331 us -> 109 us
  other arithmetic: 127 us -> 0.13 us
  waiting for transfers between devices: 107 us -> 63.7 us
  local copies, waits for them, and re-layouts: 36.9 us -> 3.58 us
  Pallas kernels: 0 us -> 20.8 us
  matrix products: 20.7 us -> 0 us
  between operations: 13.4 us -> 0.24 us
  starting transfers between devices: 26.1 us -> 21 us
    scatter-add x4 -> x0, other arithmetic: 107 us -> none  [local(): jax.ops.segment_sum(traction, target, num_segments=slot_count)]
    all_gather x3 -> x0, waiting for transfers between devices: 50.7 us -> none  [the longest x1 20.4 us: local(): lax.all_gather(surface_state, 'rep', axis=1, tiled=True)]
    ppermute x0 -> x9, waiting for transfers between devices: none -> 48.1 us  [the longest x3 32.3 us: spread_local(): lax.ppermute(notes, 'vol', [(i, i ^ step) for i in range(vol_count)])]
    all_to_all x5 -> x2, waiting for transfers between devices: 55 us -> 15.5 us  [the longest x1 15.5 us: spread_local(): returned = lax.all_to_all(summed, ('vol', 'rep'), 0, 0, tiled=True)]
    gather x17 -> x0, local copies, waits for them, and re-layouts: 26.9 us -> none  [the longest x4 10.5 us: local(): contact_gap = got_state - mapped_state[column][target]]
    pallas_call x0 -> x3, Pallas kernels: none -> 20.8 us  [the longest x1 17.7 us: spread_local(): pl.pallas_call(functools.partial(contact_kernel, tuple(order), blocks, pa...]
    dot_general x6 -> x0, matrix products: 20.7 us -> none  [the longest x1 6.23 us: local(): jnp.einsum('krcg,kfg->rcf', jnp.stack(returns), mortar, precision=highest)]
    all_to_all x5 -> x2, starting transfers between devices: 26 us -> 11.4 us  [the longest x1 6.66 us: spread_local(): lax.all_to_all(sent, ('vol', 'rep'), 0, 0, tiled=True)]
  transfers between devices with their start and end apart: 8 -> 11, of which waited for: 7 -> 8; matrix products, arithmetic and copies ran while one was open for 10% -> 0% of each run, Pallas kernels for 0% -> 0%
where the time goes in v1:
time: 110 us; the launch traced here: 109 us
  waiting for transfers between devices  63.7 us (58%)
  starting transfers between devices  21 us (19%)
  Pallas kernels  20.8 us (19%)
  local copies, waits for them, and re-layouts  3.58 us (3%)
    ppermute x3, waiting for transfers between devices, spread_local(): lax.ppermute(notes, 'vol', [(i, i ^ step) for i in range(vol_count)])  32.3 us
    pallas_call x1, Pallas kernels, spread_local(): pl.pallas_call(functools.partial(contact_kernel, tuple(order), blocks, pa...  17.7 us
    ppermute x6, waiting for transfers between devices, exchange(): lax.ppermute(pieces[d], 'rep', [(i, i ^ d) for i in range(rep_count)])  15.8 us
    all_to_all x1, waiting for transfers between devices, spread_local(): returned = lax.all_to_all(summed, ('vol', 'rep'), 0, 0, tiled=True)  15.5 us
    all_to_all x1, starting transfers between devices, spread_local(): lax.all_to_all(sent, ('vol', 'rep'), 0, 0, tiled=True)  6.66 us
    ppermute x6, starting transfers between devices, exchange(): lax.ppermute(pieces[d], 'rep', [(i, i ^ d) for i in range(rep_count)])  5.2 us
    all_to_all x1, starting transfers between devices, spread_local(): returned = lax.all_to_all(summed, ('vol', 'rep'), 0, 0, tiled=True)  4.78 us
    ppermute x3, starting transfers between devices, spread_local(): lax.ppermute(notes, 'vol', [(i, i ^ step) for i in range(vol_count)])  4.35 us
  transfers between devices with their start and end apart: 11, of which 8 were waited for; matrix products, arithmetic and copies ran while one was open for 0% of the time, Pallas kernels for 0%

profile of v1, /device:TPU:0, one launch (start us, length us, event | category | flops | bytes accessed | tf_op | source)
XLA Modules:
  0.0 109.4 jit_solution(3216546691282319770)
XLA Ops:
  0.0 1.1 %dynamic-slice_bitcast_fusion = (f32[224,128]{1,0:T(8,128)S(1)}, f32[1,224,128]{2,1,0:T(8,128)S(1)}, f32[1,224,128]{2,1,0:T(8,128)S(1)}, f32[1,224,128]{2,1,0:T(8,128)S(1)}) fusion(f32[112,8,128]{2,1,0:T(8,128)} %param.8, s32[]{:T(128)S(6)} %select_n.28, s32[]{:T(128)S(6)} %select_n.30, s32[]{:T(128)S(6)} %select_n.29, s32[]{:T(128)S(6)} %select_n.31), kind=kLoop, calls=%fused_computation.17 | loop fusion | bytes 917520 | tf_op jit(solution)/shard_map/squeeze;stack;reshape | solution.py:194
  1.2 0.1 copy-done.2
  1.3 2.4 %collective-permute-start.2 = (f32[2,224,128]{2,1,0:T(8,128)S(1)}, f32[2,224,128]{2,1,0:T(8,128)S(1)}, u32[]{:S(2)}, u32[]{:S(2)}) collective-permute-start(f32[2,224,128]{2,1,0:T(8,128)S(1)} %pad_maximum_fusion.4), channel_id=1, source_target_pairs={{0,3},{1,2},{2,1},{3,0},{4,7},{5,6},{6,5},{7,4},{8,11},{9,10},{10,... | collective-permute-start | bytes 688136 | tf_op jit(solution)/shard_map/ppermute | solution.py:182
  3.8 0.6 collective-permute-start.1
  4.4 0.2 collective-permute-start
  4.6 5.1 %collective-permute-done.2 = f32[2,224,128]{2,1,0:T(8,128)S(1)} collective-permute-done((f32[2,224,128]{2,1,0:T(8,128)S(1)}, f32[2,224,128]{2,1,0:T(8,128)S(1)}, u32[]{:S(2)}, u32[]{:S(2)}) %collective-permute-start.2) | collective-permute-done | bytes 229408 | tf_op jit(solution)/shard_map/ppermute | solution.py:182
  9.8 5.1 %collective-permute-done.1 = f32[2,224,128]{2,1,0:T(8,128)S(1)} collective-permute-done((f32[2,224,128]{2,1,0:T(8,128)S(1)}, f32[2,224,128]{2,1,0:T(8,128)S(1)}, u32[]{:S(2)}, u32[]{:S(2)}) %collective-permute-start.1) | collective-permute-done | bytes 229408 | tf_op jit(solution)/shard_map/ppermute | solution.py:182
  14.8 0.0 collective-permute-done
  14.9 0.0 copy-start.1
  14.9 0.7 copy-done.1
  15.6 2.1 %shard_map.73 = f32[32,56,128]{2,1,0:T(8,128)} custom-call(s32[1]{0:T(128)} %bitcast.place_ref, f32[32,32]{1,0:T(8,128)S(1)} %copy-done.1, f32[224,128]{1,0:T(8,128)S(1)} %get-tuple-element.14.refs_0_, f32[224,128]{1,0:T(8,128)S(1)} %get-tuple-element.21.refs_1_, f32[224,128]{1,0:T(8,128)S(1)} %get-tuple-element.19.refs_2_, ...), custom_call_target="tpu_custom_call" | custom-call | tf_op jit(solution)/shard_map/pallas_call | solution.py:188
  17.7 6.7 %all-to-all-start = ((f32[32,56,128]{2,1,0:T(8,128)}), f32[32,56,128]{2,1,0:T(8,128)S(1)}, u32[]{:S(2)}, u32[]{:S(2)}) async-start(f32[32,56,128]{2,1,0:T(8,128)} %shard_map.73), calls=%async_computation | async-start | bytes 1835008 | tf_op jit(solution)/shard_map/all_to_all | solution.py:195
  24.4 0.0 copy-start.5
  24.4 0.0 copy-start.6
  24.4 0.7 copy-done.5
  25.1 2.7 %collective-permute-start.3 = (f32[1,120,128]{2,1,0:T(8,128)S(1)}, f32[1,120,128]{2,1,0:T(8,128)S(1)}, u32[]{:S(2)}, u32[]{:S(2)}) collective-permute-start(f32[1,120,128]{2,1,0:T(8,128)S(1)} %fusion.1), channel_id=1, source_target_pairs={{0,16},{4,20},{8,24},{12,28},{16,0},{20,4},{24,8},{28,12},{1,17},{... | collective-permute-start | bytes 184328 | tf_op jit(solution)/shard_map/ppermute | solution.py:169
  27.9 22.6 %collective-permute-done.3 = f32[1,120,128]{2,1,0:T(8,128)S(1)} collective-permute-done((f32[1,120,128]{2,1,0:T(8,128)S(1)}, f32[1,120,128]{2,1,0:T(8,128)S(1)}, u32[]{:S(2)}, u32[]{:S(2)}) %collective-permute-start.3) | collective-permute-done | bytes 61472 | tf_op jit(solution)/shard_map/ppermute | solution.py:169
  50.5 0.1 collective-permute-start.4
  50.5 4.9 %collective-permute-done.4 = f32[2,120,128]{2,1,0:T(8,128)S(1)} collective-permute-done((f32[2,120,128]{2,1,0:T(8,128)S(1)}, f32[2,120,128]{2,1,0:T(8,128)S(1)}, u32[]{:S(2)}, u32[]{:S(2)}) %collective-permute-start.4) | collective-permute-done | bytes 122912 | tf_op jit(solution)/shard_map/ppermute | solution.py:169
  55.4 1.5 %collective-permute-start.5 = (f32[4,120,128]{2,1,0:T(8,128)S(1)}, f32[4,120,128]{2,1,0:T(8,128)S(1)}, u32[]{:S(2)}, u32[]{:S(2)}) collective-permute-start(f32[4,120,128]{2,1,0:T(8,128)S(1)} %pad_maximum_fusion.1), channel_id=1, source_target_pairs={{0,4},{4,0},{8,12},{12,8},{16,20},{20,16},{24,28},{28,24},{1,5},{5... | collective-permute-start | bytes 737288 | tf_op jit(solution)/shard_map/ppermute | solution.py:169
  57.0 4.9 %collective-permute-done.5 = f32[4,120,128]{2,1,0:T(8,128)S(1)} collective-permute-done((f32[4,120,128]{2,1,0:T(8,128)S(1)}, f32[4,120,128]{2,1,0:T(8,128)S(1)}, u32[]{:S(2)}, u32[]{:S(2)}) %collective-permute-start.5) | collective-permute-done | bytes 245792 | tf_op jit(solution)/shard_map/ppermute | solution.py:169
  61.9 17.7 %shard_map.74 = f32[32,32,128]{2,1,0:T(8,128)} custom-call(s32[1]{0:T(128)} %bitcast.1.place_ref, f32[1792,128]{1,0:T(8,128)S(1)} %bitcast.46, f32[8,120,128]{2,1,0:T(8,128)S(1)} %pad_maximum_fusion.notes_ref, f32[4,128,128]{2,1,0:T(8,128)S(1)} %copy-done), custom_call_target="tpu_custom_call" | custom-call | tf_op jit(solution)/shard_map/pallas_call | solution.py:197
  79.6 4.8 %all-to-all-start.1 = ((f32[32,32,128]{2,1,0:T(8,128)}), f32[32,32,128]{2,1,0:T(8,128)S(1)}, u32[]{:S(2)}, u32[]{:S(2)}) async-start(f32[32,32,128]{2,1,0:T(8,128)} %shard_map.74), calls=%async_computation.1 | async-start | bytes 1048576 | tf_op jit(solution)/shard_map/all_to_all | solution.py:214
  84.4 15.5 %all-to-all-done.1.summed_ref = f32[32,32,128]{2,1,0:T(8,128)S(1)} async-done(((f32[32,32,128]{2,1,0:T(8,128)}), f32[32,32,128]{2,1,0:T(8,128)S(1)}, u32[]{:S(2)}, u32[]{:S(2)}) %all-to-all-start.1) | async-done | bytes 524320 | tf_op jit(solution)/shard_map/all_to_all | solution.py:214
  100.0 0.9 shard_map.75
  100.9 0.1 collective-permute-start.6
  101.0 1.3 %collective-permute-start.7 = (f32[224,128]{1,0:T(8,128)S(1)}, f32[224,128]{1,0:T(8,128)S(1)}, u32[]{:S(2)}, u32[]{:S(2)}) collective-permute-start(f32[224,128]{1,0:T(8,128)S(1)} %get-tuple-element.6), channel_id=1, source_target_pairs={{0,2},{1,3},{2,0},{3,1},{4,6},{5,7},{6,4},{7,5},{8,10},{9,11},{10,... | collective-permute-start | bytes 344072 | tf_op jit(solution)/shard_map/ppermute | solution.py:182
  102.3 0.6 collective-permute-start.8
  103.0 4.1 %collective-permute-done.7 = f32[224,128]{1,0:T(8,128)S(1)} collective-permute-done((f32[224,128]{1,0:T(8,128)S(1)}, f32[224,128]{1,0:T(8,128)S(1)}, u32[]{:S(2)}, u32[]{:S(2)}) %collective-permute-start.7) | collective-permute-done | bytes 114720 | tf_op jit(solution)/shard_map/ppermute | solution.py:182
  107.0 1.5 %collective-permute-done.8 = f32[224,128]{1,0:T(8,128)S(1)} collective-permute-done((f32[224,128]{1,0:T(8,128)S(1)}, f32[224,128]{1,0:T(8,128)S(1)}, u32[]{:S(2)}, u32[]{:S(2)}) %collective-permute-start.8) | collective-permute-done | bytes 114720 | tf_op jit(solution)/shard_map/ppermute | solution.py:182
  108.6 0.0 copy-start.3
  108.6 0.8 copy-done.3
  (26 shorter events, 0.3 us)
Async XLA Ops:
  0.0 1.2 %copy-start.2 = (f32[112,8,128]{2,1,0:T(8,128)S(1)}, f32[112,8,128]{2,1,0:T(8,128)}, u32[]{:S(2)}) copy-start(f32[112,8,128]{2,1,0:T(8,128)} %param.7) | copy-start | bytes 1376260
  1.3 8.4 %collective-permute-start.2 = (f32[2,224,128]{2,1,0:T(8,128)S(1)}, f32[2,224,128]{2,1,0:T(8,128)S(1)}, u32[]{:S(2)}, u32[]{:S(2)}) collective-permute-start(f32[2,224,128]{2,1,0:T(8,128)S(1)} %pad_maximum_fusion.4), channel_id=1, source_target_pairs={{0,3},{1,2},{2,1},{3,0},{4,7},{5,6},{6,5},{7,4},{8,11},{9,10},{10,... | collective-permute-start | bytes 688136 | tf_op jit(solution)/shard_map/ppermute | solution.py:182
  3.8 11.1 %collective-permute-start.1 = (f32[2,224,128]{2,1,0:T(8,128)S(1)}, f32[2,224,128]{2,1,0:T(8,128)S(1)}, u32[]{:S(2)}, u32[]{:S(2)}) collective-permute-start(f32[2,224,128]{2,1,0:T(8,128)S(1)} %pad_maximum_fusion.3), channel_id=1, source_target_pairs={{0,2},{1,3},{2,0},{3,1},{4,6},{5,7},{6,4},{7,5},{8,10},{9,11},{10,... | collective-permute-start | bytes 688136 | tf_op jit(solution)/shard_map/ppermute | solution.py:182
  4.4 10.4 %collective-permute-start = (f32[2,224,128]{2,1,0:T(8,128)S(1)}, f32[2,224,128]{2,1,0:T(8,128)S(1)}, u32[]{:S(2)}, u32[]{:S(2)}) collective-permute-start(f32[2,224,128]{2,1,0:T(8,128)S(1)} %pad_maximum_fusion.2), channel_id=1, source_target_pairs={{0,1},{1,0},{2,3},{3,2},{4,5},{5,4},{6,7},{7,6},{8,9},{9,8},{10,11... | collective-permute-start | bytes 688136 | tf_op jit(solution)/shard_map/ppermute | solution.py:182
  14.9 0.7 copy-start.1
  17.7 7.4 %copy-start.4 = (f32[112,128]{1,0:T(8,128)S(1)}, f32[112,128]{1,0:T(8,128)}, u32[]{:S(2)}) copy-start(f32[112,128]{1,0:T(8,128)} %param.9) | copy-start | bytes 172036
  17.7 44.2 %all-to-all-start = ((f32[32,56,128]{2,1,0:T(8,128)}), f32[32,56,128]{2,1,0:T(8,128)S(1)}, u32[]{:S(2)}, u32[]{:S(2)}) async-start(f32[32,56,128]{2,1,0:T(8,128)} %shard_map.73), calls=%async_computation | async-start | bytes 1835008 | tf_op jit(solution)/shard_map/all_to_all | solution.py:195
  24.4 0.7 copy-start.5
  24.4 0.7 copy-start.6
  25.1 25.3 %collective-permute-start.3 = (f32[1,120,128]{2,1,0:T(8,128)S(1)}, f32[1,120,128]{2,1,0:T(8,128)S(1)}, u32[]{:S(2)}, u32[]{:S(2)}) collective-permute-start(f32[1,120,128]{2,1,0:T(8,128)S(1)} %fusion.1), channel_id=1, source_target_pairs={{0,16},{4,20},{8,24},{12,28},{16,0},{20,4},{24,8},{28,12},{1,17},{... | collective-permute-start | bytes 184328 | tf_op jit(solution)/shard_map/ppermute | solution.py:169
  50.5 4.9 %collective-permute-start.4 = (f32[2,120,128]{2,1,0:T(8,128)S(1)}, f32[2,120,128]{2,1,0:T(8,128)S(1)}, u32[]{:S(2)}, u32[]{:S(2)}) collective-permute-start(f32[2,120,128]{2,1,0:T(8,128)S(1)} %pad_maximum_fusion.5), channel_id=1, source_target_pairs={{0,8},{4,12},{8,0},{12,4},{16,24},{20,28},{24,16},{28,20},{1,9},{5... | collective-permute-start | bytes 368648 | tf_op jit(solution)/shard_map/ppermute | solution.py:169
  55.4 6.4 %collective-permute-start.5 = (f32[4,120,128]{2,1,0:T(8,128)S(1)}, f32[4,120,128]{2,1,0:T(8,128)S(1)}, u32[]{:S(2)}, u32[]{:S(2)}) collective-permute-start(f32[4,120,128]{2,1,0:T(8,128)S(1)} %pad_maximum_fusion.1), channel_id=1, source_target_pairs={{0,4},{4,0},{8,12},{12,8},{16,20},{20,16},{24,28},{28,24},{1,5},{5... | collective-permute-start | bytes 737288 | tf_op jit(solution)/shard_map/ppermute | solution.py:169
  57.0 4.9 %copy-start = (f32[4,128,128]{2,1,0:T(8,128)S(1)}, f32[4,128,128]{2,1,0:T(8,128)}, u32[]{:S(2)}) copy-start(f32[4,128,128]{2,1,0:T(8,128)} %mortar_ref.1) | copy-start | bytes 786436
  79.6 20.3 %all-to-all-start.1 = ((f32[32,32,128]{2,1,0:T(8,128)}), f32[32,32,128]{2,1,0:T(8,128)S(1)}, u32[]{:S(2)}, u32[]{:S(2)}) async-start(f32[32,32,128]{2,1,0:T(8,128)} %shard_map.74), calls=%async_computation.1 | async-start | bytes 1048576 | tf_op jit(solution)/shard_map/all_to_all | solution.py:214
  100.9 2.0 %collective-permute-start.6 = (f32[224,128]{1,0:T(8,128)S(1)}, f32[224,128]{1,0:T(8,128)S(1)}, u32[]{:S(2)}, u32[]{:S(2)}) collective-permute-start(f32[224,128]{1,0:T(8,128)S(1)} %get-tuple-element.7), channel_id=1, source_target_pairs={{0,1},{1,0},{2,3},{3,2},{4,5},{5,4},{6,7},{7,6},{8,9},{9,8},{10,11... | collective-permute-start | bytes 344072 | tf_op jit(solution)/shard_map/ppermute | solution.py:182
  101.0 6.0 %collective-permute-start.7 = (f32[224,128]{1,0:T(8,128)S(1)}, f32[224,128]{1,0:T(8,128)S(1)}, u32[]{:S(2)}, u32[]{:S(2)}) collective-permute-start(f32[224,128]{1,0:T(8,128)S(1)} %get-tuple-element.6), channel_id=1, source_target_pairs={{0,2},{1,3},{2,0},{3,1},{4,6},{5,7},{6,4},{7,5},{8,10},{9,11},{10,... | collective-permute-start | bytes 344072 | tf_op jit(solution)/shard_map/ppermute | solution.py:182
  102.3 6.3 %collective-permute-start.8 = (f32[224,128]{1,0:T(8,128)S(1)}, f32[224,128]{1,0:T(8,128)S(1)}, u32[]{:S(2)}, u32[]{:S(2)}) collective-permute-start(f32[224,128]{1,0:T(8,128)S(1)} %get-tuple-element.5), channel_id=1, source_target_pairs={{0,3},{1,2},{2,1},{3,0},{4,7},{5,6},{6,5},{7,4},{8,11},{9,10},{10,... | collective-permute-start | bytes 344072 | tf_op jit(solution)/shard_map/ppermute | solution.py:182
  108.6 0.8 copy-start.3

commit v2 on v1

--- a/solution.py
+++ b/solution.py
@@ -24,6 +24,11 @@
 
 def product3(a, b):
     return product(a[0], b[0]) + product(a[1], b[0]) + product(a[0], b[1])
+
+
+def three_parts(value):
+    high, low = halves(value)
+    return high, high, low
 
 
 def iota(shape, dim):
@@ -56,13 +61,21 @@
     return out
 
 
-def project_kernel(rep_count, share, place_ref, projection_ref, *refs):
+def mixers_kernel(rep_count, share, place_ref, projection_ref, mix_ref, back_mix_ref):
+    projection = projection_ref[...]
+    for part, value in enumerate(mixer(projection, place_ref[0], rep_count, share, ROWS, 2)):
+        mix_ref[part] = value
+    for part, value in enumerate(mixer(projection, place_ref[0], rep_count, share, ROWS, 1)):
+        back_mix_ref[part] = value.astype(jnp.float32).T.astype(jnp.bfloat16)
+
+
+def project_kernel(rep_count, share, mix_ref, *refs):
     out_ref = refs[-1]
     state_refs, move_refs = refs[:rep_count], refs[rep_count : 2 * rep_count]
     channels, rows, faces = out_ref.shape
     group = ROWS
     per = group // 2 * share
-    mix = mixer(projection_ref[...], place_ref[0], rep_count, share, group, 2)
+    mix = mix_ref[0], mix_ref[1]
     for g in range(rows // group):
         span = pl.ds(g * per, per)
         pieces = []
@@ -73,12 +86,11 @@
         out_ref[:, pl.ds(g * group, group), :] = out.reshape(channels, group, faces)
 
 
-def back_kernel(rep_count, share, place_ref, projection_ref, summed_ref, out_ref):
+def back_kernel(rep_count, share, mix_ref, summed_ref, out_ref):
     channels, padded, faces = summed_ref.shape
     group = ROWS
     size = channels * group
-    mix = mixer(projection_ref[...], place_ref[0], rep_count, share, group, 1)
-    mix = [m.T for m in mix]
+    mix = mix_ref[0], mix_ref[1]
     rows = out_ref.shape[1]
     for g in range(padded // group):
         values = halves(summed_ref[:, pl.ds(g * group, group), :].reshape(size, faces))
@@ -87,55 +99,98 @@
         out_ref[:, pl.ds(g * group * share, count), :] = out[:, :count]
 
 
-def contact_kernel(
-    order, blocks, partner_count, place_ref, packed_ref, notes_ref, mortar_ref, out_ref,
-    stiff_ref, columns_ref, rows_ref, mapped_ref, hot_ref, back_ref, acc_ref, tangent_ref,
+def route_kernel(
+    order, partner_count, places_ref, notes_ref, mortar_ref, columns_ref, weight_ref, mortar_parts_ref, turned_parts_ref,
+    stiff_ref,
 ):
     total, faces = stiff_ref.shape
-    me = place_ref[0]
+    vol_count = len(order)
+    blocks = total // vol_count
+    half = blocks // 2
+    me, mine = places_ref[0], places_ref[1]
     for at, d in enumerate(order):
         start = pl.multiple_of((me ^ d) * blocks, ROWS)
-        stiff_ref[pl.ds(start, blocks), :] = notes_ref[at, 0:blocks, :]
-        small = notes_ref[at, blocks : blocks + ROWS, :]
+        for side in range(2):
+            first = pl.multiple_of(start + (mine ^ side) * half, ROWS)
+            stiff_ref[pl.ds(first, half), :] = notes_ref[side, at, 0:half, :]
+        small = notes_ref[0, at, half : half + ROWS, :]
         square = jnp.concatenate([small, jnp.zeros((LANES - ROWS, LANES), jnp.float32)], axis=0)
         columns_ref[pl.ds(start, blocks), :] = square.T[:blocks]
+    owner_column = columns_ref[:, partner_count : partner_count + 1]
+    owners = jnp.broadcast_to(owner_column, (total, faces))
+    small_owners = owners.astype(jnp.bfloat16)
+    for k in range(partner_count):
+        hot = one_where(iota((total, total), 1).astype(jnp.float32) == columns_ref[:, k : k + 1])
+        agree = product(hot, small_owners) == owners
+        weight_ref[k] = jnp.where(agree, stiff_ref[...] * sharpness, 0.0)
+    for k in range(partner_count):
+        for at, part in enumerate(three_parts(mortar_ref[k])):
+            mortar_parts_ref[at * faces : (at + 1) * faces, k * faces : (k + 1) * faces] = part
+        for at, part in enumerate(three_parts(mortar_ref[k].T)):
+            turned_parts_ref[k, at * faces : (at + 1) * faces, :] = part
+
+
+def contact_kernel(
+    packed_ref, columns_ref, weight_ref, mortar_parts_ref, turned_parts_ref, out_ref,
+    mapped_ref, back_ref, tangent_ref, rows_ref,
+):
+    partner_count, total, faces = weight_ref.shape
+    rows = total // 2
+    tiles = [(k, r) for k in range(partner_count) for r in range(0, total, rows)]
     for t in range(total // LANES):
         rows_ref[:, t * LANES : (t + 1) * LANES] = columns_ref[t * LANES : (t + 1) * LANES, :].T[:ROWS]
-
-    state = packed_ref[pl.ds(0, total, stride=2), :]
-    move = packed_ref[pl.ds(1, total, stride=2), :]
-    state_parts, move_parts = halves(state), halves(move)
-    tangent_ref[...] = jnp.zeros_like(tangent_ref)
-    acc_ref[...] = jnp.zeros_like(acc_ref)
-    owner_row = rows_ref[partner_count : partner_count + 1, :]
-    owner_column = columns_ref[:, partner_count : partner_count + 1]
-
-    for k in range(partner_count):
-        mortar = halves(mortar_ref[k])
-        for part, parts in enumerate((state_parts, move_parts)):
-            high, low = halves(product3(parts, mortar))
-            mapped_ref[0, :, part * faces : (part + 1) * faces] = high
-            mapped_ref[1, :, part * faces : (part + 1) * faces] = low
-        target = columns_ref[:, k : k + 1]
-        named = iota((total, total), 1).astype(jnp.float32) == target
-        hot_ref[...] = one_where(named)
-        partner_owner = jnp.sum(jnp.where(named, owner_row, 0.0), axis=1, keepdims=True)
-        agree = (partner_owner == owner_column).astype(jnp.float32)
-        gathered = product(hot_ref[...], mapped_ref[0]) + product(hot_ref[...], mapped_ref[1])
-        gap = packed_ref[pl.ds(0, total, stride=2), :] - gathered[:, :faces]
-        change = packed_ref[pl.ds(1, total, stride=2), :] - gathered[:, faces:]
+    for which in range(2):
+        high, low = halves(packed_ref[pl.ds(which, total, stride=2), :])
+        mapped = product(jnp.concatenate([high, low, high], axis=1), mortar_parts_ref[...])
+        for k in range(partner_count):
+            high, low = halves(mapped[:, k * faces : (k + 1) * faces])
+            mapped_ref[k, 0, :, which * faces : (which + 1) * faces] = high
+            mapped_ref[k, 1, :, which * faces : (which + 1) * faces] = low
+
+    def gather(k, r):
+        named = iota((rows, total), 1).astype(jnp.float32) == columns_ref[pl.ds(r, rows), k : k + 1]
+        hot = one_where(named)
+        return product(hot, mapped_ref[k, 0]) + product(hot, mapped_ref[k, 1])
+
+    def traction_parts(k, r, gathered):
+        gap = packed_ref[pl.ds(2 * r, rows, stride=2), :] - gathered[:, :faces]
+        change = packed_ref[pl.ds(2 * r + 1, rows, stride=2), :] - gathered[:, faces:]
         small = jnp.exp(-sharpness * jnp.abs(gap))
         slope = small / ((1.0 + small) * (1.0 + small))
-        traction = stiff_ref[...] * (agree * sharpness) * slope * change
-        tangent_ref[...] += traction
-        back = product3(halves(traction), halves(mortar_ref[k].T))
-        high, low = halves(back)
-        back_ref[:, :faces] = high
-        back_ref[:, faces:] = low
-        hot_ref[...] = one_where(iota((total, total), 0).astype(jnp.float32) == rows_ref[k : k + 1, :])
-        acc_ref[...] += product(hot_ref[...], back_ref[...])
-
-    tangent_ref[...] = tangent_ref[...] - acc_ref[:, :faces] - acc_ref[:, faces:]
+        traction = weight_ref[k, pl.ds(r, rows), :] * slope * change
+        if k == 0:
+            tangent_ref[pl.ds(r, rows), :] = traction
+        else:
+            tangent_ref[pl.ds(r, rows), :] += traction
+        high, low = halves(traction)
+        return jnp.concatenate([high, low, high], axis=1)
+
+    def send_back(k, r, parts):
+        high, low = halves(product(parts, turned_parts_ref[k]))
+        back_ref[k, pl.ds(r, rows), :faces] = high
+        back_ref[k, pl.ds(r, rows), faces:] = low
+
+    ahead = 2
+    gathered = {at: gather(*tiles[at]) for at in range(ahead)}
+    waiting = None
+    for at, (k, r) in enumerate(tiles):
+        if at + ahead < len(tiles):
+            gathered[at + ahead] = gather(*tiles[at + ahead])
+        parts = traction_parts(k, r, gathered.pop(at))
+        if waiting is not None:
+            send_back(*waiting)
+        waiting = k, r, parts
+    send_back(*waiting)
+
+    def turned(k, r):
+        return one_where((iota((rows, total), 0) + r).astype(jnp.float32) == rows_ref[k : k + 1, :])
+
+    for r in range(0, total, rows):
+        span = pl.ds(r, rows)
+        back = product(turned(0, r), back_ref[0])
+        for k in range(1, partner_count):
+            back += product(turned(k, r), back_ref[k])
+        tangent_ref[span, :] = tangent_ref[span, :] - back[:, :faces] - back[:, faces:]
     devices, padded, _ = out_ref.shape
     slab = total // devices
     for device in range(devices):
@@ -154,22 +209,18 @@
     slab = blocks // rep_count
     padded = -(-slab // ROWS) * ROWS
     total = blocks * vol_count
+    size = channels * ROWS
     vmem = pl.BlockSpec(memory_space=pltpu.VMEM)
     smem = pl.BlockSpec(memory_space=pltpu.SMEM)
     rep_place = rep_index.astype(jnp.int32)[None]
-    vol_place = vol_index.astype(jnp.int32)[None]
-    params = pltpu.CompilerParams(vmem_limit_bytes=48 * 1024 * 1024)
-
-    small = jnp.concatenate([partners.T, contact_owner[None, :]], axis=0).astype(jnp.float32)
-    small = jnp.pad(small, ((0, ROWS - partner_count - 1), (0, faces - blocks)))
-    notes = jnp.concatenate([stiffness, small], axis=0)[None]
-    order = [0]
-    step = vol_count // 2
-    while step:
-        other = lax.ppermute(notes, "vol", [(i, i ^ step) for i in range(vol_count)])
-        notes = jnp.concatenate([notes, other], axis=0)
-        order += [d ^ step for d in order]
-        step //= 2
+    params = pltpu.CompilerParams(vmem_limit_bytes=18 * 1024 * 1024)
+
+    def array(*shape, dtype=jnp.float32):
+        return jax.ShapeDtypeStruct(shape, dtype)
+
+    def swap(value, axis, d):
+        count = lax.axis_size(axis)
+        return lax.ppermute(value, axis, [(i, i ^ d) for i in range(count)])
 
     def slabs(values):
         return [
@@ -178,48 +229,75 @@
         ]
 
     def exchange(pieces):
-        return pieces[:1] + [
-            lax.ppermute(pieces[d], "rep", [(i, i ^ d) for i in range(rep_count)])
-            for d in range(1, rep_count)
-        ]
-
-    both = [jnp.stack(pair) for pair in zip(slabs(surface_state), slabs(direction))]
-    both = exchange(both)
+        return pieces[:1] + [swap(pieces[d], "rep", d) for d in range(1, rep_count)]
+
+    both = exchange([jnp.stack(pair) for pair in zip(slabs(surface_state), slabs(direction))])
+
+    half = blocks // 2
+    small = jnp.concatenate([partners.T, contact_owner[None, :]], axis=0).astype(jnp.float32)
+    small = jnp.pad(small, ((0, ROWS - partner_count - 1), (0, faces - blocks)))
+    mine = rep_index % 2
+    notes = jnp.concatenate([lax.dynamic_slice_in_dim(stiffness, mine * half, half, 0), small], axis=0)
+    far = list(range(2, vol_count, 2))
+    notes = jnp.stack([notes] + [swap(notes, "vol", d) for d in far])
+    notes = jnp.concatenate([notes, swap(notes, "vol", 1)], axis=0)
+    order = [0] + far + [1] + [d ^ 1 for d in far]
+
+    mix, back_mix = pl.pallas_call(
+        functools.partial(mixers_kernel, rep_count, share),
+        out_shape=(array(2, size, size, dtype=jnp.bfloat16), array(2, size, size, dtype=jnp.bfloat16)),
+        in_specs=[smem, vmem],
+        out_specs=(vmem,) * 2,
+        compiler_params=params,
+    )(rep_place, projection)
+
+    both, notes = lax.optimization_barrier((both, notes))
     sent = pl.pallas_call(
         functools.partial(project_kernel, rep_count, share),
-        out_shape=jax.ShapeDtypeStruct((channels, 2 * slab, faces), jnp.float32),
-        in_specs=[smem] + [vmem] * (1 + 2 * rep_count),
+        out_shape=array(channels, 2 * slab, faces),
+        in_specs=[vmem] * (1 + 2 * rep_count),
         out_specs=vmem,
         compiler_params=params,
-    )(rep_place, projection, *[b[0] for b in both], *[b[1] for b in both])
+    )(mix, *[b[0] for b in both], *[b[1] for b in both])
     packed = lax.all_to_all(sent, ("vol", "rep"), 0, 0, tiled=True).reshape(2 * total, faces)
 
+    notes = jnp.stack([notes, swap(notes, "rep", 1)])
+    columns, weight, mortar_parts, turned_parts = pl.pallas_call(
+        functools.partial(route_kernel, tuple(order), partner_count),
+        out_shape=(
+            array(total, LANES),
+            array(partner_count, total, faces),
+            array(3 * faces, partner_count * faces, dtype=jnp.bfloat16),
+            array(partner_count, 3 * faces, faces, dtype=jnp.bfloat16),
+        ),
+        in_specs=[smem, vmem, vmem],
+        out_specs=(vmem,) * 4,
+        scratch_shapes=[pltpu.VMEM((total, faces), jnp.float32)],
+        compiler_params=params,
+    )(jnp.stack([vol_index, mine]).astype(jnp.int32), notes, mortar)
+
     summed = pl.pallas_call(
-        functools.partial(contact_kernel, tuple(order), blocks, partner_count),
-        out_shape=jax.ShapeDtypeStruct((devices, padded, faces), jnp.float32),
-        in_specs=[smem, vmem, vmem, vmem],
+        contact_kernel,
+        out_shape=array(devices, padded, faces),
+        in_specs=[vmem] * 5,
         out_specs=vmem,
         scratch_shapes=[
+            pltpu.VMEM((partner_count, 2, total, 2 * faces), jnp.bfloat16),
+            pltpu.VMEM((partner_count, total, 2 * faces), jnp.bfloat16),
             pltpu.VMEM((total, faces), jnp.float32),
-            pltpu.VMEM((total, LANES), jnp.float32),
             pltpu.VMEM((ROWS, total), jnp.float32),
-            pltpu.VMEM((2, total, 2 * faces), jnp.bfloat16),
-            pltpu.VMEM((total, total), jnp.bfloat16),
-            pltpu.VMEM((total, 2 * faces), jnp.bfloat16),
-            pltpu.VMEM((total, 2 * faces), jnp.float32),
-            pltpu.VMEM((total, faces), jnp.float32),
         ],
         compiler_params=params,
-    )(vol_place, packed, notes, mortar)
+    )(packed, columns, weight, mortar_parts, turned_parts)
     returned = lax.all_to_all(summed, ("vol", "rep"), 0, 0, tiled=True)
 
     pieces = pl.pallas_call(
         functools.partial(back_kernel, rep_count, share),
-        out_shape=jax.ShapeDtypeStruct((rep_count, slab * share, faces), jnp.float32),
-        in_specs=[smem, vmem, vmem],
+        out_shape=array(rep_count, slab * share, faces),
+        in_specs=[vmem, vmem],
         out_specs=vmem,
         compiler_params=params,
-    )(rep_place, projection, returned)
+    )(back_mix, returned)
     pieces = exchange([pieces[d] for d in range(rep_count)])
     out = jnp.zeros((blocks * share, faces), jnp.float32)
     for d in range(rep_count):
@@ -332,6 +410,8 @@
         and faces == LANES
         and blocks <= faces
         and blocks % (ROWS // 2 * rep_count) == 0
+        and blocks % (2 * ROWS) == 0
+        and min(vol_count, rep_count) > 1
         and total % LANES == 0
         and partner_shape[1] < ROWS
     )

time: 110 us -> 90.5 us (0.82)
  waiting for transfers between devices: 63.7 us -> 45.4 us
  Pallas kernels: 20.8 us -> 14.9 us
  local copies, waits for them, and re-layouts: 3.58 us -> 6.87 us
    ppermute x9 -> x11, waiting for transfers between devices: 48.1 us -> 13.4 us  [swap(): return lax.ppermute(value, axis, [(i, i ^ d) for i in range(count)])]
    all_to_all x1, waiting for transfers between devices: 0.01 us -> 16.5 us  [spread_local(): lax.all_to_all(sent, ('vol', 'rep'), 0, 0, tiled=True)]
    pallas_call x1 -> x3, Pallas kernels: 17.7 us -> 12.5 us  [the longest x1 9.17 us: spread_local(): pl.pallas_call(contact_kernel, out_shape=array(devices, padded, faces), i...]
    unnamed x14 -> x19, local copies, waits for them, and re-layouts: 2.24 us -> 5.36 us
    ppermute x9 -> x11, starting transfers between devices: 9.55 us -> 11.8 us  [swap(): return lax.ppermute(value, axis, [(i, i ^ d) for i in range(count)])]
    another operation x1, local copies, waits for them, and re-layouts: 0.03 us -> 1.32 us  [spread_local(): jnp.stack(pair)]
    all_to_all x1, starting transfers between devices: 4.78 us -> 3.63 us  [spread_local(): returned = lax.all_to_all(summed, ('vol', 'rep'), 0, 0, tiled=True)]
    another operation x1 -> x0, local copies, waits for them, and re-layouts: 1.15 us -> none  [spread_local(): b[1]]
  transfers between devices with their start and end apart: 11 -> 13, of which waited for: 8 -> 8; matrix products, arithmetic and copies ran while one was open for 0% -> 2% of each run, Pallas kernels for 0% -> 4%
where the time goes in v2:
time: 90.5 us; the launch traced here: 90 us
  waiting for transfers between devices  45.4 us (50%)
  starting transfers between devices  21.7 us (24%)
  Pallas kernels  14.9 us (16%)
  local copies, waits for them, and re-layouts  6.87 us (8%)
  other arithmetic  0.92 us (1%)
    all_to_all x1, waiting for transfers between devices, spread_local(): lax.all_to_all(sent, ('vol', 'rep'), 0, 0, tiled=True)  16.5 us
    all_to_all x1, waiting for transfers between devices, spread_local(): returned = lax.all_to_all(summed, ('vol', 'rep'), 0, 0, tiled=True)  15.5 us
    ppermute x11, waiting for transfers between devices, swap(): return lax.ppermute(value, axis, [(i, i ^ d) for i in range(count)])  13.4 us
    ppermute x11, starting transfers between devices, swap(): return lax.ppermute(value, axis, [(i, i ^ d) for i in range(count)])  11.8 us
    pallas_call x1, Pallas kernels, spread_local(): pl.pallas_call(contact_kernel, out_shape=array(devices, padded, faces), i...  9.17 us
    all_to_all x1, starting transfers between devices, spread_local(): lax.all_to_all(sent, ('vol', 'rep'), 0, 0, tiled=True)  6.2 us
    unnamed x19, local copies, waits for them, and re-layouts  5.36 us
    all_to_all x1, starting transfers between devices, spread_local(): returned = lax.all_to_all(summed, ('vol', 'rep'), 0, 0, tiled=True)  3.63 us
  transfers between devices with their start and end apart: 13, of which 8 were waited for; matrix products, arithmetic and copies ran while one was open for 2% of the time, Pallas kernels for 4%

profile of v2, /device:TPU:0, one launch (start us, length us, event | category | flops | bytes accessed | tf_op | source)
XLA Modules:
  0.0 90.0 jit_solution(6880015303260782310)
XLA Ops:
  0.0 0.7 add_convert_fusion
  0.9 4.1 %collective-permute-start.4 = (f32[64,128]{1,0:T(8,128)S(1)}, f32[64,128]{1,0:T(8,128)S(1)}, u32[]{:S(2)}, u32[]{:S(2)}) collective-permute-start(f32[64,128]{1,0:T(8,128)S(1)} %get-tuple-element.47), channel_id=1, source_target_pairs={{0,16},{4,20},{8,24},{12,28},{16,0},{20,4},{24,8},{28,12},{1,17},{... | collective-permute-start | bytes 98312 | tf_op jit(solution)/shard_map/ppermute | solution.py:223
  5.0 1.6 %collective-permute-start.3 = (f32[64,128]{1,0:T(8,128)S(1)}, f32[64,128]{1,0:T(8,128)S(1)}, u32[]{:S(2)}, u32[]{:S(2)}) collective-permute-start(f32[64,128]{1,0:T(8,128)S(1)} %get-tuple-element.47), channel_id=1, source_target_pairs={{0,8},{4,12},{8,0},{12,4},{16,24},{20,28},{24,16},{28,20},{1,9},{5... | collective-permute-start | bytes 98312 | tf_op jit(solution)/shard_map/ppermute | solution.py:223
  6.5 1.3 %dynamic-slice_bitcast_fusion = (f32[1,224,128]{2,1,0:T(8,128)S(1)}, f32[1,224,128]{2,1,0:T(8,128)S(1)}, f32[1,224,128]{2,1,0:T(8,128)S(1)}, f32[1,224,128]{2,1,...) fusion(f32[112,8,128]{2,1,0:T(8,128)} %param.8, ...), kind=kLoop, calls=%fused_computation.19 | loop fusion | bytes 1835024 | tf_op jit(solution)/shard_map/stack;reshape | solution.py:234
  7.9 1.8 %collective-permute-start.1 = (f32[2,224,128]{2,1,0:T(8,128)S(1)}, f32[2,224,128]{2,1,0:T(8,128)S(1)}, u32[]{:S(2)}, u32[]{:S(2)}) collective-permute-start(f32[2,224,128]{2,1,0:T(8,128)S(1)} %pad_maximum_fusion.3), channel_id=1, source_target_pairs={{0,2},{1,3},{2,0},{3,1},{4,6},{5,7},{6,4},{7,5},{8,10},{9,11},{10,... | collective-permute-start | bytes 688136 | tf_op jit(solution)/shard_map/ppermute | solution.py:223
  9.8 0.5 shard_map.73
  10.4 0.5 collective-permute-start.2
  10.8 1.4 %collective-permute-done.5 = f32[64,128]{1,0:T(8,128)S(1)} collective-permute-done((f32[64,128]{1,0:T(8,128)S(1)}, f32[64,128]{1,0:T(8,128)S(1)}, u32[]{:S(2)}, u32[]{:S(2)}) %collective-permute-start.5) | collective-permute-done | bytes 32800 | tf_op jit(solution)/shard_map/ppermute | solution.py:223
  12.3 1.6 %collective-permute-start.6 = (f32[4,64,128]{2,1,0:T(8,128)S(1)}, f32[4,64,128]{2,1,0:T(8,128)S(1)}, u32[]{:S(2)}, u32[]{:S(2)}) collective-permute-start(f32[4,64,128]{2,1,0:T(8,128)S(1)} %pad_maximum_fusion.5), channel_id=1, source_target_pairs={{0,4},{4,0},{8,12},{12,8},{16,20},{20,16},{24,28},{28,24},{1,5},{5... | collective-permute-start | bytes 393224 | tf_op jit(solution)/shard_map/ppermute | solution.py:223
  13.9 3.4 %collective-permute-done.6 = f32[4,64,128]{2,1,0:T(8,128)S(1)} collective-permute-done((f32[4,64,128]{2,1,0:T(8,128)S(1)}, f32[4,64,128]{2,1,0:T(8,128)S(1)}, u32[]{:S(2)}, u32[]{:S(2)}) %collective-permute-start.6) | collective-permute-done | bytes 131104 | tf_op jit(solution)/shard_map/ppermute | solution.py:223
  17.3 1.3 %collective-permute-done.2 = f32[2,224,128]{2,1,0:T(8,128)S(1)} collective-permute-done((f32[2,224,128]{2,1,0:T(8,128)S(1)}, f32[2,224,128]{2,1,0:T(8,128)S(1)}, u32[]{:S(2)}, u32[]{:S(2)}) %collective-permute-start.2) | collective-permute-done | bytes 229408 | tf_op jit(solution)/shard_map/ppermute | solution.py:223
  18.8 1.8 %shard_map.74 = f32[32,56,128]{2,1,0:T(8,128)} custom-call(bf16[2,256,256]{2,1,0:T(8,128)(2,1)S(1)} %get-tuple-element.17.mix_ref, f32[224,128]{1,0:T(8,128)S(1)} %get-tuple-element.45.refs_0_, f32[224,128]{1,0:T(8,128)S(1)} %get-tuple-element.43.refs_1_, f32[224,128]{1,0:T(8,128)S(1)} %get-tuple-element.41.refs_2_, ...), custom_call_target="tpu_custom_call" | custom-call | tf_op jit(solution)/shard_map/pallas_call | solution.py:255
  20.6 6.2 %all-to-all-start = ((f32[32,56,128]{2,1,0:T(8,128)}), f32[32,56,128]{2,1,0:T(8,128)S(1)}, u32[]{:S(2)}, u32[]{:S(2)}) async-start(f32[32,56,128]{2,1,0:T(8,128)} %shard_map.74), calls=%async_computation | async-start | bytes 1835008 | tf_op jit(solution)/shard_map/all_to_all | solution.py:262
  26.8 0.3 collective-permute-start.7
  27.2 1.2 %collective-permute-done.7 = f32[8,64,128]{2,1,0:T(8,128)S(1)} collective-permute-done((f32[8,64,128]{2,1,0:T(8,128)S(1)}, f32[8,64,128]{2,1,0:T(8,128)S(1)}, u32[]{:S(2)}, u32[]{:S(2)}) %collective-permute-start.7) | collective-permute-done | bytes 262176 | tf_op jit(solution)/shard_map/ppermute | solution.py:223
  28.5 0.9 %copy-done.5 = f32[4,128,128]{2,1,0:T(8,128)S(1)} copy-done((f32[4,128,128]{2,1,0:T(8,128)S(1)}, f32[4,128,128]{2,1,0:T(8,128)}, u32[]{:S(2)}) %copy-start.5) | copy-done | bytes 262168
  29.4 2.8 %shard_map.75 = (f32[896,128]{1,0:T(8,128)S(1)}, f32[4,896,128]{2,1,0:T(8,128)S(1)}, bf16[384,512]{1,0:T(8,128)(2,1)S(1)}, bf16[4,384,128]{2,1,0:T(8,128)(2,1)S(1)}) custom-call(s32[2]{0:T(128)S(1)} %pad_add_fusion.places_ref, f32[2,8,64,128]{3,2,1,0:T(8,128)S(1)} %pad_maximum_fusion.notes_ref, f32[4,128,128]{2,1,0:T(8,128)S(1)} %copy-done.5), custom_call_target="tpu_custom_call" | custom-call | tf_op jit(solution)/shard_map/pallas_call | solution.py:265
  32.2 0.7 copy-done.1
  33.0 0.8 copy-done.3
  33.7 16.5 %all-to-all-done = f32[32,56,128]{2,1,0:T(8,128)S(1)} async-done(((f32[32,56,128]{2,1,0:T(8,128)}), f32[32,56,128]{2,1,0:T(8,128)S(1)}, u32[]{:S(2)}, u32[]{:S(2)}) %all-to-all-start) | async-done | bytes 917536 | tf_op jit(solution)/shard_map/all_to_all | solution.py:262
  50.2 1.0 %copy-done.2 = bf16[384,512]{1,0:T(8,128)(2,1)S(1)} copy-done((bf16[384,512]{1,0:T(8,128)(2,1)S(1)}, bf16[384,512]{1,0:T(8,128)(2,1)}, u32[]{:S(2)}) %copy-start.2) | copy-done | bytes 393240
  51.2 1.0 %copy-done.4 = bf16[4,384,128]{2,1,0:T(8,128)(2,1)S(1)} copy-done((bf16[4,384,128]{2,1,0:T(8,128)(2,1)S(1)}, bf16[4,384,128]{2,1,0:T(8,128)(2,1)}, u32[]{:S(2)}) %copy-start.4) | copy-done | bytes 393240
  52.2 9.2 %shard_map.76 = f32[32,32,128]{2,1,0:T(8,128)} custom-call(f32[1792,128]{1,0:T(8,128)S(1)} %bitcast.60, f32[896,128]{1,0:T(8,128)S(1)} %get-tuple-element.23.columns_ref, f32[4,896,128]{2,1,0:T(8,128)S(1)} %get-tuple-element.24.weight_ref, bf16[384,512]{1,0:T(8,128)(2,1)S(1)} %copy-done.2, bf16[4,384,128]{2,1,0:T(8,128)(2,1)S(1)} %copy-done.4), custom_call_target="tpu_custom_call" | custom-call | tf_op jit(solution)/shard_map/pallas_call | solution.py:279
  61.4 3.6 %all-to-all-start.1 = ((f32[32,32,128]{2,1,0:T(8,128)}), f32[32,32,128]{2,1,0:T(8,128)S(1)}, u32[]{:S(2)}, u32[]{:S(2)}) async-start(f32[32,32,128]{2,1,0:T(8,128)} %shard_map.76), calls=%async_computation.1 | async-start | bytes 1048576 | tf_op jit(solution)/shard_map/all_to_all | solution.py:292
  65.1 15.5 %all-to-all-done.1.summed_ref = f32[32,32,128]{2,1,0:T(8,128)S(1)} async-done(((f32[32,32,128]{2,1,0:T(8,128)}), f32[32,32,128]{2,1,0:T(8,128)S(1)}, u32[]{:S(2)}, u32[]{:S(2)}) %all-to-all-start.1) | async-done | bytes 524320 | tf_op jit(solution)/shard_map/all_to_all | solution.py:292
  80.6 0.6 shard_map.77
  81.2 1.0 %collective-permute-start.10 = (f32[224,128]{1,0:T(8,128)S(1)}, f32[224,128]{1,0:T(8,128)S(1)}, u32[]{:S(2)}, u32[]{:S(2)}) collective-permute-start(f32[224,128]{1,0:T(8,128)S(1)} %get-tuple-element.27), channel_id=1, source_target_pairs={{0,3},{1,2},{2,1},{3,0},{4,7},{5,6},{6,5},{7,4},{8,11},{9,10},{10,... | collective-permute-start | bytes 344072 | tf_op jit(solution)/shard_map/ppermute | solution.py:223
  82.2 0.6 collective-permute-start.9
  82.8 0.3 collective-permute-start.8
  83.2 0.9 %collective-permute-done.8 = f32[224,128]{1,0:T(8,128)S(1)} collective-permute-done((f32[224,128]{1,0:T(8,128)S(1)}, f32[224,128]{1,0:T(8,128)S(1)}, u32[]{:S(2)}, u32[]{:S(2)}) %collective-permute-start.8) | collective-permute-done | bytes 114720 | tf_op jit(solution)/shard_map/ppermute | solution.py:223
  84.1 5.0 %collective-permute-done.9 = f32[224,128]{1,0:T(8,128)S(1)} collective-permute-done((f32[224,128]{1,0:T(8,128)S(1)}, f32[224,128]{1,0:T(8,128)S(1)}, u32[]{:S(2)}, u32[]{:S(2)}) %collective-permute-start.9) | collective-permute-done | bytes 114720 | tf_op jit(solution)/shard_map/ppermute | solution.py:223
  89.2 0.8 copy-done.7
  (41 shorter events, 0.7 us)
Async XLA Ops:
  0.0 0.9 copy-start
  0.9 9.5 %collective-permute-start.4 = (f32[64,128]{1,0:T(8,128)S(1)}, f32[64,128]{1,0:T(8,128)S(1)}, u32[]{:S(2)}, u32[]{:S(2)}) collective-permute-start(f32[64,128]{1,0:T(8,128)S(1)} %get-tuple-element.47), channel_id=1, source_target_pairs={{0,16},{4,20},{8,24},{12,28},{16,0},{20,4},{24,8},{28,12},{1,17},{... | collective-permute-start | bytes 98312 | tf_op jit(solution)/shard_map/ppermute | solution.py:223
  5.0 5.9 %collective-permute-start.3 = (f32[64,128]{1,0:T(8,128)S(1)}, f32[64,128]{1,0:T(8,128)S(1)}, u32[]{:S(2)}, u32[]{:S(2)}) collective-permute-start(f32[64,128]{1,0:T(8,128)S(1)} %get-tuple-element.47), channel_id=1, source_target_pairs={{0,8},{4,12},{8,0},{12,4},{16,24},{20,28},{24,16},{28,20},{1,9},{5... | collective-permute-start | bytes 98312 | tf_op jit(solution)/shard_map/ppermute | solution.py:223
  6.5 5.7 %collective-permute-start.5 = (f32[64,128]{1,0:T(8,128)S(1)}, f32[64,128]{1,0:T(8,128)S(1)}, u32[]{:S(2)}, u32[]{:S(2)}) collective-permute-start(f32[64,128]{1,0:T(8,128)S(1)} %get-tuple-element.47), channel_id=1, source_target_pairs={{0,24},{4,28},{8,16},{12,20},{16,8},{20,12},{24,0},{28,4},{1,25},{... | collective-permute-start | bytes 98312 | tf_op jit(solution)/shard_map/ppermute | solution.py:223
  6.5 3.3 %copy-start.6 = (f32[32,32]{1,0:T(8,128)S(1)}, f32[32,32]{1,0:T(8,128)}, u32[]{:S(2)}) copy-start(f32[32,32]{1,0:T(8,128)} %projection_ref.1) | copy-start | bytes 12292
  7.9 9.4 %collective-permute-start.1 = (f32[2,224,128]{2,1,0:T(8,128)S(1)}, f32[2,224,128]{2,1,0:T(8,128)S(1)}, u32[]{:S(2)}, u32[]{:S(2)}) collective-permute-start(f32[2,224,128]{2,1,0:T(8,128)S(1)} %pad_maximum_fusion.3), channel_id=1, source_target_pairs={{0,2},{1,3},{2,0},{3,1},{4,6},{5,7},{6,4},{7,5},{8,10},{9,11},{10,... | collective-permute-start | bytes 688136 | tf_op jit(solution)/shard_map/ppermute | solution.py:223
  9.7 7.6 %collective-permute-start = (f32[2,224,128]{2,1,0:T(8,128)S(1)}, f32[2,224,128]{2,1,0:T(8,128)S(1)}, u32[]{:S(2)}, u32[]{:S(2)}) collective-permute-start(f32[2,224,128]{2,1,0:T(8,128)S(1)} %pad_maximum_fusion.2), channel_id=1, source_target_pairs={{0,1},{1,0},{2,3},{3,2},{4,5},{5,4},{6,7},{7,6},{8,9},{9,8},{10,11... | collective-permute-start | bytes 688136 | tf_op jit(solution)/shard_map/ppermute | solution.py:223
  10.4 8.3 %collective-permute-start.2 = (f32[2,224,128]{2,1,0:T(8,128)S(1)}, f32[2,224,128]{2,1,0:T(8,128)S(1)}, u32[]{:S(2)}, u32[]{:S(2)}) collective-permute-start(f32[2,224,128]{2,1,0:T(8,128)S(1)} %pad_maximum_fusion.4), channel_id=1, source_target_pairs={{0,3},{1,2},{2,1},{3,0},{4,7},{5,6},{6,5},{7,4},{8,11},{9,10},{10,... | collective-permute-start | bytes 688136 | tf_op jit(solution)/shard_map/ppermute | solution.py:223
  12.3 5.0 %collective-permute-start.6 = (f32[4,64,128]{2,1,0:T(8,128)S(1)}, f32[4,64,128]{2,1,0:T(8,128)S(1)}, u32[]{:S(2)}, u32[]{:S(2)}) collective-permute-start(f32[4,64,128]{2,1,0:T(8,128)S(1)} %pad_maximum_fusion.5), channel_id=1, source_target_pairs={{0,4},{4,0},{8,12},{12,8},{16,20},{20,16},{24,28},{28,24},{1,5},{5... | collective-permute-start | bytes 393224 | tf_op jit(solution)/shard_map/ppermute | solution.py:223
  20.6 29.6 %all-to-all-start = ((f32[32,56,128]{2,1,0:T(8,128)}), f32[32,56,128]{2,1,0:T(8,128)S(1)}, u32[]{:S(2)}, u32[]{:S(2)}) async-start(f32[32,56,128]{2,1,0:T(8,128)} %shard_map.74), calls=%async_computation | async-start | bytes 1835008 | tf_op jit(solution)/shard_map/all_to_all | solution.py:262
  26.8 1.6 %collective-permute-start.7 = (f32[8,64,128]{2,1,0:T(8,128)S(1)}, f32[8,64,128]{2,1,0:T(8,128)S(1)}, u32[]{:S(2)}, u32[]{:S(2)}) collective-permute-start(f32[8,64,128]{2,1,0:T(8,128)S(1)} %constant_dynamic-update-slice_fusion), channel_id=1, source_target_pairs={{0,1},{1,0},{2,3},{3,2},{4,5},{5,4},{6,7},{7,6},{8,9},{9,8},{10,11... | collective-permute-start | bytes 786440 | tf_op jit(solution)/shard_map/ppermute | solution.py:223
  28.5 1.0 %copy-start.5 = (f32[4,128,128]{2,1,0:T(8,128)S(1)}, f32[4,128,128]{2,1,0:T(8,128)}, u32[]{:S(2)}) copy-start(f32[4,128,128]{2,1,0:T(8,128)} %mortar_ref.1) | copy-start | bytes 786436
  32.2 0.7 copy-start.1
  33.0 0.8 copy-start.3
  50.2 1.0 %copy-start.2 = (bf16[384,512]{1,0:T(8,128)(2,1)S(1)}, bf16[384,512]{1,0:T(8,128)(2,1)}, u32[]{:S(2)}) copy-start(bf16[384,512]{1,0:T(8,128)(2,1)} %copy-done.1) | copy-start | bytes 1179652
  51.2 1.0 %copy-start.4 = (bf16[4,384,128]{2,1,0:T(8,128)(2,1)S(1)}, bf16[4,384,128]{2,1,0:T(8,128)(2,1)}, u32[]{:S(2)}) copy-start(bf16[4,384,128]{2,1,0:T(8,128)(2,1)} %copy-done.3) | copy-start | bytes 1179652
  61.4 19.2 %all-to-all-start.1 = ((f32[32,32,128]{2,1,0:T(8,128)}), f32[32,32,128]{2,1,0:T(8,128)S(1)}, u32[]{:S(2)}, u32[]{:S(2)}) async-start(f32[32,32,128]{2,1,0:T(8,128)} %shard_map.76), calls=%async_computation.1 | async-start | bytes 1048576 | tf_op jit(solution)/shard_map/all_to_all | solution.py:292
  81.2 8.0 %collective-permute-start.10 = (f32[224,128]{1,0:T(8,128)S(1)}, f32[224,128]{1,0:T(8,128)S(1)}, u32[]{:S(2)}, u32[]{:S(2)}) collective-permute-start(f32[224,128]{1,0:T(8,128)S(1)} %get-tuple-element.27), channel_id=1, source_target_pairs={{0,3},{1,2},{2,1},{3,0},{4,7},{5,6},{6,5},{7,4},{8,11},{9,10},{10,... | collective-permute-start | bytes 344072 | tf_op jit(solution)/shard_map/ppermute | solution.py:223
  82.2 6.9 %collective-permute-start.9 = (f32[224,128]{1,0:T(8,128)S(1)}, f32[224,128]{1,0:T(8,128)S(1)}, u32[]{:S(2)}, u32[]{:S(2)}) collective-permute-start(f32[224,128]{1,0:T(8,128)S(1)} %get-tuple-element.28), channel_id=1, source_target_pairs={{0,2},{1,3},{2,0},{3,1},{4,6},{5,7},{6,4},{7,5},{8,10},{9,11},{10,... | collective-permute-start | bytes 344072 | tf_op jit(solution)/shard_map/ppermute | solution.py:223
  82.8 1.3 %collective-permute-start.8 = (f32[224,128]{1,0:T(8,128)S(1)}, f32[224,128]{1,0:T(8,128)S(1)}, u32[]{:S(2)}, u32[]{:S(2)}) collective-permute-start(f32[224,128]{1,0:T(8,128)S(1)} %get-tuple-element.29), channel_id=1, source_target_pairs={{0,1},{1,0},{2,3},{3,2},{4,5},{5,4},{6,7},{7,6},{8,9},{9,8},{10,11... | collective-permute-start | bytes 344072 | tf_op jit(solution)/shard_map/ppermute | solution.py:223
  89.2 0.8 copy-start.7

commit v3 on v0

--- a/solution.py
+++ b/solution.py
@@ -1,12 +1,387 @@
+import functools
+
 import jax
 import jax.numpy as jnp
 from jax import lax
+from jax.experimental import pallas as pl
+from jax.experimental.pallas import tpu as pltpu
 from jax.sharding import PartitionSpec as P
 
 sharpness = 1.5
-
-
-def local(surface_state, direction, stiffness, partners, contact_owner, projection, mortar):
+LANES = 128
+ROWS = 8
+
+
+def halves(value):
+    high = value.astype(jnp.bfloat16)
+    low = (value - high.astype(jnp.float32)).astype(jnp.bfloat16)
+    return high, low
+
+
+def product(a, b):
+    return jnp.dot(a, b, preferred_element_type=jnp.float32)
+
+
+def product3(a, b):
+    return product(a[0], b[0]) + product(a[1], b[0]) + product(a[0], b[1])
+
+
+def three_parts(value):
+    high, low = halves(value)
+    return high, high, low
+
+
+def iota(shape, dim):
+    return lax.broadcasted_iota(jnp.int32, shape, dim)
+
+
+def one_where(cond):
+    return jnp.where(cond, 1.0, 0.0).astype(jnp.bfloat16)
+
+
+def mixer(projection, channel_of, height, rep_index, rep_count, share, group):
+    channels = projection.shape[0]
+    width = rep_count * group * share
+    place = iota((height, channels), 0) // group
+    spread = one_where(channel_of(place) == iota((height, channels), 1))
+    col = iota((channels, width), 1)
+    j = (rep_index ^ (col // (group * share))) * share + col % share
+    pick = one_where(iota((channels, width), 0) == j)
+    keep = iota((height, width), 0) % group == (iota((height, width), 1) // share) % group
+    out = []
+    for part in halves(projection):
+        wide = product(product(spread, part).astype(jnp.bfloat16), pick)
+        out.append(jnp.where(keep, wide, 0.0).astype(jnp.bfloat16))
+    return out
+
+
+def back_mixer_kernel(rep_count, share, places_ref, projection_ref, after_ref, mix_ref):
+    projection, rep_index = projection_ref[...], places_ref[1]
+    parts = mixer(projection, lambda i: i, mix_ref.shape[2], rep_index, rep_count, share, ROWS)
+    for at, part in enumerate(parts):
+        mix_ref[at] = part.astype(jnp.float32).T.astype(jnp.bfloat16)
+
+
+def project_state_kernel(share, slab, places_ref, projection_ref, labels_ref, *refs):
+    slab_refs, out_ref = refs[:-1], refs[-1]
+    channels, padded, faces = out_ref.shape
+    rep_count = len(slab_refs)
+    mix = mixer(projection_ref[...], lambda i: i, channels * ROWS, places_ref[1], rep_count, share, ROWS)
+    count = labels_ref.shape[0]
+    spare = jnp.zeros((padded - slab - count, faces), jnp.float32)
+    tail = jnp.concatenate([labels_ref[...], spare], axis=0) if spare.shape[0] else labels_ref[...]
+    for b in range(0, slab, ROWS):
+        count = min(ROWS, slab - b)
+        pieces = []
+        for ref in slab_refs:
+            pieces.append(ref[pl.ds(b * share, count * share), :])
+            if count < ROWS:
+                pieces.append(jnp.zeros(((ROWS - count) * share, faces), jnp.float32))
+        out = product3(mix, halves(jnp.concatenate(pieces, axis=0))).reshape(channels, ROWS, faces)
+        out_ref[:, pl.ds(b, count), :] = out[:, :count]
+    out_ref[:, slab:padded, :] = jnp.broadcast_to(tail[None], (channels, padded - slab, faces))
+
+
+def project_move_kernel(rep_count, share, places_ref, projection_ref, *refs):
+    in_refs, out_refs = refs[:rep_count], refs[rep_count:]
+    blocks, faces = out_refs[0].shape
+    per = ROWS * share
+    me, rep_index = places_ref[0], places_ref[1]
+
+    def channel_of(d):
+        return (me ^ d) * rep_count + rep_index
+
+    mix = mixer(projection_ref[...], channel_of, len(out_refs) * ROWS, rep_index, rep_count, share, ROWS)
+    groups = blocks // ROWS
+    for g in range(0, groups, 2):
+        pair = range(g, min(g + 2, groups))
+        wide = [jnp.concatenate([ref[pl.ds(p * per, per), :] for ref in in_refs], axis=0) for p in pair]
+        out = product3(mix, halves(jnp.concatenate(wide, axis=1)))
+        for at, p in enumerate(pair):
+            for d, out_ref in enumerate(out_refs):
+                out_ref[pl.ds(p * ROWS, ROWS), :] = out[d * ROWS : (d + 1) * ROWS, at * faces : (at + 1) * faces]
+
+
+def back_kernel(rep_count, share, mix_ref, summed_ref, out_ref):
+    channels, padded, faces = summed_ref.shape
+    size = channels * ROWS
+    mix = mix_ref[0], mix_ref[1]
+    rows = out_ref.shape[1]
+    for b in range(0, padded, ROWS):
+        values = halves(summed_ref[:, pl.ds(b, ROWS), :].reshape(size, faces))
+        out = product3(mix, values).reshape(rep_count, ROWS * share, faces)
+        count = min(ROWS * share, rows - b * share)
+        out_ref[:, pl.ds(b * share, count), :] = out[:, :count]
+
+
+def map_parts(values, partner_count, faces, info_ref, maps_ref, mapped_ref):
+    for k in range(partner_count):
+        mortar = info_ref[partner_count + 1, k * faces : (k + 1) * faces, :]
+        for at, part in enumerate(three_parts(mortar)):
+            maps_ref[at * faces : (at + 1) * faces, k * faces : (k + 1) * faces] = part
+    high, low = halves(values)
+    mapped = product(jnp.concatenate([high, low, high], axis=1), maps_ref[...])
+    for k in range(partner_count):
+        high, low = halves(mapped[:, k * faces : (k + 1) * faces])
+        mapped_ref[k, :, :faces] = high
+        mapped_ref[k, :, faces:] = low
+
+
+def one_hot(k, r, rows, partner_count, info_ref):
+    column = info_ref[partner_count, pl.ds(r, rows), k : k + 1]
+    return one_where(iota((rows, info_ref.shape[1]), 1).astype(jnp.float32) == column)
+
+
+def gather(hot, mapped):
+    faces = mapped.shape[1] // 2
+    parts = product(hot, mapped)
+    return parts[:, :faces] + parts[:, faces:]
+
+
+def in_turn(tiles, ahead, first, then):
+    made = {at: first(*tiles[at]) for at in range(min(ahead, len(tiles)))}
+    for at, tile in enumerate(tiles):
+        if at + ahead < len(tiles):
+            made[at + ahead] = first(*tiles[at + ahead])
+        then(*tile, made.pop(at))
+
+
+def slope_kernel(rep_count, slab, packed_ref, mortar_ref, info_ref, state_ref, maps_ref, mapped_ref, labels_ref, arrived):
+    planes, total, faces = info_ref.shape
+    partner_count = planes - 2
+    devices = packed_ref.shape[0]
+    blocks = slab * rep_count
+    taken = ROWS // rep_count
+    copy = pltpu.make_async_copy(
+        mortar_ref, info_ref.at[partner_count + 1, pl.ds(0, partner_count * faces)], arrived
+    )
+    copy.start()
+    for device in range(devices):
+        state_ref[device * slab : (device + 1) * slab, :] = packed_ref[device, 0:slab, :]
+    labels_ref[...] = jnp.zeros_like(labels_ref)
+    for vol in range(devices // rep_count):
+        for rep in range(rep_count):
+            row = rep * taken
+            labels_ref[row : row + taken, :] = packed_ref[vol * rep_count + rep, slab : slab + taken, :]
+        info_ref[partner_count, vol * blocks : (vol + 1) * blocks, :] = labels_ref[...].T[:blocks]
+    owner_column = info_ref[partner_count, :, partner_count : partner_count + 1]
+    owners = jnp.broadcast_to(owner_column, (total, faces))
+    small_owners = owners.astype(jnp.bfloat16)
+    copy.wait()
+    map_parts(state_ref[...], partner_count, faces, info_ref, maps_ref, mapped_ref)
+    rows = total // 2
+
+    def first(k, r):
+        hot = one_hot(k, r, rows, partner_count, info_ref)
+        return gather(hot, mapped_ref[k]), product(hot, small_owners)
+
+    def then(k, r, made):
+        gathered, partner_owner = made
+        span = pl.ds(r, rows)
+        agree = partner_owner == info_ref[partner_count, span, partner_count : partner_count + 1]
+        small = jnp.exp(-sharpness * jnp.abs(state_ref[span, :] - gathered))
+        slope = sharpness * small / ((1.0 + small) * (1.0 + small))
+        info_ref[k, span, :] = jnp.where(agree, slope, 0.0)
+
+    tiles = [(k, r) for k in range(partner_count) for r in range(0, total, rows)]
+    in_turn(tiles, 2, first, then)
+
+
+def contact_kernel(order, places_ref, stiffness_ref, info_ref, *refs):
+    swaps = len(order)
+    piece_refs, refs = refs[:swaps], refs[swaps:]
+    out_ref, move_ref, stiff_ref, maps_ref, turned_maps_ref, mapped_ref, back_ref, tangent_ref, rows_ref = refs
+    total, faces = tangent_ref.shape
+    partner_count = info_ref.shape[0] - 2
+    blocks = total // swaps
+    half = blocks // 2
+    rows = total // 2
+    for at, d in enumerate(order):
+        start = pl.multiple_of((places_ref[0] ^ d) * blocks, ROWS)
+        move_ref[pl.ds(start, blocks), :] = piece_refs[d][...]
+        for side in range(2):
+            first = pl.multiple_of(start + (places_ref[1] % 2 ^ side) * half, ROWS)
+            stiff_ref[pl.ds(first, half), :] = stiffness_ref[side, at]
+    map_parts(move_ref[...], partner_count, faces, info_ref, maps_ref, mapped_ref)
+    for k in range(partner_count):
+        mortar = info_ref[partner_count + 1, k * faces : (k + 1) * faces, :]
+        for at, part in enumerate(three_parts(mortar.T)):
+            turned_maps_ref[k, at * faces : (at + 1) * faces, :] = part
+    for t in range(0, total, LANES):
+        rows_ref[:, t : t + LANES] = info_ref[partner_count, t : t + LANES, :].T[:ROWS]
+    waiting = []
+
+    def send_back(k, r, parts):
+        high, low = halves(product(parts, turned_maps_ref[k]))
+        back_ref[k, pl.ds(r, rows), :faces] = high
+        back_ref[k, pl.ds(r, rows), faces:] = low
+
+    def then(k, r, gathered):
+        span = pl.ds(r, rows)
+        traction = stiff_ref[span, :] * info_ref[k, span, :] * (move_ref[span, :] - gathered)
+        if k == 0:
+            tangent_ref[span, :] = traction
+        else:
+            tangent_ref[span, :] += traction
+        high, low = halves(traction)
+        if waiting:
+            send_back(*waiting.pop())
+        waiting.append((k, r, jnp.concatenate([high, low, high], axis=1)))
+
+    tiles = [(k, r) for k in range(partner_count) for r in range(0, total, rows)]
+    in_turn(tiles, 2, lambda k, r: gather(one_hot(k, r, rows, partner_count, info_ref), mapped_ref[k]), then)
+    send_back(*waiting.pop())
+
+    def turned(k, r):
+        return one_where((iota((rows, total), 0) + r).astype(jnp.float32) == rows_ref[k : k + 1, :])
+
+    for r in range(0, total, rows):
+        span = pl.ds(r, rows)
+        back = product(turned(0, r), back_ref[0])
+        for k in range(1, partner_count):
+            back += product(turned(k, r), back_ref[k])
+        tangent_ref[span, :] = tangent_ref[span, :] - back[:, :faces] - back[:, faces:]
+    devices, padded, _ = out_ref.shape
+    slab = total // devices
+    for device in range(devices):
+        out_ref[device, 0:slab, :] = tangent_ref[device * slab : (device + 1) * slab, :]
+        if padded > slab:
+            out_ref[device, slab:padded, :] = jnp.zeros((padded - slab, faces), jnp.float32)
+
+
+def spread_local(surface_state, direction, stiffness, partners, contact_owner, projection, mortar):
+    vol_count, rep_count = lax.axis_size("vol"), lax.axis_size("rep")
+    devices = vol_count * rep_count
+    vol_index, rep_index = lax.axis_index("vol"), lax.axis_index("rep")
+    blocks, share, faces = surface_state.shape
+    channels = projection.shape[0]
+    partner_count = partners.shape[1]
+    slab = blocks // rep_count
+    padded = -(-slab // ROWS) * ROWS
+    total = blocks * vol_count
+    size = channels * ROWS
+    vmem = pl.BlockSpec(memory_space=pltpu.VMEM)
+    smem = pl.BlockSpec(memory_space=pltpu.SMEM)
+    params = pltpu.CompilerParams(vmem_limit_bytes=18 * 1024 * 1024)
+    places = jnp.stack([vol_index, rep_index]).astype(jnp.int32)
+
+    def array(*shape, dtype=jnp.float32):
+        return jax.ShapeDtypeStruct(shape, dtype)
+
+    def scratch(*shape, dtype=jnp.float32):
+        return pltpu.VMEM(shape, dtype)
+
+    def swap(value, axis, d):
+        count = lax.axis_size(axis)
+        return lax.ppermute(value, axis, [(i, i ^ d) for i in range(count)])
+
+    def exchange(pieces):
+        return pieces[:1] + [swap(pieces[d], "rep", d) for d in range(1, rep_count)]
+
+    state = exchange([
+        lax.dynamic_slice_in_dim(surface_state, (rep_index ^ d) * slab, slab, 0).reshape(slab * share, faces)
+        for d in range(rep_count)
+    ])
+
+    state[rep_count // 2], direction = lax.optimization_barrier((state[rep_count // 2], direction))
+
+    move = {0: direction.reshape(blocks * share, faces)}
+    step = rep_count // 2
+    while step:
+        move.update({d ^ step: swap(value, "rep", step) for d, value in move.items()})
+        step //= 2
+
+    half = blocks // 2
+    stiffness = lax.dynamic_slice_in_dim(stiffness, rep_index % 2 * half, half, 0)
+    stiffness = jnp.stack([stiffness, swap(stiffness, "vol", 1)])
+    far = list(range(2, vol_count, 2))
+    order = [d ^ near for d in [0] + far for near in range(2)]
+    stiffness = [stiffness] + [swap(stiffness, "vol", d) for d in far]
+
+    taken = ROWS // rep_count
+    labels = jnp.concatenate([partners.T, contact_owner[None, :]], axis=0).astype(jnp.float32)
+    labels = jnp.pad(labels, ((0, ROWS - partner_count - 1), (0, faces - blocks)))
+    labels = lax.dynamic_slice_in_dim(labels, rep_index * taken, taken, 0)
+
+    sent = pl.pallas_call(
+        functools.partial(project_state_kernel, share, slab),
+        out_shape=array(channels, padded, faces),
+        in_specs=[smem] + [vmem] * (2 + rep_count),
+        out_specs=vmem,
+        compiler_params=params,
+    )(places, projection, labels, *state)
+    sent, stiffness = lax.optimization_barrier((sent, stiffness))
+    packed = lax.all_to_all(sent, ("vol", "rep"), 0, 0, tiled=True)
+
+    stiffness = jnp.concatenate(stiffness, axis=0)
+    stiffness = jnp.stack([stiffness, swap(stiffness, "rep", 1)])
+    move, stiffness = lax.optimization_barrier((move, stiffness))
+    moved = list(pl.pallas_call(
+        functools.partial(project_move_kernel, rep_count, share),
+        out_shape=(array(blocks, faces),) * vol_count,
+        in_specs=[smem] + [vmem] * (1 + rep_count),
+        out_specs=(vmem,) * vol_count,
+        compiler_params=params,
+    )(places, projection, *[move[d] for d in range(rep_count)]))
+    moved = [swap(piece, "vol", d) if d else piece for d, piece in enumerate(moved)]
+
+    info = pl.pallas_call(
+        functools.partial(slope_kernel, rep_count, slab),
+        out_shape=array(partner_count + 2, total, faces),
+        in_specs=[vmem, pl.BlockSpec(memory_space=pl.ANY)],
+        out_specs=vmem,
+        scratch_shapes=[
+            scratch(total, faces),
+            scratch(3 * faces, partner_count * faces, dtype=jnp.bfloat16),
+            scratch(partner_count, total, 2 * faces, dtype=jnp.bfloat16),
+            scratch(LANES, LANES),
+            pltpu.SemaphoreType.DMA,
+        ],
+        compiler_params=params,
+    )(packed, mortar.reshape(partner_count * faces, faces))
+
+    summed = pl.pallas_call(
+        functools.partial(contact_kernel, tuple(order)),
+        out_shape=array(devices, padded, faces),
+        in_specs=[smem] + [vmem] * (2 + vol_count),
+        out_specs=vmem,
+        scratch_shapes=[
+            scratch(total, faces),
+            scratch(total, faces),
+            scratch(3 * faces, partner_count * faces, dtype=jnp.bfloat16),
+            scratch(partner_count, 3 * faces, faces, dtype=jnp.bfloat16),
+            scratch(partner_count, total, 2 * faces, dtype=jnp.bfloat16),
+            scratch(partner_count, total, 2 * faces, dtype=jnp.bfloat16),
+            scratch(total, faces),
+            scratch(ROWS, total),
+        ],
+        compiler_params=params,
+    )(places, stiffness, info, *moved)
+    summed, after = lax.optimization_barrier((summed, places))
+    back_mix = pl.pallas_call(
+        functools.partial(back_mixer_kernel, rep_count, share),
+        out_shape=array(2, size, size, dtype=jnp.bfloat16),
+        in_specs=[smem, vmem, smem],
+        out_specs=vmem,
+        compiler_params=params,
+    )(places, projection, after)
+    returned = lax.all_to_all(summed, ("vol", "rep"), 0, 0, tiled=True)
+
+    pieces = pl.pallas_call(
+        functools.partial(back_kernel, rep_count, share),
+        out_shape=array(rep_count, slab * share, faces),
+        in_specs=[vmem, vmem],
+        out_specs=vmem,
+        compiler_params=params,
+    )(back_mix, returned)
+    pieces = exchange([pieces[d] for d in range(rep_count)])
+    out = jnp.zeros((blocks * share, faces), jnp.float32)
+    for d in range(rep_count):
+        out = lax.dynamic_update_slice_in_dim(out, pieces[d], (rep_index ^ d) * slab * share, 0)
+    return out.reshape(blocks, share, faces)
+
+
+def routed_local(surface_state, direction, stiffness, partners, contact_owner, projection, mortar):
     highest = lax.Precision.HIGHEST
     vol_count = lax.axis_size("vol")
     rep_index = lax.axis_index("rep")
@@ -99,6 +474,28 @@
     )
 
 
+def one_channel_each(mesh, state_shape, partner_shape):
+    vol_count, rep_count = mesh.shape["vol"], mesh.shape["rep"]
+    total, channels, faces = state_shape
+    blocks = total // vol_count
+    powers = all(n & (n - 1) == 0 for n in (vol_count, rep_count))
+    return (
+        powers
+        and channels == vol_count * rep_count
+        and channels // rep_count == ROWS
+        and faces == LANES
+        and blocks <= faces
+        and blocks % (ROWS // 2 * rep_count) == 0
+        and blocks % (2 * ROWS) == 0
+        and ROWS % rep_count == 0
+        and -(blocks // rep_count) % ROWS >= ROWS // rep_count
+        and min(vol_count, rep_count) > 1
+        and total % LANES == 0
+        and partner_shape[1] < ROWS
+        and partner_shape[1] * LANES <= total
+    )
+
+
 def solution(mesh):
     placed = (
         P("vol", "rep", None),
@@ -109,6 +506,12 @@
         P(),
         P(),
     )
-    return jax.shard_map(
-        local, mesh=mesh, in_specs=placed, out_specs=P("vol", "rep", None), check_vma=False
-    )
+
+    def program(surface_state, direction, stiffness, partners, *rest):
+        fits = one_channel_each(mesh, surface_state.shape, partners.shape)
+        plan = spread_local if fits else routed_local
+        return jax.shard_map(
+            plan, mesh=mesh, in_specs=placed, out_specs=P("vol", "rep", None), check_vma=False
+        )(surface_state, direction, stiffness, partners, *rest)
+
+    return program

time: 336 us -> 82.1 us (0.24); the launches traced: 331 us -> 81.7 us
  other arithmetic: 127 us -> 0.86 us
  waiting for transfers between devices: 107 us -> 27.9 us
  local copies, waits for them, and re-layouts: 36.9 us -> 2.79 us
  matrix products: 20.7 us -> 0 us
  Pallas kernels: 0 us -> 17 us
  between operations: 13.4 us -> 0.23 us
  starting transfers between devices: 26.1 us -> 32.9 us
    scatter-add x4 -> x0, other arithmetic: 107 us -> none  [local(): jax.ops.segment_sum(traction, target, num_segments=slot_count)]
    all_gather x3 -> x0, waiting for transfers between devices: 50.7 us -> none  [the longest x1 20.4 us: local(): lax.all_gather(surface_state, 'rep', axis=1, tiled=True)]
    all_to_all x5 -> x2, waiting for transfers between devices: 55 us -> 14.5 us  [the longest x1 14.5 us: spread_local(): returned = lax.all_to_all(summed, ('vol', 'rep'), 0, 0, tiled=True)]
    gather x17 -> x0, local copies, waits for them, and re-layouts: 26.9 us -> none  [the longest x4 10.5 us: local(): contact_gap = got_state - mapped_state[column][target]]
    ppermute x0 -> x21, starting transfers between devices: none -> 25.5 us  [swap(): return lax.ppermute(value, axis, [(i, i ^ d) for i in range(count)])]
    dot_general x6 -> x0, matrix products: 20.7 us -> none  [the longest x1 6.23 us: local(): jnp.einsum('krcg,kfg->rcf', jnp.stack(returns), mortar, precision=highest)]
    all_to_all x5 -> x2, starting transfers between devices: 26 us -> 7.45 us  [the longest x1 3.82 us: spread_local(): returned = lax.all_to_all(summed, ('vol', 'rep'), 0, 0, tiled=True)]
    pallas_call x0 -> x6, Pallas kernels: none -> 17 us  [the longest x1 6.97 us: spread_local(): pl.pallas_call(functools.partial(contact_kernel, tuple(order)), out_shape...]
  transfers between devices with their start and end apart: 8 -> 23, of which waited for: 7 -> 8; matrix products, arithmetic and copies ran while one was open for 10% -> 1% of each run, Pallas kernels for 0% -> 12%
where the time goes in v3:
time: 82.1 us; the launch traced here: 81.7 us
  starting transfers between devices  32.9 us (40%)
  waiting for transfers between devices  27.9 us (34%)
  Pallas kernels  17 us (21%)
  local copies, waits for them, and re-layouts  2.79 us (3%)
  other arithmetic  0.86 us (1%)
    ppermute x21, starting transfers between devices, swap(): return lax.ppermute(value, axis, [(i, i ^ d) for i in range(count)])  25.5 us
    all_to_all x1, waiting for transfers between devices, spread_local(): returned = lax.all_to_all(summed, ('vol', 'rep'), 0, 0, tiled=True)  14.5 us
    ppermute x21, waiting for transfers between devices, swap(): return lax.ppermute(value, axis, [(i, i ^ d) for i in range(count)])  13.4 us
    pallas_call x1, Pallas kernels, spread_local(): pl.pallas_call(functools.partial(contact_kernel, tuple(order)), out_shape...  6.97 us
    pallas_call x1, Pallas kernels, spread_local(): pl.pallas_call(functools.partial(slope_kernel, rep_count, slab), out_shap...  4.93 us
    all_to_all x1, starting transfers between devices, spread_local(): returned = lax.all_to_all(summed, ('vol', 'rep'), 0, 0, tiled=True)  3.82 us
    all_to_all x1, starting transfers between devices, spread_local(): packed = lax.all_to_all(sent, ('vol', 'rep'), 0, 0, tiled=True)  3.63 us
    pallas_call x1, Pallas kernels, spread_local(): pl.pallas_call(functools.partial(project_state_kernel, share, slab), out_...  2.15 us
  transfers between devices with their start and end apart: 23, of which 8 were waited for; matrix products, arithmetic and copies ran while one was open for 1% of the time, Pallas kernels for 12%

profile of v3, /device:TPU:0, one launch (start us, length us, event | category | flops | bytes accessed | tf_op | source)
XLA Modules:
  0.0 81.7 jit_solution(12955361018374900773)
XLA Ops:
  0.0 1.1 %dynamic-slice_bitcast_fusion = (f32[224,128]{1,0:T(8,128)S(1)}, f32[224,128]{1,0:T(8,128)S(1)}, f32[224,128]{1,0:T(8,128)S(1)}, f32[224,128]{1,0:T(8,128)S(1)}) fusion(f32[112,8,128]{2,1,0:T(8,128)} %param.7, s32[]{:T(128)S(6)} %select_n.41, s32[]{:T(128)S(6)} %select_n.39, s32[]{:T(128)S(6)} %select_n.37, s32[]{:T(128)S(6)} %select_n.40), kind=kLoop, calls=%fused_computation.6 | loop fusion | bytes 917520 | tf_op jit(solution)/shard_map/reshape | solution.py:282
  1.2 3.0 %collective-permute-start = (f32[224,128]{1,0:T(8,128)S(1)}, f32[224,128]{1,0:T(8,128)S(1)}, u32[]{:S(2)}, u32[]{:S(2)}) collective-permute-start(f32[224,128]{1,0:T(8,128)S(1)} %get-tuple-element.54), channel_id=1, source_target_pairs={{0,2},{1,3},{2,0},{3,1},{4,6},{5,7},{6,4},{7,5},{8,10},{9,11},{10,... | collective-permute-start | bytes 344072 | tf_op jit(solution)/shard_map/ppermute | solution.py:276
  4.4 2.0 %collective-permute-start.6 = (f32[56,128]{1,0:T(8,128)S(1)}, f32[56,128]{1,0:T(8,128)S(1)}, u32[]{:S(2)}, u32[]{:S(2)}) collective-permute-start(f32[56,128]{1,0:T(8,128)S(1)} %constant_dynamic-slice_fusion), channel_id=1, source_target_pairs={{0,4},{4,0},{8,12},{12,8},{16,20},{20,16},{24,28},{28,24},{1,5},{5... | collective-permute-start | bytes 86024 | tf_op jit(solution)/shard_map/ppermute | solution.py:276
  6.4 0.7 add_convert_fusion
  7.1 1.2 %collective-permute-done.6 = f32[56,128]{1,0:T(8,128)S(1)} collective-permute-done((f32[56,128]{1,0:T(8,128)S(1)}, f32[56,128]{1,0:T(8,128)S(1)}, u32[]{:S(2)}, u32[]{:S(2)}) %collective-permute-start.6) | collective-permute-done | bytes 28704 | tf_op jit(solution)/shard_map/ppermute | solution.py:276
  8.3 2.0 %collective-permute-start.7 = (f32[2,56,128]{2,1,0:T(8,128)S(1)}, f32[2,56,128]{2,1,0:T(8,128)S(1)}, u32[]{:S(2)}, u32[]{:S(2)}) collective-permute-start(f32[2,56,128]{2,1,0:T(8,128)S(1)} %pad_maximum_fusion.1), channel_id=1, source_target_pairs={{0,8},{4,12},{8,0},{12,4},{16,24},{20,28},{24,16},{28,20},{1,9},{5... | collective-permute-start | bytes 172040 | tf_op jit(solution)/shard_map/ppermute | solution.py:276
  10.3 2.6 %collective-permute-start.8 = (f32[2,56,128]{2,1,0:T(8,128)S(1)}, f32[2,56,128]{2,1,0:T(8,128)S(1)}, u32[]{:S(2)}, u32[]{:S(2)}) collective-permute-start(f32[2,56,128]{2,1,0:T(8,128)S(1)} %pad_maximum_fusion.1), channel_id=1, source_target_pairs={{0,16},{4,20},{8,24},{12,28},{16,0},{20,4},{24,8},{28,12},{1,17},{... | collective-permute-start | bytes 172040 | tf_op jit(solution)/shard_map/ppermute | solution.py:276
  12.9 1.7 %collective-permute-start.2 = (f32[896,128]{1,0:T(8,128)}, f32[896,128]{1,0:T(8,128)S(1)}, u32[]{:S(2)}, u32[]{:S(2)}) collective-permute-start(f32[896,128]{1,0:T(8,128)} %bitcast.30), channel_id=1, source_target_pairs={{0,2},{1,3},{2,0},{3,1},{4,6},{5,7},{6,4},{7,5},{8,10},{9,11},{10,... | collective-permute-start | bytes 1376264 | tf_op jit(solution)/shard_map/ppermute | solution.py:276
  14.7 0.7 copy-done.3
  15.4 2.1 %shard_map.73 = f32[32,32,128]{2,1,0:T(8,128)} custom-call(s32[2]{0:T(128)S(1)} %pad_add_fusion.places_ref.after_ref, f32[32,32]{1,0:T(8,128)S(1)} %copy-done.3, f32[2,128]{1,0:T(2,128)S(1)} %pad_dynamic-slice_fusion.labels_ref, f32[224,128]{1,0:T(8,128)S(1)} %get-tuple-element.53.refs_0_, f32[224,128]{1,0:T(8,128)S(1)} %collective-permute-done.4.refs_1_, ...), custom_call_target="tpu_custom_call" | custom-call | tf_op jit(solution)/shard_map/pallas_call | solution.py:306
  17.6 1.3 %collective-permute-done.9 = f32[2,56,128]{2,1,0:T(8,128)S(1)} collective-permute-done((f32[2,56,128]{2,1,0:T(8,128)S(1)}, f32[2,56,128]{2,1,0:T(8,128)S(1)}, u32[]{:S(2)}, u32[]{:S(2)}) %collective-permute-start.9) | collective-permute-done | bytes 57376 | tf_op jit(solution)/shard_map/ppermute | solution.py:276
  18.9 3.6 %all-to-all-start = ((f32[32,32,128]{2,1,0:T(8,128)}), f32[32,32,128]{2,1,0:T(8,128)S(1)}, u32[]{:S(2)}, u32[]{:S(2)}) async-start(f32[32,32,128]{2,1,0:T(8,128)} %shard_map.73), calls=%async_computation | async-start | bytes 1048576 | tf_op jit(solution)/shard_map/all_to_all | solution.py:314
  22.9 1.3 %collective-permute-done.2.refs_2_ = f32[896,128]{1,0:T(8,128)S(1)} collective-permute-done((f32[896,128]{1,0:T(8,128)}, f32[896,128]{1,0:T(8,128)S(1)}, u32[]{:S(2)}, u32[]{:S(2)}) %collective-permute-start.2) | collective-permute-done | bytes 458784 | tf_op jit(solution)/shard_map/ppermute | solution.py:276
  24.7 1.6 %collective-permute-done.10 = f32[8,56,128]{2,1,0:T(8,128)S(1)} collective-permute-done((f32[8,56,128]{2,1,0:T(8,128)S(1)}, f32[8,56,128]{2,1,0:T(8,128)S(1)}, u32[]{:S(2)}, u32[]{:S(2)}) %collective-permute-start.10) | collective-permute-done | bytes 229408 | tf_op jit(solution)/shard_map/ppermute | solution.py:276
  26.4 1.4 %shard_map.75 = (f32[112,128]{1,0:T(8,128)S(1)}, f32[112,128]{1,0:T(8,128)S(1)}, f32[112,128]{1,0:T(8,128)S(1)}, f32[112,128]{1,0:T(8,128)S(1)}, f32[112,128]{1,...) custom-call(s32[2]{0:T(128)S(1)} %pad_add_fusion.places_ref.after_ref, ...), custom_call_target="tpu_custom_call" | custom-call | tf_op jit(solution)/shard_map/pallas_call | solution.py:319
  27.8 1.6 %collective-permute-start.11 = (f32[112,128]{1,0:T(8,128)S(1)}, f32[112,128]{1,0:T(8,128)S(1)}, u32[]{:S(2)}, u32[]{:S(2)}) collective-permute-start(f32[112,128]{1,0:T(8,128)S(1)} %get-tuple-element.40), channel_id=1, source_target_pairs={{0,4},{4,0},{8,12},{12,8},{16,20},{20,16},{24,28},{28,24},{1,5},{5... | collective-permute-start | bytes 172040 | tf_op jit(solution)/shard_map/ppermute | solution.py:276
  29.4 0.8 collective-permute-start.12
  30.1 1.2 %collective-permute-start.13 = (f32[112,128]{1,0:T(8,128)S(1)}, f32[112,128]{1,0:T(8,128)S(1)}, u32[]{:S(2)}, u32[]{:S(2)}) collective-permute-start(f32[112,128]{1,0:T(8,128)S(1)} %get-tuple-element.42), channel_id=1, source_target_pairs={{0,12},{4,8},{8,4},{12,0},{16,28},{20,24},{24,20},{28,16},{1,13},{... | collective-permute-start | bytes 172040 | tf_op jit(solution)/shard_map/ppermute | solution.py:276
  31.3 2.1 %collective-permute-start.14 = (f32[112,128]{1,0:T(8,128)S(1)}, f32[112,128]{1,0:T(8,128)S(1)}, u32[]{:S(2)}, u32[]{:S(2)}) collective-permute-start(f32[112,128]{1,0:T(8,128)S(1)} %get-tuple-element.43), channel_id=1, source_target_pairs={{0,16},{4,20},{8,24},{12,28},{16,0},{20,4},{24,8},{28,12},{1,17},{... | collective-permute-start | bytes 172040 | tf_op jit(solution)/shard_map/ppermute | solution.py:276
  33.4 1.8 %collective-permute-start.15 = (f32[112,128]{1,0:T(8,128)S(1)}, f32[112,128]{1,0:T(8,128)S(1)}, u32[]{:S(2)}, u32[]{:S(2)}) collective-permute-start(f32[112,128]{1,0:T(8,128)S(1)} %get-tuple-element.44), channel_id=1, source_target_pairs={{0,20},{4,16},{8,28},{12,24},{16,4},{20,0},{24,12},{28,8},{1,21},{... | collective-permute-start | bytes 172040 | tf_op jit(solution)/shard_map/ppermute | solution.py:276
  35.2 3.5 %collective-permute-start.16 = (f32[112,128]{1,0:T(8,128)S(1)}, f32[112,128]{1,0:T(8,128)S(1)}, u32[]{:S(2)}, u32[]{:S(2)}) collective-permute-start(f32[112,128]{1,0:T(8,128)S(1)} %get-tuple-element.45), channel_id=1, source_target_pairs={{0,24},{4,28},{8,16},{12,20},{16,8},{20,12},{24,0},{28,4},{1,25},{... | collective-permute-start | bytes 172040 | tf_op jit(solution)/shard_map/ppermute | solution.py:276
  39.0 4.9 %shard_map.74.info_ref = f32[6,896,128]{2,1,0:T(8,128)S(1)} custom-call(f32[32,32,128]{2,1,0:T(8,128)S(1)} %all-to-all-done.packed_ref, f32[512,128]{1,0:T(8,128)S(1)} %bitcast.33), custom_call_target="tpu_custom_call" | custom-call | tf_op jit(solution)/shard_map/pallas_call | solution.py:328
  44.0 2.3 %collective-permute-done.15.refs_5_ = f32[112,128]{1,0:T(8,128)S(1)} collective-permute-done((f32[112,128]{1,0:T(8,128)S(1)}, f32[112,128]{1,0:T(8,128)S(1)}, u32[]{:S(2)}, u32[]{:S(2)}) %collective-permute-start.15) | collective-permute-done | bytes 57376 | tf_op jit(solution)/shard_map/ppermute | solution.py:276
  46.3 7.0 %shard_map.76 = f32[32,32,128]{2,1,0:T(8,128)} custom-call(s32[2]{0:T(128)S(1)} %pad_add_fusion.places_ref.after_ref, f32[2,8,56,128]{3,2,1,0:T(8,128)S(1)} %pad_maximum_fusion.stiffness_ref, f32[6,896,128]{2,1,0:T(8,128)S(1)} %shard_map.74.info_ref, f32[112,128]{1,0:T(8,128)S(1)} %get-tuple-element.39.refs_0_, ...), custom_call_target="tpu_custom_call" | custom-call | tf_op jit(solution)/shard_map/pallas_call | solution.py:343
  53.3 3.8 %all-to-all-start.1 = ((f32[32,32,128]{2,1,0:T(8,128)}), f32[32,32,128]{2,1,0:T(8,128)S(1)}, u32[]{:S(2)}, u32[]{:S(2)}) async-start(f32[32,32,128]{2,1,0:T(8,128)} %shard_map.76), calls=%async_computation.1 | async-start | bytes 1048576 | tf_op jit(solution)/shard_map/all_to_all | solution.py:368
  57.1 1.0 %shard_map.77.mix_ref = bf16[2,256,256]{2,1,0:T(8,128)(2,1)S(1)} custom-call(s32[2]{0:T(128)S(1)} %pad_add_fusion.places_ref.after_ref, f32[32,32]{1,0:T(8,128)S(1)} %copy-done.4, s32[2]{0:T(128)S(1)} %pad_add_fusion.places_ref.after_ref), custom_call_target="tpu_custom_call" | custom-call | tf_op jit(solution)/shard_map/pallas_call | solution.py:361
  58.1 14.5 %all-to-all-done.1.summed_ref = f32[32,32,128]{2,1,0:T(8,128)S(1)} async-done(((f32[32,32,128]{2,1,0:T(8,128)}), f32[32,32,128]{2,1,0:T(8,128)S(1)}, u32[]{:S(2)}, u32[]{:S(2)}) %all-to-all-start.1) | async-done | bytes 524320 | tf_op jit(solution)/shard_map/all_to_all | solution.py:368
  72.6 0.6 shard_map.78
  73.3 1.3 %collective-permute-start.19 = (f32[224,128]{1,0:T(8,128)S(1)}, f32[224,128]{1,0:T(8,128)S(1)}, u32[]{:S(2)}, u32[]{:S(2)}) collective-permute-start(f32[224,128]{1,0:T(8,128)S(1)} %get-tuple-element.50), channel_id=1, source_target_pairs={{0,2},{1,3},{2,0},{3,1},{4,6},{5,7},{6,4},{7,5},{8,10},{9,11},{10,... | collective-permute-start | bytes 344072 | tf_op jit(solution)/shard_map/ppermute | solution.py:276
  75.3 4.1 %collective-permute-done.19 = f32[224,128]{1,0:T(8,128)S(1)} collective-permute-done((f32[224,128]{1,0:T(8,128)S(1)}, f32[224,128]{1,0:T(8,128)S(1)}, u32[]{:S(2)}, u32[]{:S(2)}) %collective-permute-start.19) | collective-permute-done | bytes 114720 | tf_op jit(solution)/shard_map/ppermute | solution.py:276
  79.3 1.5 %collective-permute-done.20 = f32[224,128]{1,0:T(8,128)S(1)} collective-permute-done((f32[224,128]{1,0:T(8,128)S(1)}, f32[224,128]{1,0:T(8,128)S(1)}, u32[]{:S(2)}, u32[]{:S(2)}) %collective-permute-start.20) | collective-permute-done | bytes 114720 | tf_op jit(solution)/shard_map/ppermute | solution.py:276
  80.9 0.8 copy-done.5
  (50 shorter events, 2.3 us)
Async XLA Ops:
  0.0 4.4 %copy-start = (f32[112,128]{1,0:T(8,128)S(1)}, f32[112,128]{1,0:T(8,128)}, u32[]{:S(2)}) copy-start(f32[112,128]{1,0:T(8,128)} %param.9) | copy-start | bytes 172036
  0.0 22.5 %copy-start.1 = (f32[112,8,128]{2,1,0:T(8,128)S(1)}, f32[112,8,128]{2,1,0:T(8,128)}, u32[]{:S(2)}) copy-start(f32[112,8,128]{2,1,0:T(8,128)} %param.8) | copy-start | bytes 1376260
  0.0 26.4 %copy-start.4 = (f32[32,32]{1,0:T(8,128)S(1)}, f32[32,32]{1,0:T(8,128)}, u32[]{:S(2)}) copy-start(f32[32,32]{1,0:T(8,128)} %projection_ref.5) | copy-start | bytes 12292
  1.2 11.7 %collective-permute-start = (f32[224,128]{1,0:T(8,128)S(1)}, f32[224,128]{1,0:T(8,128)S(1)}, u32[]{:S(2)}, u32[]{:S(2)}) collective-permute-start(f32[224,128]{1,0:T(8,128)S(1)} %get-tuple-element.54), channel_id=1, source_target_pairs={{0,2},{1,3},{2,0},{3,1},{4,6},{5,7},{6,4},{7,5},{8,10},{9,11},{10,... | collective-permute-start | bytes 344072 | tf_op jit(solution)/shard_map/ppermute | solution.py:276
  4.2 8.7 %collective-permute-start.4 = (f32[224,128]{1,0:T(8,128)S(1)}, f32[224,128]{1,0:T(8,128)S(1)}, u32[]{:S(2)}, u32[]{:S(2)}) collective-permute-start(f32[224,128]{1,0:T(8,128)S(1)} %get-tuple-element.55), channel_id=1, source_target_pairs={{0,1},{1,0},{2,3},{3,2},{4,5},{5,4},{6,7},{7,6},{8,9},{9,8},{10,11... | collective-permute-start | bytes 344072 | tf_op jit(solution)/shard_map/ppermute | solution.py:276
  4.2 10.5 %collective-permute-start.5 = (f32[224,128]{1,0:T(8,128)S(1)}, f32[224,128]{1,0:T(8,128)S(1)}, u32[]{:S(2)}, u32[]{:S(2)}) collective-permute-start(f32[224,128]{1,0:T(8,128)S(1)} %get-tuple-element.52), channel_id=1, source_target_pairs={{0,3},{1,2},{2,1},{3,0},{4,7},{5,6},{6,5},{7,4},{8,11},{9,10},{10,... | collective-permute-start | bytes 344072 | tf_op jit(solution)/shard_map/ppermute | solution.py:276
  4.4 3.9 %collective-permute-start.6 = (f32[56,128]{1,0:T(8,128)S(1)}, f32[56,128]{1,0:T(8,128)S(1)}, u32[]{:S(2)}, u32[]{:S(2)}) collective-permute-start(f32[56,128]{1,0:T(8,128)S(1)} %constant_dynamic-slice_fusion), channel_id=1, source_target_pairs={{0,4},{4,0},{8,12},{12,8},{16,20},{20,16},{24,28},{28,24},{1,5},{5... | collective-permute-start | bytes 86024 | tf_op jit(solution)/shard_map/ppermute | solution.py:276
  6.4 32.6 %copy-start.2 = (f32[4,128,128]{2,1,0:T(8,128)S(1)}, f32[4,128,128]{2,1,0:T(8,128)}, u32[]{:S(2)}) copy-start(f32[4,128,128]{2,1,0:T(8,128)} %param.13) | copy-start | bytes 786436
  8.3 9.3 %collective-permute-start.7 = (f32[2,56,128]{2,1,0:T(8,128)S(1)}, f32[2,56,128]{2,1,0:T(8,128)S(1)}, u32[]{:S(2)}, u32[]{:S(2)}) collective-permute-start(f32[2,56,128]{2,1,0:T(8,128)S(1)} %pad_maximum_fusion.1), channel_id=1, source_target_pairs={{0,8},{4,12},{8,0},{12,4},{16,24},{20,28},{24,16},{28,20},{1,9},{5... | collective-permute-start | bytes 172040 | tf_op jit(solution)/shard_map/ppermute | solution.py:276
  10.3 7.3 %collective-permute-start.8 = (f32[2,56,128]{2,1,0:T(8,128)S(1)}, f32[2,56,128]{2,1,0:T(8,128)S(1)}, u32[]{:S(2)}, u32[]{:S(2)}) collective-permute-start(f32[2,56,128]{2,1,0:T(8,128)S(1)} %pad_maximum_fusion.1), channel_id=1, source_target_pairs={{0,16},{4,20},{8,24},{12,28},{16,0},{20,4},{24,8},{28,12},{1,17},{... | collective-permute-start | bytes 172040 | tf_op jit(solution)/shard_map/ppermute | solution.py:276
  12.9 6.0 %collective-permute-start.9 = (f32[2,56,128]{2,1,0:T(8,128)S(1)}, f32[2,56,128]{2,1,0:T(8,128)S(1)}, u32[]{:S(2)}, u32[]{:S(2)}) collective-permute-start(f32[2,56,128]{2,1,0:T(8,128)S(1)} %pad_maximum_fusion.1), channel_id=1, source_target_pairs={{0,24},{4,28},{8,16},{12,20},{16,8},{20,12},{24,0},{28,4},{1,25},{... | collective-permute-start | bytes 172040 | tf_op jit(solution)/shard_map/ppermute | solution.py:276
  12.9 11.3 %collective-permute-start.2 = (f32[896,128]{1,0:T(8,128)}, f32[896,128]{1,0:T(8,128)S(1)}, u32[]{:S(2)}, u32[]{:S(2)}) collective-permute-start(f32[896,128]{1,0:T(8,128)} %bitcast.30), channel_id=1, source_target_pairs={{0,2},{1,3},{2,0},{3,1},{4,6},{5,7},{6,4},{7,5},{8,10},{9,11},{10,... | collective-permute-start | bytes 1376264 | tf_op jit(solution)/shard_map/ppermute | solution.py:276
  14.7 0.7 copy-start.3
  18.9 20.1 %all-to-all-start = ((f32[32,32,128]{2,1,0:T(8,128)}), f32[32,32,128]{2,1,0:T(8,128)S(1)}, u32[]{:S(2)}, u32[]{:S(2)}) async-start(f32[32,32,128]{2,1,0:T(8,128)} %shard_map.73), calls=%async_computation | async-start | bytes 1048576 | tf_op jit(solution)/shard_map/all_to_all | solution.py:314
  22.5 3.9 %collective-permute-start.1 = (f32[896,128]{1,0:T(8,128)S(1)}, f32[896,128]{1,0:T(8,128)S(1)}, u32[]{:S(2)}, u32[]{:S(2)}) collective-permute-start(f32[896,128]{1,0:T(8,128)S(1)} %bitcast.31), channel_id=1, source_target_pairs={{0,1},{1,0},{2,3},{3,2},{4,5},{5,4},{6,7},{7,6},{8,9},{9,8},{10,11... | collective-permute-start | bytes 1376264 | tf_op jit(solution)/shard_map/ppermute | solution.py:276
  24.2 2.2 %collective-permute-start.3 = (f32[896,128]{1,0:T(8,128)S(1)}, f32[896,128]{1,0:T(8,128)S(1)}, u32[]{:S(2)}, u32[]{:S(2)}) collective-permute-start(f32[896,128]{1,0:T(8,128)S(1)} %collective-permute-done.2.refs_2_), channel_id=1, source_target_pairs={{0,1},{1,0},{2,3},{3,2},{4,5},{5,4},{6,7},{7,6},{8,9},{9,8},{10,11... | collective-permute-start | bytes 1376264 | tf_op jit(solution)/shard_map/ppermute | solution.py:276
  24.2 2.1 %collective-permute-start.10 = (f32[8,56,128]{2,1,0:T(8,128)S(1)}, f32[8,56,128]{2,1,0:T(8,128)S(1)}, u32[]{:S(2)}, u32[]{:S(2)}) collective-permute-start(f32[8,56,128]{2,1,0:T(8,128)S(1)} %constant_dynamic-update-slice_fusion), channel_id=1, source_target_pairs={{0,1},{1,0},{2,3},{3,2},{4,5},{5,4},{6,7},{7,6},{8,9},{9,8},{10,11... | collective-permute-start | bytes 688136 | tf_op jit(solution)/shard_map/ppermute | solution.py:276
  27.8 7.4 %collective-permute-start.11 = (f32[112,128]{1,0:T(8,128)S(1)}, f32[112,128]{1,0:T(8,128)S(1)}, u32[]{:S(2)}, u32[]{:S(2)}) collective-permute-start(f32[112,128]{1,0:T(8,128)S(1)} %get-tuple-element.40), channel_id=1, source_target_pairs={{0,4},{4,0},{8,12},{12,8},{16,20},{20,16},{24,28},{28,24},{1,5},{5... | collective-permute-start | bytes 172040 | tf_op jit(solution)/shard_map/ppermute | solution.py:276
  29.4 9.3 %collective-permute-start.12 = (f32[112,128]{1,0:T(8,128)S(1)}, f32[112,128]{1,0:T(8,128)S(1)}, u32[]{:S(2)}, u32[]{:S(2)}) collective-permute-start(f32[112,128]{1,0:T(8,128)S(1)} %get-tuple-element.41), channel_id=1, source_target_pairs={{0,8},{4,12},{8,0},{12,4},{16,24},{20,28},{24,16},{28,20},{1,9},{5... | collective-permute-start | bytes 172040 | tf_op jit(solution)/shard_map/ppermute | solution.py:276
  30.1 13.8 %collective-permute-start.13 = (f32[112,128]{1,0:T(8,128)S(1)}, f32[112,128]{1,0:T(8,128)S(1)}, u32[]{:S(2)}, u32[]{:S(2)}) collective-permute-start(f32[112,128]{1,0:T(8,128)S(1)} %get-tuple-element.42), channel_id=1, source_target_pairs={{0,12},{4,8},{8,4},{12,0},{16,28},{20,24},{24,20},{28,16},{1,13},{... | collective-permute-start | bytes 172040 | tf_op jit(solution)/shard_map/ppermute | solution.py:276
  31.3 12.6 %collective-permute-start.14 = (f32[112,128]{1,0:T(8,128)S(1)}, f32[112,128]{1,0:T(8,128)S(1)}, u32[]{:S(2)}, u32[]{:S(2)}) collective-permute-start(f32[112,128]{1,0:T(8,128)S(1)} %get-tuple-element.43), channel_id=1, source_target_pairs={{0,16},{4,20},{8,24},{12,28},{16,0},{20,4},{24,8},{28,12},{1,17},{... | collective-permute-start | bytes 172040 | tf_op jit(solution)/shard_map/ppermute | solution.py:276
  33.4 12.9 %collective-permute-start.15 = (f32[112,128]{1,0:T(8,128)S(1)}, f32[112,128]{1,0:T(8,128)S(1)}, u32[]{:S(2)}, u32[]{:S(2)}) collective-permute-start(f32[112,128]{1,0:T(8,128)S(1)} %get-tuple-element.44), channel_id=1, source_target_pairs={{0,20},{4,16},{8,28},{12,24},{16,4},{20,0},{24,12},{28,8},{1,21},{... | collective-permute-start | bytes 172040 | tf_op jit(solution)/shard_map/ppermute | solution.py:276
  35.2 11.1 %collective-permute-start.16 = (f32[112,128]{1,0:T(8,128)S(1)}, f32[112,128]{1,0:T(8,128)S(1)}, u32[]{:S(2)}, u32[]{:S(2)}) collective-permute-start(f32[112,128]{1,0:T(8,128)S(1)} %get-tuple-element.45), channel_id=1, source_target_pairs={{0,24},{4,28},{8,16},{12,20},{16,8},{20,12},{24,0},{28,4},{1,25},{... | collective-permute-start | bytes 172040 | tf_op jit(solution)/shard_map/ppermute | solution.py:276
  38.7 7.6 %collective-permute-start.17 = (f32[112,128]{1,0:T(8,128)S(1)}, f32[112,128]{1,0:T(8,128)S(1)}, u32[]{:S(2)}, u32[]{:S(2)}) collective-permute-start(f32[112,128]{1,0:T(8,128)S(1)} %get-tuple-element.46), channel_id=1, source_target_pairs={{0,28},{4,24},{8,20},{12,16},{16,12},{20,8},{24,4},{28,0},{1,29},{... | collective-permute-start | bytes 172040 | tf_op jit(solution)/shard_map/ppermute | solution.py:276
  53.3 19.4 %all-to-all-start.1 = ((f32[32,32,128]{2,1,0:T(8,128)}), f32[32,32,128]{2,1,0:T(8,128)S(1)}, u32[]{:S(2)}, u32[]{:S(2)}) async-start(f32[32,32,128]{2,1,0:T(8,128)} %shard_map.76), calls=%async_computation.1 | async-start | bytes 1048576 | tf_op jit(solution)/shard_map/all_to_all | solution.py:368
  73.2 2.0 %collective-permute-start.18 = (f32[224,128]{1,0:T(8,128)S(1)}, f32[224,128]{1,0:T(8,128)S(1)}, u32[]{:S(2)}, u32[]{:S(2)}) collective-permute-start(f32[224,128]{1,0:T(8,128)S(1)} %get-tuple-element.51), channel_id=1, source_target_pairs={{0,1},{1,0},{2,3},{3,2},{4,5},{5,4},{6,7},{7,6},{8,9},{9,8},{10,11... | collective-permute-start | bytes 344072 | tf_op jit(solution)/shard_map/ppermute | solution.py:276
  73.3 6.0 %collective-permute-start.19 = (f32[224,128]{1,0:T(8,128)S(1)}, f32[224,128]{1,0:T(8,128)S(1)}, u32[]{:S(2)}, u32[]{:S(2)}) collective-permute-start(f32[224,128]{1,0:T(8,128)S(1)} %get-tuple-element.50), channel_id=1, source_target_pairs={{0,2},{1,3},{2,0},{3,1},{4,6},{5,7},{6,4},{7,5},{8,10},{9,11},{10,... | collective-permute-start | bytes 344072 | tf_op jit(solution)/shard_map/ppermute | solution.py:276
  74.6 6.3 %collective-permute-start.20 = (f32[224,128]{1,0:T(8,128)S(1)}, f32[224,128]{1,0:T(8,128)S(1)}, u32[]{:S(2)}, u32[]{:S(2)}) collective-permute-start(f32[224,128]{1,0:T(8,128)S(1)} %get-tuple-element.49), channel_id=1, source_target_pairs={{0,3},{1,2},{2,1},{3,0},{4,7},{5,6},{6,5},{7,4},{8,11},{9,10},{10,... | collective-permute-start | bytes 344072 | tf_op jit(solution)/shard_map/ppermute | solution.py:276
  80.9 0.8 copy-start.5

commit v4 on v3

--- a/solution.py
+++ b/solution.py
@@ -37,6 +37,10 @@
 
 def one_where(cond):
     return jnp.where(cond, 1.0, 0.0).astype(jnp.bfloat16)
+
+
+def starts(slab):
+    return [min(b, slab - ROWS) for b in range(0, slab, ROWS)]
 
 
 def mixer(projection, channel_of, height, rep_index, rep_count, share, group):
@@ -62,24 +66,24 @@
         mix_ref[at] = part.astype(jnp.float32).T.astype(jnp.bfloat16)
 
 
-def project_state_kernel(share, slab, places_ref, projection_ref, labels_ref, *refs):
+def state_mixer_kernel(rep_count, share, places_ref, table_ref, mix_ref):
+    channels = table_ref.shape[0] - ROWS
+    projection = table_ref[ROWS:, 0:channels]
+    parts = mixer(projection, lambda i: i, mix_ref.shape[1], places_ref[1], rep_count, share, ROWS)
+    for at, part in enumerate(parts):
+        mix_ref[at] = part
+
+
+def project_state_kernel(share, slab, places_ref, mix_ref, table_ref, *refs):
     slab_refs, out_ref = refs[:-1], refs[-1]
-    channels, padded, faces = out_ref.shape
-    rep_count = len(slab_refs)
-    mix = mixer(projection_ref[...], lambda i: i, channels * ROWS, places_ref[1], rep_count, share, ROWS)
-    count = labels_ref.shape[0]
-    spare = jnp.zeros((padded - slab - count, faces), jnp.float32)
-    tail = jnp.concatenate([labels_ref[...], spare], axis=0) if spare.shape[0] else labels_ref[...]
-    for b in range(0, slab, ROWS):
-        count = min(ROWS, slab - b)
-        pieces = []
-        for ref in slab_refs:
-            pieces.append(ref[pl.ds(b * share, count * share), :])
-            if count < ROWS:
-                pieces.append(jnp.zeros(((ROWS - count) * share, faces), jnp.float32))
+    channels, length, faces = out_ref.shape
+    mix = mix_ref[0], mix_ref[1]
+    for b in starts(slab):
+        pieces = [ref[pl.ds(b * share, ROWS * share), :] for ref in slab_refs]
         out = product3(mix, halves(jnp.concatenate(pieces, axis=0))).reshape(channels, ROWS, faces)
-        out_ref[:, pl.ds(b, count), :] = out[:, :count]
-    out_ref[:, slab:padded, :] = jnp.broadcast_to(tail[None], (channels, padded - slab, faces))
+        out_ref[:, pl.ds(b, ROWS), :] = out
+    tail = table_ref[pl.ds(places_ref[1] * (length - slab), length - slab), :]
+    out_ref[:, slab:length, :] = jnp.broadcast_to(tail[None], (channels,) + tail.shape)
 
 
 def project_move_kernel(rep_count, share, places_ref, projection_ref, *refs):
@@ -103,15 +107,12 @@
 
 
 def back_kernel(rep_count, share, mix_ref, summed_ref, out_ref):
-    channels, padded, faces = summed_ref.shape
-    size = channels * ROWS
+    channels, slab, faces = summed_ref.shape
     mix = mix_ref[0], mix_ref[1]
-    rows = out_ref.shape[1]
-    for b in range(0, padded, ROWS):
-        values = halves(summed_ref[:, pl.ds(b, ROWS), :].reshape(size, faces))
+    for b in starts(slab):
+        values = halves(summed_ref[:, pl.ds(b, ROWS), :].reshape(channels * ROWS, faces))
         out = product3(mix, values).reshape(rep_count, ROWS * share, faces)
-        count = min(ROWS * share, rows - b * share)
-        out_ref[:, pl.ds(b * share, count), :] = out[:, :count]
+        out_ref[:, pl.ds(b * share, ROWS * share), :] = out
 
 
 def map_parts(values, partner_count, faces, info_ref, maps_ref, mapped_ref):
@@ -241,12 +242,9 @@
         for k in range(1, partner_count):
             back += product(turned(k, r), back_ref[k])
         tangent_ref[span, :] = tangent_ref[span, :] - back[:, :faces] - back[:, faces:]
-    devices, padded, _ = out_ref.shape
-    slab = total // devices
+    devices, slab, _ = out_ref.shape
     for device in range(devices):
-        out_ref[device, 0:slab, :] = tangent_ref[device * slab : (device + 1) * slab, :]
-        if padded > slab:
-            out_ref[device, slab:padded, :] = jnp.zeros((padded - slab, faces), jnp.float32)
+        out_ref[device] = tangent_ref[device * slab : (device + 1) * slab, :]
 
 
 def spread_local(surface_state, direction, stiffness, partners, contact_owner, projection, mortar):
@@ -257,7 +255,6 @@
     channels = projection.shape[0]
     partner_count = partners.shape[1]
     slab = blocks // rep_count
-    padded = -(-slab // ROWS) * ROWS
     total = blocks * vol_count
     size = channels * ROWS
     vmem = pl.BlockSpec(memory_space=pltpu.VMEM)
@@ -283,7 +280,6 @@
         for d in range(rep_count)
     ])
 
-    state[rep_count // 2], direction = lax.optimization_barrier((state[rep_count // 2], direction))
 
     move = {0: direction.reshape(blocks * share, faces)}
     step = rep_count // 2
@@ -294,22 +290,30 @@
     half = blocks // 2
     stiffness = lax.dynamic_slice_in_dim(stiffness, rep_index % 2 * half, half, 0)
     stiffness = jnp.stack([stiffness, swap(stiffness, "vol", 1)])
-    far = list(range(2, vol_count, 2))
+    far = list(range(vol_count - 2, 0, -2))
     order = [d ^ near for d in [0] + far for near in range(2)]
+    stiffness, state[0] = lax.optimization_barrier((stiffness, state[0]))
     stiffness = [stiffness] + [swap(stiffness, "vol", d) for d in far]
 
     taken = ROWS // rep_count
     labels = jnp.concatenate([partners.T, contact_owner[None, :]], axis=0).astype(jnp.float32)
     labels = jnp.pad(labels, ((0, ROWS - partner_count - 1), (0, faces - blocks)))
-    labels = lax.dynamic_slice_in_dim(labels, rep_index * taken, taken, 0)
+    table = jnp.concatenate([labels, jnp.pad(projection, ((0, 0), (0, faces - channels)))], axis=0)
+    state_mix = pl.pallas_call(
+        functools.partial(state_mixer_kernel, rep_count, share),
+        out_shape=array(2, size, size, dtype=jnp.bfloat16),
+        in_specs=[smem, vmem],
+        out_specs=vmem,
+        compiler_params=params,
+    )(places, table)
 
     sent = pl.pallas_call(
         functools.partial(project_state_kernel, share, slab),
-        out_shape=array(channels, padded, faces),
+        out_shape=array(channels, slab + taken, faces),
         in_specs=[smem] + [vmem] * (2 + rep_count),
         out_specs=vmem,
         compiler_params=params,
-    )(places, projection, labels, *state)
+    )(places, state_mix, table, *state)
     sent, stiffness = lax.optimization_barrier((sent, stiffness))
     packed = lax.all_to_all(sent, ("vol", "rep"), 0, 0, tiled=True)
 
@@ -342,7 +346,7 @@
 
     summed = pl.pallas_call(
         functools.partial(contact_kernel, tuple(order)),
-        out_shape=array(devices, padded, faces),
+        out_shape=array(devices, slab, faces),
         in_specs=[smem] + [vmem] * (2 + vol_count),
         out_specs=vmem,
         scratch_shapes=[
@@ -488,7 +492,7 @@
         and blocks % (ROWS // 2 * rep_count) == 0
         and blocks % (2 * ROWS) == 0
         and ROWS % rep_count == 0
-        and -(blocks // rep_count) % ROWS >= ROWS // rep_count
+        and blocks // rep_count >= ROWS
         and min(vol_count, rep_count) > 1
         and total % LANES == 0
         and partner_shape[1] < ROWS

time: 82.1 us -> 81.7 us (level)
  starting transfers between devices: 32.9 us -> 31.8 us
    all_to_all x1, starting transfers between devices: 3.63 us -> 2.72 us  [spread_local(): packed = lax.all_to_all(sent, ('vol', 'rep'), 0, 0, tiled=True)]
    pallas_call x0 -> x1, Pallas kernels: none -> 0.87 us  [spread_local(): pl.pallas_call(functools.partial(state_mixer_kernel, rep_count, share), o...]
  transfers between devices with their start and end apart: 23 -> 23, of which waited for: 8 -> 8; matrix products, arithmetic and copies ran while one was open for 1% -> 3% of each run, Pallas kernels for 12% -> 12%
where the time goes in v4:
time: 81.7 us; the launch traced here: 81.2 us
  starting transfers between devices  31.8 us (39%)
  waiting for transfers between devices  27.2 us (33%)
  Pallas kernels  17.6 us (22%)
  local copies, waits for them, and re-layouts  2.82 us (3%)
  other arithmetic  1.54 us (2%)
    ppermute x21, starting transfers between devices, swap(): return lax.ppermute(value, axis, [(i, i ^ d) for i in range(count)])  24.8 us
    all_to_all x1, waiting for transfers between devices, spread_local(): returned = lax.all_to_all(summed, ('vol', 'rep'), 0, 0, tiled=True)  14.5 us
    ppermute x21, waiting for transfers between devices, swap(): return lax.ppermute(value, axis, [(i, i ^ d) for i in range(count)])  12.6 us
    pallas_call x1, Pallas kernels, spread_local(): pl.pallas_call(functools.partial(contact_kernel, tuple(order)), out_shape...  7 us
    pallas_call x1, Pallas kernels, spread_local(): pl.pallas_call(functools.partial(slope_kernel, rep_count, slab), out_shap...  4.92 us
    all_to_all x1, starting transfers between devices, spread_local(): returned = lax.all_to_all(summed, ('vol', 'rep'), 0, 0, tiled=True)  4.31 us
    all_to_all x1, starting transfers between devices, spread_local(): packed = lax.all_to_all(sent, ('vol', 'rep'), 0, 0, tiled=True)  2.72 us
    pallas_call x1, Pallas kernels, spread_local(): pl.pallas_call(functools.partial(project_state_kernel, share, slab), out_...  1.93 us
  transfers between devices with their start and end apart: 23, of which 8 were waited for; matrix products, arithmetic and copies ran while one was open for 3% of the time, Pallas kernels for 12%

profile of v4, /device:TPU:0, one launch (start us, length us, event | category | flops | bytes accessed | tf_op | source)
XLA Modules:
  0.0 81.2 jit_solution(7653734031195181225)
XLA Ops:
  0.0 0.8 %copy-done = f32[112,128]{1,0:T(8,128)S(1)} copy-done((f32[112,128]{1,0:T(8,128)S(1)}, f32[112,128]{1,0:T(8,128)}, u32[]{:S(2)}) %copy-start) | copy-done | bytes 57368
  0.8 3.0 %collective-permute-start.3 = (f32[56,128]{1,0:T(8,128)S(1)}, f32[56,128]{1,0:T(8,128)S(1)}, u32[]{:S(2)}, u32[]{:S(2)}) collective-permute-start(f32[56,128]{1,0:T(8,128)S(1)} %constant_dynamic-slice_fusion), channel_id=1, source_target_pairs={{0,4},{4,0},{8,12},{12,8},{16,20},{20,16},{24,28},{28,24},{1,5},{5... | collective-permute-start | bytes 86024 | tf_op jit(solution)/shard_map/ppermute | solution.py:273
  3.8 1.1 %dynamic-slice_bitcast_fusion = (f32[224,128]{1,0:T(8,128)S(1)}, f32[224,128]{1,0:T(8,128)S(1)}, f32[224,128]{1,0:T(8,128)S(1)}, f32[224,128]{1,0:T(8,128)S(1)}) fusion(f32[112,8,128]{2,1,0:T(8,128)} %param.7, s32[]{:T(128)S(6)} %select_n.39, s32[]{:T(128)S(6)} %select_n.37, s32[]{:T(128)S(6)} %select_n.36, s32[]{:T(128)S(6)} %select_n.38), kind=kLoop, calls=%fused_computation.6 | loop fusion | bytes 917520 | tf_op jit(solution)/shard_map/reshape | solution.py:279
  5.0 1.6 %collective-permute-start.5 = (f32[224,128]{1,0:T(8,128)S(1)}, f32[224,128]{1,0:T(8,128)S(1)}, u32[]{:S(2)}, u32[]{:S(2)}) collective-permute-start(f32[224,128]{1,0:T(8,128)S(1)} %get-tuple-element.55), channel_id=1, source_target_pairs={{0,2},{1,3},{2,0},{3,1},{4,6},{5,7},{6,4},{7,5},{8,10},{9,11},{10,... | collective-permute-start | bytes 344072 | tf_op jit(solution)/shard_map/ppermute | solution.py:273
  6.8 1.5 %collective-permute-start.1 = (f32[896,128]{1,0:T(8,128)}, f32[896,128]{1,0:T(8,128)S(1)}, u32[]{:S(2)}, u32[]{:S(2)}) collective-permute-start(f32[896,128]{1,0:T(8,128)} %bitcast.30), channel_id=1, source_target_pairs={{0,2},{1,3},{2,0},{3,1},{4,6},{5,7},{6,4},{7,5},{8,10},{9,11},{10,... | collective-permute-start | bytes 1376264 | tf_op jit(solution)/shard_map/ppermute | solution.py:273
  8.3 0.7 add_convert_fusion
  9.0 0.7 select_maximum_fusion.table_ref
  9.8 3.7 %collective-permute-start.7 = (f32[2,56,128]{2,1,0:T(8,128)S(1)}, f32[2,56,128]{2,1,0:T(8,128)S(1)}, u32[]{:S(2)}, u32[]{:S(2)}) collective-permute-start(f32[2,56,128]{2,1,0:T(8,128)S(1)} %pad_maximum_fusion.1), channel_id=1, source_target_pairs={{0,24},{4,28},{8,16},{12,20},{16,8},{20,12},{24,0},{28,4},{1,25},{... | collective-permute-start | bytes 172040 | tf_op jit(solution)/shard_map/ppermute | solution.py:273
  13.4 0.8 collective-permute-start.9
  14.3 0.9 %shard_map.73.mix_ref = bf16[2,256,256]{2,1,0:T(8,128)(2,1)S(1)} custom-call(s32[2]{0:T(128)S(1)} %pad_add_fusion.places_ref.after_ref, f32[40,128]{1,0:T(8,128)S(1)} %select_maximum_fusion.table_ref), custom_call_target="tpu_custom_call" | custom-call | tf_op jit(solution)/shard_map/pallas_call | solution.py:302
  15.2 1.9 %shard_map.74 = f32[32,30,128]{2,1,0:T(8,128)} custom-call(s32[2]{0:T(128)S(1)} %pad_add_fusion.places_ref.after_ref, bf16[2,256,256]{2,1,0:T(8,128)(2,1)S(1)} %shard_map.73.mix_ref, f32[40,128]{1,0:T(8,128)S(1)} %select_maximum_fusion.table_ref, f32[224,128]{1,0:T(8,128)S(1)} %get-tuple-element.27.refs_0_, f32[224,128]{1,0:T(8,128)S(1)} %collective-permute-done.4.refs_1_, ...), custom_call_target="tpu_custom_call" | custom-call | tf_op jit(solution)/shard_map/pallas_call | solution.py:310
  17.1 1.6 %collective-permute-done.8 = f32[2,56,128]{2,1,0:T(8,128)S(1)} collective-permute-done((f32[2,56,128]{2,1,0:T(8,128)S(1)}, f32[2,56,128]{2,1,0:T(8,128)S(1)}, u32[]{:S(2)}, u32[]{:S(2)}) %collective-permute-start.8) | collective-permute-done | bytes 57376 | tf_op jit(solution)/shard_map/ppermute | solution.py:273
  18.8 2.7 %all-to-all-start = ((f32[32,30,128]{2,1,0:T(8,128)}), f32[32,30,128]{2,1,0:T(8,128)S(1)}, u32[]{:S(2)}, u32[]{:S(2)}) async-start(f32[32,30,128]{2,1,0:T(8,128)} %shard_map.74), calls=%async_computation | async-start | bytes 1048576 | tf_op jit(solution)/shard_map/all_to_all | solution.py:318
  21.9 0.9 %collective-permute-done.1.refs_2_ = f32[896,128]{1,0:T(8,128)S(1)} collective-permute-done((f32[896,128]{1,0:T(8,128)}, f32[896,128]{1,0:T(8,128)S(1)}, u32[]{:S(2)}, u32[]{:S(2)}) %collective-permute-start.1) | collective-permute-done | bytes 458784 | tf_op jit(solution)/shard_map/ppermute | solution.py:273
  23.3 1.6 %collective-permute-done.10 = f32[8,56,128]{2,1,0:T(8,128)S(1)} collective-permute-done((f32[8,56,128]{2,1,0:T(8,128)S(1)}, f32[8,56,128]{2,1,0:T(8,128)S(1)}, u32[]{:S(2)}, u32[]{:S(2)}) %collective-permute-start.10) | collective-permute-done | bytes 229408 | tf_op jit(solution)/shard_map/ppermute | solution.py:273
  25.0 1.4 %shard_map.76 = (f32[112,128]{1,0:T(8,128)S(1)}, f32[112,128]{1,0:T(8,128)S(1)}, f32[112,128]{1,0:T(8,128)S(1)}, f32[112,128]{1,0:T(8,128)S(1)}, f32[112,128]{1,...) custom-call(s32[2]{0:T(128)S(1)} %pad_add_fusion.places_ref.after_ref, ...), custom_call_target="tpu_custom_call" | custom-call | tf_op jit(solution)/shard_map/pallas_call | solution.py:323
  26.4 1.3 %collective-permute-start.11 = (f32[112,128]{1,0:T(8,128)S(1)}, f32[112,128]{1,0:T(8,128)S(1)}, u32[]{:S(2)}, u32[]{:S(2)}) collective-permute-start(f32[112,128]{1,0:T(8,128)S(1)} %get-tuple-element.40), channel_id=1, source_target_pairs={{0,4},{4,0},{8,12},{12,8},{16,20},{20,16},{24,28},{28,24},{1,5},{5... | collective-permute-start | bytes 172040 | tf_op jit(solution)/shard_map/ppermute | solution.py:273
  27.7 1.5 %collective-permute-start.12 = (f32[112,128]{1,0:T(8,128)S(1)}, f32[112,128]{1,0:T(8,128)S(1)}, u32[]{:S(2)}, u32[]{:S(2)}) collective-permute-start(f32[112,128]{1,0:T(8,128)S(1)} %get-tuple-element.41), channel_id=1, source_target_pairs={{0,8},{4,12},{8,0},{12,4},{16,24},{20,28},{24,16},{28,20},{1,9},{5... | collective-permute-start | bytes 172040 | tf_op jit(solution)/shard_map/ppermute | solution.py:273
  29.2 0.8 collective-permute-start.13
  29.9 2.6 %collective-permute-start.14 = (f32[112,128]{1,0:T(8,128)S(1)}, f32[112,128]{1,0:T(8,128)S(1)}, u32[]{:S(2)}, u32[]{:S(2)}) collective-permute-start(f32[112,128]{1,0:T(8,128)S(1)} %get-tuple-element.43), channel_id=1, source_target_pairs={{0,16},{4,20},{8,24},{12,28},{16,0},{20,4},{24,8},{28,12},{1,17},{... | collective-permute-start | bytes 172040 | tf_op jit(solution)/shard_map/ppermute | solution.py:273
  32.5 1.0 %collective-permute-start.15 = (f32[112,128]{1,0:T(8,128)S(1)}, f32[112,128]{1,0:T(8,128)S(1)}, u32[]{:S(2)}, u32[]{:S(2)}) collective-permute-start(f32[112,128]{1,0:T(8,128)S(1)} %get-tuple-element.44), channel_id=1, source_target_pairs={{0,20},{4,16},{8,28},{12,24},{16,4},{20,0},{24,12},{28,8},{1,21},{... | collective-permute-start | bytes 172040 | tf_op jit(solution)/shard_map/ppermute | solution.py:273
  33.6 3.3 %collective-permute-start.16 = (f32[112,128]{1,0:T(8,128)S(1)}, f32[112,128]{1,0:T(8,128)S(1)}, u32[]{:S(2)}, u32[]{:S(2)}) collective-permute-start(f32[112,128]{1,0:T(8,128)S(1)} %get-tuple-element.45), channel_id=1, source_target_pairs={{0,24},{4,28},{8,16},{12,20},{16,8},{20,12},{24,0},{28,4},{1,25},{... | collective-permute-start | bytes 172040 | tf_op jit(solution)/shard_map/ppermute | solution.py:273
  37.6 4.9 %shard_map.75.info_ref = f32[6,896,128]{2,1,0:T(8,128)S(1)} custom-call(f32[32,30,128]{2,1,0:T(8,128)S(1)} %all-to-all-done.packed_ref, f32[512,128]{1,0:T(8,128)S(1)} %bitcast.33), custom_call_target="tpu_custom_call" | custom-call | tf_op jit(solution)/shard_map/pallas_call | solution.py:332
  42.6 2.8 %collective-permute-done.15.refs_5_ = f32[112,128]{1,0:T(8,128)S(1)} collective-permute-done((f32[112,128]{1,0:T(8,128)S(1)}, f32[112,128]{1,0:T(8,128)S(1)}, u32[]{:S(2)}, u32[]{:S(2)}) %collective-permute-start.15) | collective-permute-done | bytes 57376 | tf_op jit(solution)/shard_map/ppermute | solution.py:273
  45.3 7.0 %shard_map.77 = f32[32,28,128]{2,1,0:T(8,128)} custom-call(s32[2]{0:T(128)S(1)} %pad_add_fusion.places_ref.after_ref, f32[2,8,56,128]{3,2,1,0:T(8,128)S(1)} %pad_maximum_fusion.stiffness_ref, f32[6,896,128]{2,1,0:T(8,128)S(1)} %shard_map.75.info_ref, f32[112,128]{1,0:T(8,128)S(1)} %get-tuple-element.39.refs_0_, ...), custom_call_target="tpu_custom_call" | custom-call | tf_op jit(solution)/shard_map/pallas_call | solution.py:347
  52.3 4.3 %all-to-all-start.1 = ((f32[32,28,128]{2,1,0:T(8,128)}), f32[32,28,128]{2,1,0:T(8,128)S(1)}, u32[]{:S(2)}, u32[]{:S(2)}) async-start(f32[32,28,128]{2,1,0:T(8,128)} %shard_map.77), calls=%async_computation.1 | async-start | bytes 1048576 | tf_op jit(solution)/shard_map/all_to_all | solution.py:372
  56.7 1.0 %shard_map.78.mix_ref = bf16[2,256,256]{2,1,0:T(8,128)(2,1)S(1)} custom-call(s32[2]{0:T(128)S(1)} %pad_add_fusion.places_ref.after_ref, f32[32,32]{1,0:T(8,128)S(1)} %copy-done.3, s32[2]{0:T(128)S(1)} %pad_add_fusion.places_ref.after_ref), custom_call_target="tpu_custom_call" | custom-call | tf_op jit(solution)/shard_map/pallas_call | solution.py:365
  57.7 14.5 %all-to-all-done.1.summed_ref = f32[32,28,128]{2,1,0:T(8,128)S(1)} async-done(((f32[32,28,128]{2,1,0:T(8,128)}), f32[32,28,128]{2,1,0:T(8,128)S(1)}, u32[]{:S(2)}, u32[]{:S(2)}) %all-to-all-start.1) | async-done | bytes 458784 | tf_op jit(solution)/shard_map/all_to_all | solution.py:372
  72.9 1.3 %collective-permute-start.19 = (f32[224,128]{1,0:T(8,128)S(1)}, f32[224,128]{1,0:T(8,128)S(1)}, u32[]{:S(2)}, u32[]{:S(2)}) collective-permute-start(f32[224,128]{1,0:T(8,128)S(1)} %get-tuple-element.50), channel_id=1, source_target_pairs={{0,2},{1,3},{2,0},{3,1},{4,6},{5,7},{6,4},{7,5},{8,10},{9,11},{10,... | collective-permute-start | bytes 344072 | tf_op jit(solution)/shard_map/ppermute | solution.py:273
  74.8 4.1 %collective-permute-done.19 = f32[224,128]{1,0:T(8,128)S(1)} collective-permute-done((f32[224,128]{1,0:T(8,128)S(1)}, f32[224,128]{1,0:T(8,128)S(1)}, u32[]{:S(2)}, u32[]{:S(2)}) %collective-permute-start.19) | collective-permute-done | bytes 114720 | tf_op jit(solution)/shard_map/ppermute | solution.py:273
  78.9 1.5 %collective-permute-done.20 = f32[224,128]{1,0:T(8,128)S(1)} collective-permute-done((f32[224,128]{1,0:T(8,128)S(1)}, f32[224,128]{1,0:T(8,128)S(1)}, u32[]{:S(2)}, u32[]{:S(2)}) %collective-permute-start.20) | collective-permute-done | bytes 114720 | tf_op jit(solution)/shard_map/ppermute | solution.py:273
  80.5 0.8 copy-done.4
  (49 shorter events, 3.5 us)
Async XLA Ops:
  0.0 0.8 %copy-start = (f32[112,128]{1,0:T(8,128)S(1)}, f32[112,128]{1,0:T(8,128)}, u32[]{:S(2)}) copy-start(f32[112,128]{1,0:T(8,128)} %param.9) | copy-start | bytes 172036
  0.0 21.6 %copy-start.1 = (f32[112,8,128]{2,1,0:T(8,128)S(1)}, f32[112,8,128]{2,1,0:T(8,128)}, u32[]{:S(2)}) copy-start(f32[112,8,128]{2,1,0:T(8,128)} %param.8) | copy-start | bytes 1376260
  0.0 25.0 %copy-start.3 = (f32[32,32]{1,0:T(8,128)S(1)}, f32[32,32]{1,0:T(8,128)}, u32[]{:S(2)}) copy-start(f32[32,32]{1,0:T(8,128)} %projection_ref.3) | copy-start | bytes 12292
  0.8 8.9 %collective-permute-start.3 = (f32[56,128]{1,0:T(8,128)S(1)}, f32[56,128]{1,0:T(8,128)S(1)}, u32[]{:S(2)}, u32[]{:S(2)}) collective-permute-start(f32[56,128]{1,0:T(8,128)S(1)} %constant_dynamic-slice_fusion), channel_id=1, source_target_pairs={{0,4},{4,0},{8,12},{12,8},{16,20},{20,16},{24,28},{28,24},{1,5},{5... | collective-permute-start | bytes 86024 | tf_op jit(solution)/shard_map/ppermute | solution.py:273
  4.9 8.5 %collective-permute-start.4 = (f32[224,128]{1,0:T(8,128)S(1)}, f32[224,128]{1,0:T(8,128)S(1)}, u32[]{:S(2)}, u32[]{:S(2)}) collective-permute-start(f32[224,128]{1,0:T(8,128)S(1)} %get-tuple-element.53), channel_id=1, source_target_pairs={{0,1},{1,0},{2,3},{3,2},{4,5},{5,4},{6,7},{7,6},{8,9},{9,8},{10,11... | collective-permute-start | bytes 344072 | tf_op jit(solution)/shard_map/ppermute | solution.py:273
  5.0 8.5 %collective-permute-start.5 = (f32[224,128]{1,0:T(8,128)S(1)}, f32[224,128]{1,0:T(8,128)S(1)}, u32[]{:S(2)}, u32[]{:S(2)}) collective-permute-start(f32[224,128]{1,0:T(8,128)S(1)} %get-tuple-element.55), channel_id=1, source_target_pairs={{0,2},{1,3},{2,0},{3,1},{4,6},{5,7},{6,4},{7,5},{8,10},{9,11},{10,... | collective-permute-start | bytes 344072 | tf_op jit(solution)/shard_map/ppermute | solution.py:273
  6.5 8.7 %collective-permute-start.6 = (f32[224,128]{1,0:T(8,128)S(1)}, f32[224,128]{1,0:T(8,128)S(1)}, u32[]{:S(2)}, u32[]{:S(2)}) collective-permute-start(f32[224,128]{1,0:T(8,128)S(1)} %get-tuple-element.52), channel_id=1, source_target_pairs={{0,3},{1,2},{2,1},{3,0},{4,7},{5,6},{6,5},{7,4},{8,11},{9,10},{10,... | collective-permute-start | bytes 344072 | tf_op jit(solution)/shard_map/ppermute | solution.py:273
  6.8 16.0 %collective-permute-start.1 = (f32[896,128]{1,0:T(8,128)}, f32[896,128]{1,0:T(8,128)S(1)}, u32[]{:S(2)}, u32[]{:S(2)}) collective-permute-start(f32[896,128]{1,0:T(8,128)} %bitcast.30), channel_id=1, source_target_pairs={{0,2},{1,3},{2,0},{3,1},{4,6},{5,7},{6,4},{7,5},{8,10},{9,11},{10,... | collective-permute-start | bytes 1376264 | tf_op jit(solution)/shard_map/ppermute | solution.py:273
  9.8 7.4 %collective-permute-start.7 = (f32[2,56,128]{2,1,0:T(8,128)S(1)}, f32[2,56,128]{2,1,0:T(8,128)S(1)}, u32[]{:S(2)}, u32[]{:S(2)}) collective-permute-start(f32[2,56,128]{2,1,0:T(8,128)S(1)} %pad_maximum_fusion.1), channel_id=1, source_target_pairs={{0,24},{4,28},{8,16},{12,20},{16,8},{20,12},{24,0},{28,4},{1,25},{... | collective-permute-start | bytes 172040 | tf_op jit(solution)/shard_map/ppermute | solution.py:273
  13.4 5.3 %collective-permute-start.8 = (f32[2,56,128]{2,1,0:T(8,128)S(1)}, f32[2,56,128]{2,1,0:T(8,128)S(1)}, u32[]{:S(2)}, u32[]{:S(2)}) collective-permute-start(f32[2,56,128]{2,1,0:T(8,128)S(1)} %pad_maximum_fusion.1), channel_id=1, source_target_pairs={{0,16},{4,20},{8,24},{12,28},{16,0},{20,4},{24,8},{28,12},{1,17},{... | collective-permute-start | bytes 172040 | tf_op jit(solution)/shard_map/ppermute | solution.py:273
  13.4 5.4 %collective-permute-start.9 = (f32[2,56,128]{2,1,0:T(8,128)S(1)}, f32[2,56,128]{2,1,0:T(8,128)S(1)}, u32[]{:S(2)}, u32[]{:S(2)}) collective-permute-start(f32[2,56,128]{2,1,0:T(8,128)S(1)} %pad_maximum_fusion.1), channel_id=1, source_target_pairs={{0,8},{4,12},{8,0},{12,4},{16,24},{20,28},{24,16},{28,20},{1,9},{5... | collective-permute-start | bytes 172040 | tf_op jit(solution)/shard_map/ppermute | solution.py:273
  15.2 22.4 %copy-start.2 = (f32[4,128,128]{2,1,0:T(8,128)S(1)}, f32[4,128,128]{2,1,0:T(8,128)}, u32[]{:S(2)}) copy-start(f32[4,128,128]{2,1,0:T(8,128)} %param.13) | copy-start | bytes 786436
  18.8 18.8 %all-to-all-start = ((f32[32,30,128]{2,1,0:T(8,128)}), f32[32,30,128]{2,1,0:T(8,128)S(1)}, u32[]{:S(2)}, u32[]{:S(2)}) async-start(f32[32,30,128]{2,1,0:T(8,128)} %shard_map.74), calls=%async_computation | async-start | bytes 1048576 | tf_op jit(solution)/shard_map/all_to_all | solution.py:318
  21.6 3.4 %collective-permute-start = (f32[896,128]{1,0:T(8,128)S(1)}, f32[896,128]{1,0:T(8,128)S(1)}, u32[]{:S(2)}, u32[]{:S(2)}) collective-permute-start(f32[896,128]{1,0:T(8,128)S(1)} %bitcast.31), channel_id=1, source_target_pairs={{0,1},{1,0},{2,3},{3,2},{4,5},{5,4},{6,7},{7,6},{8,9},{9,8},{10,11... | collective-permute-start | bytes 1376264 | tf_op jit(solution)/shard_map/ppermute | solution.py:273
  22.8 2.2 %collective-permute-start.2 = (f32[896,128]{1,0:T(8,128)S(1)}, f32[896,128]{1,0:T(8,128)S(1)}, u32[]{:S(2)}, u32[]{:S(2)}) collective-permute-start(f32[896,128]{1,0:T(8,128)S(1)} %collective-permute-done.1.refs_2_), channel_id=1, source_target_pairs={{0,1},{1,0},{2,3},{3,2},{4,5},{5,4},{6,7},{7,6},{8,9},{9,8},{10,11... | collective-permute-start | bytes 1376264 | tf_op jit(solution)/shard_map/ppermute | solution.py:273
  22.8 2.1 %collective-permute-start.10 = (f32[8,56,128]{2,1,0:T(8,128)S(1)}, f32[8,56,128]{2,1,0:T(8,128)S(1)}, u32[]{:S(2)}, u32[]{:S(2)}) collective-permute-start(f32[8,56,128]{2,1,0:T(8,128)S(1)} %constant_dynamic-update-slice_fusion), channel_id=1, source_target_pairs={{0,1},{1,0},{2,3},{3,2},{4,5},{5,4},{6,7},{7,6},{8,9},{9,8},{10,11... | collective-permute-start | bytes 688136 | tf_op jit(solution)/shard_map/ppermute | solution.py:273
  26.4 7.2 %collective-permute-start.11 = (f32[112,128]{1,0:T(8,128)S(1)}, f32[112,128]{1,0:T(8,128)S(1)}, u32[]{:S(2)}, u32[]{:S(2)}) collective-permute-start(f32[112,128]{1,0:T(8,128)S(1)} %get-tuple-element.40), channel_id=1, source_target_pairs={{0,4},{4,0},{8,12},{12,8},{16,20},{20,16},{24,28},{28,24},{1,5},{5... | collective-permute-start | bytes 172040 | tf_op jit(solution)/shard_map/ppermute | solution.py:273
  27.7 9.2 %collective-permute-start.12 = (f32[112,128]{1,0:T(8,128)S(1)}, f32[112,128]{1,0:T(8,128)S(1)}, u32[]{:S(2)}, u32[]{:S(2)}) collective-permute-start(f32[112,128]{1,0:T(8,128)S(1)} %get-tuple-element.41), channel_id=1, source_target_pairs={{0,8},{4,12},{8,0},{12,4},{16,24},{20,28},{24,16},{28,20},{1,9},{5... | collective-permute-start | bytes 172040 | tf_op jit(solution)/shard_map/ppermute | solution.py:273
  29.2 13.4 %collective-permute-start.13 = (f32[112,128]{1,0:T(8,128)S(1)}, f32[112,128]{1,0:T(8,128)S(1)}, u32[]{:S(2)}, u32[]{:S(2)}) collective-permute-start(f32[112,128]{1,0:T(8,128)S(1)} %get-tuple-element.42), channel_id=1, source_target_pairs={{0,12},{4,8},{8,4},{12,0},{16,28},{20,24},{24,20},{28,16},{1,13},{... | collective-permute-start | bytes 172040 | tf_op jit(solution)/shard_map/ppermute | solution.py:273
  29.9 12.6 %collective-permute-start.14 = (f32[112,128]{1,0:T(8,128)S(1)}, f32[112,128]{1,0:T(8,128)S(1)}, u32[]{:S(2)}, u32[]{:S(2)}) collective-permute-start(f32[112,128]{1,0:T(8,128)S(1)} %get-tuple-element.43), channel_id=1, source_target_pairs={{0,16},{4,20},{8,24},{12,28},{16,0},{20,4},{24,8},{28,12},{1,17},{... | collective-permute-start | bytes 172040 | tf_op jit(solution)/shard_map/ppermute | solution.py:273
  32.5 12.8 %collective-permute-start.15 = (f32[112,128]{1,0:T(8,128)S(1)}, f32[112,128]{1,0:T(8,128)S(1)}, u32[]{:S(2)}, u32[]{:S(2)}) collective-permute-start(f32[112,128]{1,0:T(8,128)S(1)} %get-tuple-element.44), channel_id=1, source_target_pairs={{0,20},{4,16},{8,28},{12,24},{16,4},{20,0},{24,12},{28,8},{1,21},{... | collective-permute-start | bytes 172040 | tf_op jit(solution)/shard_map/ppermute | solution.py:273
  33.6 11.8 %collective-permute-start.16 = (f32[112,128]{1,0:T(8,128)S(1)}, f32[112,128]{1,0:T(8,128)S(1)}, u32[]{:S(2)}, u32[]{:S(2)}) collective-permute-start(f32[112,128]{1,0:T(8,128)S(1)} %get-tuple-element.45), channel_id=1, source_target_pairs={{0,24},{4,28},{8,16},{12,20},{16,8},{20,12},{24,0},{28,4},{1,25},{... | collective-permute-start | bytes 172040 | tf_op jit(solution)/shard_map/ppermute | solution.py:273
  36.9 8.4 %collective-permute-start.17 = (f32[112,128]{1,0:T(8,128)S(1)}, f32[112,128]{1,0:T(8,128)S(1)}, u32[]{:S(2)}, u32[]{:S(2)}) collective-permute-start(f32[112,128]{1,0:T(8,128)S(1)} %get-tuple-element.46), channel_id=1, source_target_pairs={{0,28},{4,24},{8,20},{12,16},{16,12},{20,8},{24,4},{28,0},{1,29},{... | collective-permute-start | bytes 172040 | tf_op jit(solution)/shard_map/ppermute | solution.py:273
  52.3 19.9 %all-to-all-start.1 = ((f32[32,28,128]{2,1,0:T(8,128)}), f32[32,28,128]{2,1,0:T(8,128)S(1)}, u32[]{:S(2)}, u32[]{:S(2)}) async-start(f32[32,28,128]{2,1,0:T(8,128)} %shard_map.77), calls=%async_computation.1 | async-start | bytes 1048576 | tf_op jit(solution)/shard_map/all_to_all | solution.py:372
  72.8 2.0 %collective-permute-start.18 = (f32[224,128]{1,0:T(8,128)S(1)}, f32[224,128]{1,0:T(8,128)S(1)}, u32[]{:S(2)}, u32[]{:S(2)}) collective-permute-start(f32[224,128]{1,0:T(8,128)S(1)} %get-tuple-element.51), channel_id=1, source_target_pairs={{0,1},{1,0},{2,3},{3,2},{4,5},{5,4},{6,7},{7,6},{8,9},{9,8},{10,11... | collective-permute-start | bytes 344072 | tf_op jit(solution)/shard_map/ppermute | solution.py:273
  72.9 6.0 %collective-permute-start.19 = (f32[224,128]{1,0:T(8,128)S(1)}, f32[224,128]{1,0:T(8,128)S(1)}, u32[]{:S(2)}, u32[]{:S(2)}) collective-permute-start(f32[224,128]{1,0:T(8,128)S(1)} %get-tuple-element.50), channel_id=1, source_target_pairs={{0,2},{1,3},{2,0},{3,1},{4,6},{5,7},{6,4},{7,5},{8,10},{9,11},{10,... | collective-permute-start | bytes 344072 | tf_op jit(solution)/shard_map/ppermute | solution.py:273
  74.2 6.3 %collective-permute-start.20 = (f32[224,128]{1,0:T(8,128)S(1)}, f32[224,128]{1,0:T(8,128)S(1)}, u32[]{:S(2)}, u32[]{:S(2)}) collective-permute-start(f32[224,128]{1,0:T(8,128)S(1)} %get-tuple-element.49), channel_id=1, source_target_pairs={{0,3},{1,2},{2,1},{3,0},{4,7},{5,6},{6,5},{7,4},{8,11},{9,10},{10,... | collective-permute-start | bytes 344072 | tf_op jit(solution)/shard_map/ppermute | solution.py:273
  80.5 0.8 copy-start.4

commit v5 on v4

--- a/solution.py
+++ b/solution.py
@@ -188,9 +188,9 @@
     in_turn(tiles, 2, first, then)
 
 
-def contact_kernel(order, places_ref, stiffness_ref, info_ref, *refs):
+def contact_kernel(order, turns, places_ref, stiffness_ref, info_ref, *refs):
     swaps = len(order)
-    piece_refs, refs = refs[:swaps], refs[swaps:]
+    pieces, refs = dict(zip(turns, refs[:swaps])), refs[swaps:]
     out_ref, move_ref, stiff_ref, maps_ref, turned_maps_ref, mapped_ref, back_ref, tangent_ref, rows_ref = refs
     total, faces = tangent_ref.shape
     partner_count = info_ref.shape[0] - 2
@@ -199,7 +199,7 @@
     rows = total // 2
     for at, d in enumerate(order):
         start = pl.multiple_of((places_ref[0] ^ d) * blocks, ROWS)
-        move_ref[pl.ds(start, blocks), :] = piece_refs[d][...]
+        move_ref[pl.ds(start, blocks), :] = pieces[d][...]
         for side in range(2):
             first = pl.multiple_of(start + (places_ref[1] % 2 ^ side) * half, ROWS)
             stiff_ref[pl.ds(first, half), :] = stiffness_ref[side, at]
@@ -344,8 +344,10 @@
         compiler_params=params,
     )(packed, mortar.reshape(partner_count * faces, faces))
 
+    turns = list(range(vol_count))
+    turns.insert(vol_count // 2 + 1, turns.pop(vol_count // 2 - 1))
     summed = pl.pallas_call(
-        functools.partial(contact_kernel, tuple(order)),
+        functools.partial(contact_kernel, tuple(order), tuple(turns)),
         out_shape=array(devices, slab, faces),
         in_specs=[smem] + [vmem] * (2 + vol_count),
         out_specs=vmem,
@@ -360,7 +362,7 @@
             scratch(ROWS, total),
         ],
         compiler_params=params,
-    )(places, stiffness, info, *moved)
+    )(places, stiffness, info, *[moved[d] for d in turns])
     summed, after = lax.optimization_barrier((summed, places))
     back_mix = pl.pallas_call(
         functools.partial(back_mixer_kernel, rep_count, share),

time: 81.7 us -> 81.2 us (level)
    ppermute x21, waiting for transfers between devices: 12.6 us -> 10.4 us  [swap(): return lax.ppermute(value, axis, [(i, i ^ d) for i in range(count)])]
    all_to_all x1, waiting for transfers between devices: 0.01 us -> 2.24 us  [spread_local(): packed = lax.all_to_all(sent, ('vol', 'rep'), 0, 0, tiled=True)]
  transfers between devices with their start and end apart: 23 -> 23, of which waited for: 8 -> 9; matrix products, arithmetic and copies ran while one was open for 3% -> 3% of each run, Pallas kernels for 12% -> 12%
where the time goes in v5:
time: 81.2 us; the launch traced here: 80.7 us
  starting transfers between devices  31.3 us (39%)
  waiting for transfers between devices  27.2 us (33%)
  Pallas kernels  17.6 us (22%)
  local copies, waits for them, and re-layouts  2.82 us (3%)
  other arithmetic  1.54 us (2%)
    ppermute x21, starting transfers between devices, swap(): return lax.ppermute(value, axis, [(i, i ^ d) for i in range(count)])  24.8 us
    all_to_all x1, waiting for transfers between devices, spread_local(): returned = lax.all_to_all(summed, ('vol', 'rep'), 0, 0, tiled=True)  14.5 us
    ppermute x21, waiting for transfers between devices, swap(): return lax.ppermute(value, axis, [(i, i ^ d) for i in range(count)])  10.4 us
    pallas_call x1, Pallas kernels, spread_local(): pl.pallas_call(functools.partial(contact_kernel, tuple(order), tuple(turn...  7 us
    pallas_call x1, Pallas kernels, spread_local(): pl.pallas_call(functools.partial(slope_kernel, rep_count, slab), out_shap...  4.93 us
    all_to_all x1, starting transfers between devices, spread_local(): returned = lax.all_to_all(summed, ('vol', 'rep'), 0, 0, tiled=True)  3.8 us
    all_to_all x1, starting transfers between devices, spread_local(): packed = lax.all_to_all(sent, ('vol', 'rep'), 0, 0, tiled=True)  2.72 us
    all_to_all x1, waiting for transfers between devices, spread_local(): packed = lax.all_to_all(sent, ('vol', 'rep'), 0, 0, tiled=True)  2.24 us
  transfers between devices with their start and end apart: 23, of which 9 were waited for; matrix products, arithmetic and copies ran while one was open for 3% of the time, Pallas kernels for 12%

profile of v5, /device:TPU:0, one launch (start us, length us, event | category | flops | bytes accessed | tf_op | source)
XLA Modules:
  0.0 80.7 jit_solution(16802703795537959948)
XLA Ops:
  0.0 0.8 %copy-done = f32[112,128]{1,0:T(8,128)S(1)} copy-done((f32[112,128]{1,0:T(8,128)S(1)}, f32[112,128]{1,0:T(8,128)}, u32[]{:S(2)}) %copy-start) | copy-done | bytes 57368
  0.8 3.0 %collective-permute-start.3 = (f32[56,128]{1,0:T(8,128)S(1)}, f32[56,128]{1,0:T(8,128)S(1)}, u32[]{:S(2)}, u32[]{:S(2)}) collective-permute-start(f32[56,128]{1,0:T(8,128)S(1)} %constant_dynamic-slice_fusion), channel_id=1, source_target_pairs={{0,4},{4,0},{8,12},{12,8},{16,20},{20,16},{24,28},{28,24},{1,5},{5... | collective-permute-start | bytes 86024 | tf_op jit(solution)/shard_map/ppermute | solution.py:273
  3.8 1.1 %dynamic-slice_bitcast_fusion = (f32[224,128]{1,0:T(8,128)S(1)}, f32[224,128]{1,0:T(8,128)S(1)}, f32[224,128]{1,0:T(8,128)S(1)}, f32[224,128]{1,0:T(8,128)S(1)}) fusion(f32[112,8,128]{2,1,0:T(8,128)} %param.7, s32[]{:T(128)S(6)} %select_n.39, s32[]{:T(128)S(6)} %select_n.37, s32[]{:T(128)S(6)} %select_n.36, s32[]{:T(128)S(6)} %select_n.38), kind=kLoop, calls=%fused_computation.6 | loop fusion | bytes 917520 | tf_op jit(solution)/shard_map/reshape | solution.py:279
  5.0 1.6 %collective-permute-start.5 = (f32[224,128]{1,0:T(8,128)S(1)}, f32[224,128]{1,0:T(8,128)S(1)}, u32[]{:S(2)}, u32[]{:S(2)}) collective-permute-start(f32[224,128]{1,0:T(8,128)S(1)} %get-tuple-element.55), channel_id=1, source_target_pairs={{0,2},{1,3},{2,0},{3,1},{4,6},{5,7},{6,4},{7,5},{8,10},{9,11},{10,... | collective-permute-start | bytes 344072 | tf_op jit(solution)/shard_map/ppermute | solution.py:273
  6.8 1.5 %collective-permute-start.1 = (f32[896,128]{1,0:T(8,128)}, f32[896,128]{1,0:T(8,128)S(1)}, u32[]{:S(2)}, u32[]{:S(2)}) collective-permute-start(f32[896,128]{1,0:T(8,128)} %bitcast.30), channel_id=1, source_target_pairs={{0,2},{1,3},{2,0},{3,1},{4,6},{5,7},{6,4},{7,5},{8,10},{9,11},{10,... | collective-permute-start | bytes 1376264 | tf_op jit(solution)/shard_map/ppermute | solution.py:273
  8.3 0.7 add_convert_fusion
  9.0 0.7 select_maximum_fusion.table_ref
  9.8 3.7 %collective-permute-start.7 = (f32[2,56,128]{2,1,0:T(8,128)S(1)}, f32[2,56,128]{2,1,0:T(8,128)S(1)}, u32[]{:S(2)}, u32[]{:S(2)}) collective-permute-start(f32[2,56,128]{2,1,0:T(8,128)S(1)} %pad_maximum_fusion.1), channel_id=1, source_target_pairs={{0,24},{4,28},{8,16},{12,20},{16,8},{20,12},{24,0},{28,4},{1,25},{... | collective-permute-start | bytes 172040 | tf_op jit(solution)/shard_map/ppermute | solution.py:273
  13.4 0.8 collective-permute-start.9
  14.3 0.9 %shard_map.73.mix_ref = bf16[2,256,256]{2,1,0:T(8,128)(2,1)S(1)} custom-call(s32[2]{0:T(128)S(1)} %pad_add_fusion.places_ref.after_ref, f32[40,128]{1,0:T(8,128)S(1)} %select_maximum_fusion.table_ref), custom_call_target="tpu_custom_call" | custom-call | tf_op jit(solution)/shard_map/pallas_call | solution.py:302
  15.2 1.9 %shard_map.74 = f32[32,30,128]{2,1,0:T(8,128)} custom-call(s32[2]{0:T(128)S(1)} %pad_add_fusion.places_ref.after_ref, bf16[2,256,256]{2,1,0:T(8,128)(2,1)S(1)} %shard_map.73.mix_ref, f32[40,128]{1,0:T(8,128)S(1)} %select_maximum_fusion.table_ref, f32[224,128]{1,0:T(8,128)S(1)} %get-tuple-element.27.refs_0_, f32[224,128]{1,0:T(8,128)S(1)} %collective-permute-done.4.refs_1_, ...), custom_call_target="tpu_custom_call" | custom-call | tf_op jit(solution)/shard_map/pallas_call | solution.py:310
  17.1 1.6 %collective-permute-done.8 = f32[2,56,128]{2,1,0:T(8,128)S(1)} collective-permute-done((f32[2,56,128]{2,1,0:T(8,128)S(1)}, f32[2,56,128]{2,1,0:T(8,128)S(1)}, u32[]{:S(2)}, u32[]{:S(2)}) %collective-permute-start.8) | collective-permute-done | bytes 57376 | tf_op jit(solution)/shard_map/ppermute | solution.py:273
  18.8 2.7 %all-to-all-start = ((f32[32,30,128]{2,1,0:T(8,128)}), f32[32,30,128]{2,1,0:T(8,128)S(1)}, u32[]{:S(2)}, u32[]{:S(2)}) async-start(f32[32,30,128]{2,1,0:T(8,128)} %shard_map.74), calls=%async_computation | async-start | bytes 1048576 | tf_op jit(solution)/shard_map/all_to_all | solution.py:318
  21.9 0.9 %collective-permute-done.1.refs_2_ = f32[896,128]{1,0:T(8,128)S(1)} collective-permute-done((f32[896,128]{1,0:T(8,128)}, f32[896,128]{1,0:T(8,128)S(1)}, u32[]{:S(2)}, u32[]{:S(2)}) %collective-permute-start.1) | collective-permute-done | bytes 458784 | tf_op jit(solution)/shard_map/ppermute | solution.py:273
  23.3 1.6 %collective-permute-done.10 = f32[8,56,128]{2,1,0:T(8,128)S(1)} collective-permute-done((f32[8,56,128]{2,1,0:T(8,128)S(1)}, f32[8,56,128]{2,1,0:T(8,128)S(1)}, u32[]{:S(2)}, u32[]{:S(2)}) %collective-permute-start.10) | collective-permute-done | bytes 229408 | tf_op jit(solution)/shard_map/ppermute | solution.py:273
  25.0 1.4 %shard_map.76 = (f32[112,128]{1,0:T(8,128)S(1)}, f32[112,128]{1,0:T(8,128)S(1)}, f32[112,128]{1,0:T(8,128)S(1)}, f32[112,128]{1,0:T(8,128)S(1)}, f32[112,128]{1,...) custom-call(s32[2]{0:T(128)S(1)} %pad_add_fusion.places_ref.after_ref, ...), custom_call_target="tpu_custom_call" | custom-call | tf_op jit(solution)/shard_map/pallas_call | solution.py:323
  26.4 1.3 %collective-permute-start.11 = (f32[112,128]{1,0:T(8,128)S(1)}, f32[112,128]{1,0:T(8,128)S(1)}, u32[]{:S(2)}, u32[]{:S(2)}) collective-permute-start(f32[112,128]{1,0:T(8,128)S(1)} %get-tuple-element.40), channel_id=1, source_target_pairs={{0,4},{4,0},{8,12},{12,8},{16,20},{20,16},{24,28},{28,24},{1,5},{5... | collective-permute-start | bytes 172040 | tf_op jit(solution)/shard_map/ppermute | solution.py:273
  27.7 1.5 %collective-permute-start.12 = (f32[112,128]{1,0:T(8,128)S(1)}, f32[112,128]{1,0:T(8,128)S(1)}, u32[]{:S(2)}, u32[]{:S(2)}) collective-permute-start(f32[112,128]{1,0:T(8,128)S(1)} %get-tuple-element.41), channel_id=1, source_target_pairs={{0,8},{4,12},{8,0},{12,4},{16,24},{20,28},{24,16},{28,20},{1,9},{5... | collective-permute-start | bytes 172040 | tf_op jit(solution)/shard_map/ppermute | solution.py:273
  29.2 2.4 %collective-permute-start.13 = (f32[112,128]{1,0:T(8,128)S(1)}, f32[112,128]{1,0:T(8,128)S(1)}, u32[]{:S(2)}, u32[]{:S(2)}) collective-permute-start(f32[112,128]{1,0:T(8,128)S(1)} %get-tuple-element.42), channel_id=1, source_target_pairs={{0,16},{4,20},{8,24},{12,28},{16,0},{20,4},{24,8},{28,12},{1,17},{... | collective-permute-start | bytes 172040 | tf_op jit(solution)/shard_map/ppermute | solution.py:273
  31.6 0.8 %collective-permute-start.14 = (f32[112,128]{1,0:T(8,128)S(1)}, f32[112,128]{1,0:T(8,128)S(1)}, u32[]{:S(2)}, u32[]{:S(2)}) collective-permute-start(f32[112,128]{1,0:T(8,128)S(1)} %get-tuple-element.43), channel_id=1, source_target_pairs={{0,20},{4,16},{8,28},{12,24},{16,4},{20,0},{24,12},{28,8},{1,21},{... | collective-permute-start | bytes 172040 | tf_op jit(solution)/shard_map/ppermute | solution.py:273
  32.4 1.1 %collective-permute-start.15 = (f32[112,128]{1,0:T(8,128)S(1)}, f32[112,128]{1,0:T(8,128)S(1)}, u32[]{:S(2)}, u32[]{:S(2)}) collective-permute-start(f32[112,128]{1,0:T(8,128)S(1)} %get-tuple-element.44), channel_id=1, source_target_pairs={{0,12},{4,8},{8,4},{12,0},{16,28},{20,24},{24,20},{28,16},{1,13},{... | collective-permute-start | bytes 172040 | tf_op jit(solution)/shard_map/ppermute | solution.py:273
  33.6 3.3 %collective-permute-start.16 = (f32[112,128]{1,0:T(8,128)S(1)}, f32[112,128]{1,0:T(8,128)S(1)}, u32[]{:S(2)}, u32[]{:S(2)}) collective-permute-start(f32[112,128]{1,0:T(8,128)S(1)} %get-tuple-element.45), channel_id=1, source_target_pairs={{0,24},{4,28},{8,16},{12,20},{16,8},{20,12},{24,0},{28,4},{1,25},{... | collective-permute-start | bytes 172040 | tf_op jit(solution)/shard_map/ppermute | solution.py:273
  37.6 2.2 %all-to-all-done.packed_ref = f32[32,30,128]{2,1,0:T(8,128)S(1)} async-done(((f32[32,30,128]{2,1,0:T(8,128)}), f32[32,30,128]{2,1,0:T(8,128)S(1)}, u32[]{:S(2)}, u32[]{:S(2)}) %all-to-all-start) | async-done | bytes 491552 | tf_op jit(solution)/shard_map/all_to_all | solution.py:318
  39.8 4.9 %shard_map.75.info_ref = f32[6,896,128]{2,1,0:T(8,128)S(1)} custom-call(f32[32,30,128]{2,1,0:T(8,128)S(1)} %all-to-all-done.packed_ref, f32[512,128]{1,0:T(8,128)S(1)} %bitcast.33), custom_call_target="tpu_custom_call" | custom-call | tf_op jit(solution)/shard_map/pallas_call | solution.py:332
  45.3 7.0 %shard_map.77 = f32[32,28,128]{2,1,0:T(8,128)} custom-call(s32[2]{0:T(128)S(1)} %pad_add_fusion.places_ref.after_ref, f32[2,8,56,128]{3,2,1,0:T(8,128)S(1)} %pad_maximum_fusion.stiffness_ref, f32[6,896,128]{2,1,0:T(8,128)S(1)} %shard_map.75.info_ref, f32[112,128]{1,0:T(8,128)S(1)} %get-tuple-element.39.refs_0_, ...), custom_call_target="tpu_custom_call" | custom-call | tf_op jit(solution)/shard_map/pallas_call | solution.py:349
  52.3 3.8 %all-to-all-start.1 = ((f32[32,28,128]{2,1,0:T(8,128)}), f32[32,28,128]{2,1,0:T(8,128)S(1)}, u32[]{:S(2)}, u32[]{:S(2)}) async-start(f32[32,28,128]{2,1,0:T(8,128)} %shard_map.77), calls=%async_computation.1 | async-start | bytes 1048576 | tf_op jit(solution)/shard_map/all_to_all | solution.py:374
  56.2 1.0 %shard_map.78.mix_ref = bf16[2,256,256]{2,1,0:T(8,128)(2,1)S(1)} custom-call(s32[2]{0:T(128)S(1)} %pad_add_fusion.places_ref.after_ref, f32[32,32]{1,0:T(8,128)S(1)} %copy-done.3, s32[2]{0:T(128)S(1)} %pad_add_fusion.places_ref.after_ref), custom_call_target="tpu_custom_call" | custom-call | tf_op jit(solution)/shard_map/pallas_call | solution.py:367
  57.1 14.5 %all-to-all-done.1.summed_ref = f32[32,28,128]{2,1,0:T(8,128)S(1)} async-done(((f32[32,28,128]{2,1,0:T(8,128)}), f32[32,28,128]{2,1,0:T(8,128)S(1)}, u32[]{:S(2)}, u32[]{:S(2)}) %all-to-all-start.1) | async-done | bytes 458784 | tf_op jit(solution)/shard_map/all_to_all | solution.py:374
  72.4 1.3 %collective-permute-start.19 = (f32[224,128]{1,0:T(8,128)S(1)}, f32[224,128]{1,0:T(8,128)S(1)}, u32[]{:S(2)}, u32[]{:S(2)}) collective-permute-start(f32[224,128]{1,0:T(8,128)S(1)} %get-tuple-element.50), channel_id=1, source_target_pairs={{0,2},{1,3},{2,0},{3,1},{4,6},{5,7},{6,4},{7,5},{8,10},{9,11},{10,... | collective-permute-start | bytes 344072 | tf_op jit(solution)/shard_map/ppermute | solution.py:273
  74.3 4.1 %collective-permute-done.19 = f32[224,128]{1,0:T(8,128)S(1)} collective-permute-done((f32[224,128]{1,0:T(8,128)S(1)}, f32[224,128]{1,0:T(8,128)S(1)}, u32[]{:S(2)}, u32[]{:S(2)}) %collective-permute-start.19) | collective-permute-done | bytes 114720 | tf_op jit(solution)/shard_map/ppermute | solution.py:273
  78.4 1.5 %collective-permute-done.20 = f32[224,128]{1,0:T(8,128)S(1)} collective-permute-done((f32[224,128]{1,0:T(8,128)S(1)}, f32[224,128]{1,0:T(8,128)S(1)}, u32[]{:S(2)}, u32[]{:S(2)}) %collective-permute-start.20) | collective-permute-done | bytes 114720 | tf_op jit(solution)/shard_map/ppermute | solution.py:273
  80.0 0.8 copy-done.4
  (49 shorter events, 4.0 us)
Async XLA Ops:
  0.0 0.8 %copy-start = (f32[112,128]{1,0:T(8,128)S(1)}, f32[112,128]{1,0:T(8,128)}, u32[]{:S(2)}) copy-start(f32[112,128]{1,0:T(8,128)} %param.9) | copy-start | bytes 172036
  0.0 21.6 %copy-start.1 = (f32[112,8,128]{2,1,0:T(8,128)S(1)}, f32[112,8,128]{2,1,0:T(8,128)}, u32[]{:S(2)}) copy-start(f32[112,8,128]{2,1,0:T(8,128)} %param.8) | copy-start | bytes 1376260
  0.0 25.0 %copy-start.3 = (f32[32,32]{1,0:T(8,128)S(1)}, f32[32,32]{1,0:T(8,128)}, u32[]{:S(2)}) copy-start(f32[32,32]{1,0:T(8,128)} %projection_ref.3) | copy-start | bytes 12292
  0.8 8.9 %collective-permute-start.3 = (f32[56,128]{1,0:T(8,128)S(1)}, f32[56,128]{1,0:T(8,128)S(1)}, u32[]{:S(2)}, u32[]{:S(2)}) collective-permute-start(f32[56,128]{1,0:T(8,128)S(1)} %constant_dynamic-slice_fusion), channel_id=1, source_target_pairs={{0,4},{4,0},{8,12},{12,8},{16,20},{20,16},{24,28},{28,24},{1,5},{5... | collective-permute-start | bytes 86024 | tf_op jit(solution)/shard_map/ppermute | solution.py:273
  4.9 8.5 %collective-permute-start.4 = (f32[224,128]{1,0:T(8,128)S(1)}, f32[224,128]{1,0:T(8,128)S(1)}, u32[]{:S(2)}, u32[]{:S(2)}) collective-permute-start(f32[224,128]{1,0:T(8,128)S(1)} %get-tuple-element.53), channel_id=1, source_target_pairs={{0,1},{1,0},{2,3},{3,2},{4,5},{5,4},{6,7},{7,6},{8,9},{9,8},{10,11... | collective-permute-start | bytes 344072 | tf_op jit(solution)/shard_map/ppermute | solution.py:273
  5.0 8.5 %collective-permute-start.5 = (f32[224,128]{1,0:T(8,128)S(1)}, f32[224,128]{1,0:T(8,128)S(1)}, u32[]{:S(2)}, u32[]{:S(2)}) collective-permute-start(f32[224,128]{1,0:T(8,128)S(1)} %get-tuple-element.55), channel_id=1, source_target_pairs={{0,2},{1,3},{2,0},{3,1},{4,6},{5,7},{6,4},{7,5},{8,10},{9,11},{10,... | collective-permute-start | bytes 344072 | tf_op jit(solution)/shard_map/ppermute | solution.py:273
  6.5 8.7 %collective-permute-start.6 = (f32[224,128]{1,0:T(8,128)S(1)}, f32[224,128]{1,0:T(8,128)S(1)}, u32[]{:S(2)}, u32[]{:S(2)}) collective-permute-start(f32[224,128]{1,0:T(8,128)S(1)} %get-tuple-element.52), channel_id=1, source_target_pairs={{0,3},{1,2},{2,1},{3,0},{4,7},{5,6},{6,5},{7,4},{8,11},{9,10},{10,... | collective-permute-start | bytes 344072 | tf_op jit(solution)/shard_map/ppermute | solution.py:273
  6.8 16.0 %collective-permute-start.1 = (f32[896,128]{1,0:T(8,128)}, f32[896,128]{1,0:T(8,128)S(1)}, u32[]{:S(2)}, u32[]{:S(2)}) collective-permute-start(f32[896,128]{1,0:T(8,128)} %bitcast.30), channel_id=1, source_target_pairs={{0,2},{1,3},{2,0},{3,1},{4,6},{5,7},{6,4},{7,5},{8,10},{9,11},{10,... | collective-permute-start | bytes 1376264 | tf_op jit(solution)/shard_map/ppermute | solution.py:273
  9.8 7.4 %collective-permute-start.7 = (f32[2,56,128]{2,1,0:T(8,128)S(1)}, f32[2,56,128]{2,1,0:T(8,128)S(1)}, u32[]{:S(2)}, u32[]{:S(2)}) collective-permute-start(f32[2,56,128]{2,1,0:T(8,128)S(1)} %pad_maximum_fusion.1), channel_id=1, source_target_pairs={{0,24},{4,28},{8,16},{12,20},{16,8},{20,12},{24,0},{28,4},{1,25},{... | collective-permute-start | bytes 172040 | tf_op jit(solution)/shard_map/ppermute | solution.py:273
  13.4 5.3 %collective-permute-start.8 = (f32[2,56,128]{2,1,0:T(8,128)S(1)}, f32[2,56,128]{2,1,0:T(8,128)S(1)}, u32[]{:S(2)}, u32[]{:S(2)}) collective-permute-start(f32[2,56,128]{2,1,0:T(8,128)S(1)} %pad_maximum_fusion.1), channel_id=1, source_target_pairs={{0,16},{4,20},{8,24},{12,28},{16,0},{20,4},{24,8},{28,12},{1,17},{... | collective-permute-start | bytes 172040 | tf_op jit(solution)/shard_map/ppermute | solution.py:273
  13.4 5.4 %collective-permute-start.9 = (f32[2,56,128]{2,1,0:T(8,128)S(1)}, f32[2,56,128]{2,1,0:T(8,128)S(1)}, u32[]{:S(2)}, u32[]{:S(2)}) collective-permute-start(f32[2,56,128]{2,1,0:T(8,128)S(1)} %pad_maximum_fusion.1), channel_id=1, source_target_pairs={{0,8},{4,12},{8,0},{12,4},{16,24},{20,28},{24,16},{28,20},{1,9},{5... | collective-permute-start | bytes 172040 | tf_op jit(solution)/shard_map/ppermute | solution.py:273
  15.2 24.7 %copy-start.2 = (f32[4,128,128]{2,1,0:T(8,128)S(1)}, f32[4,128,128]{2,1,0:T(8,128)}, u32[]{:S(2)}) copy-start(f32[4,128,128]{2,1,0:T(8,128)} %param.13) | copy-start | bytes 786436
  18.8 21.0 %all-to-all-start = ((f32[32,30,128]{2,1,0:T(8,128)}), f32[32,30,128]{2,1,0:T(8,128)S(1)}, u32[]{:S(2)}, u32[]{:S(2)}) async-start(f32[32,30,128]{2,1,0:T(8,128)} %shard_map.74), calls=%async_computation | async-start | bytes 1048576 | tf_op jit(solution)/shard_map/all_to_all | solution.py:318
  21.6 3.4 %collective-permute-start = (f32[896,128]{1,0:T(8,128)S(1)}, f32[896,128]{1,0:T(8,128)S(1)}, u32[]{:S(2)}, u32[]{:S(2)}) collective-permute-start(f32[896,128]{1,0:T(8,128)S(1)} %bitcast.31), channel_id=1, source_target_pairs={{0,1},{1,0},{2,3},{3,2},{4,5},{5,4},{6,7},{7,6},{8,9},{9,8},{10,11... | collective-permute-start | bytes 1376264 | tf_op jit(solution)/shard_map/ppermute | solution.py:273
  22.8 2.2 %collective-permute-start.2 = (f32[896,128]{1,0:T(8,128)S(1)}, f32[896,128]{1,0:T(8,128)S(1)}, u32[]{:S(2)}, u32[]{:S(2)}) collective-permute-start(f32[896,128]{1,0:T(8,128)S(1)} %collective-permute-done.1.refs_2_), channel_id=1, source_target_pairs={{0,1},{1,0},{2,3},{3,2},{4,5},{5,4},{6,7},{7,6},{8,9},{9,8},{10,11... | collective-permute-start | bytes 1376264 | tf_op jit(solution)/shard_map/ppermute | solution.py:273
  22.8 2.1 %collective-permute-start.10 = (f32[8,56,128]{2,1,0:T(8,128)S(1)}, f32[8,56,128]{2,1,0:T(8,128)S(1)}, u32[]{:S(2)}, u32[]{:S(2)}) collective-permute-start(f32[8,56,128]{2,1,0:T(8,128)S(1)} %constant_dynamic-update-slice_fusion), channel_id=1, source_target_pairs={{0,1},{1,0},{2,3},{3,2},{4,5},{5,4},{6,7},{7,6},{8,9},{9,8},{10,11... | collective-permute-start | bytes 688136 | tf_op jit(solution)/shard_map/ppermute | solution.py:273
  26.4 7.2 %collective-permute-start.11 = (f32[112,128]{1,0:T(8,128)S(1)}, f32[112,128]{1,0:T(8,128)S(1)}, u32[]{:S(2)}, u32[]{:S(2)}) collective-permute-start(f32[112,128]{1,0:T(8,128)S(1)} %get-tuple-element.40), channel_id=1, source_target_pairs={{0,4},{4,0},{8,12},{12,8},{16,20},{20,16},{24,28},{28,24},{1,5},{5... | collective-permute-start | bytes 172040 | tf_op jit(solution)/shard_map/ppermute | solution.py:273
  27.7 9.2 %collective-permute-start.12 = (f32[112,128]{1,0:T(8,128)S(1)}, f32[112,128]{1,0:T(8,128)S(1)}, u32[]{:S(2)}, u32[]{:S(2)}) collective-permute-start(f32[112,128]{1,0:T(8,128)S(1)} %get-tuple-element.41), channel_id=1, source_target_pairs={{0,8},{4,12},{8,0},{12,4},{16,24},{20,28},{24,16},{28,20},{1,9},{5... | collective-permute-start | bytes 172040 | tf_op jit(solution)/shard_map/ppermute | solution.py:273
  29.2 15.6 %collective-permute-start.13 = (f32[112,128]{1,0:T(8,128)S(1)}, f32[112,128]{1,0:T(8,128)S(1)}, u32[]{:S(2)}, u32[]{:S(2)}) collective-permute-start(f32[112,128]{1,0:T(8,128)S(1)} %get-tuple-element.42), channel_id=1, source_target_pairs={{0,16},{4,20},{8,24},{12,28},{16,0},{20,4},{24,8},{28,12},{1,17},{... | collective-permute-start | bytes 172040 | tf_op jit(solution)/shard_map/ppermute | solution.py:273
  31.6 13.7 %collective-permute-start.14 = (f32[112,128]{1,0:T(8,128)S(1)}, f32[112,128]{1,0:T(8,128)S(1)}, u32[]{:S(2)}, u32[]{:S(2)}) collective-permute-start(f32[112,128]{1,0:T(8,128)S(1)} %get-tuple-element.43), channel_id=1, source_target_pairs={{0,20},{4,16},{8,28},{12,24},{16,4},{20,0},{24,12},{28,8},{1,21},{... | collective-permute-start | bytes 172040 | tf_op jit(solution)/shard_map/ppermute | solution.py:273
  32.4 12.9 %collective-permute-start.15 = (f32[112,128]{1,0:T(8,128)S(1)}, f32[112,128]{1,0:T(8,128)S(1)}, u32[]{:S(2)}, u32[]{:S(2)}) collective-permute-start(f32[112,128]{1,0:T(8,128)S(1)} %get-tuple-element.44), channel_id=1, source_target_pairs={{0,12},{4,8},{8,4},{12,0},{16,28},{20,24},{24,20},{28,16},{1,13},{... | collective-permute-start | bytes 172040 | tf_op jit(solution)/shard_map/ppermute | solution.py:273
  33.6 11.8 %collective-permute-start.16 = (f32[112,128]{1,0:T(8,128)S(1)}, f32[112,128]{1,0:T(8,128)S(1)}, u32[]{:S(2)}, u32[]{:S(2)}) collective-permute-start(f32[112,128]{1,0:T(8,128)S(1)} %get-tuple-element.45), channel_id=1, source_target_pairs={{0,24},{4,28},{8,16},{12,20},{16,8},{20,12},{24,0},{28,4},{1,25},{... | collective-permute-start | bytes 172040 | tf_op jit(solution)/shard_map/ppermute | solution.py:273
  36.9 8.4 %collective-permute-start.17 = (f32[112,128]{1,0:T(8,128)S(1)}, f32[112,128]{1,0:T(8,128)S(1)}, u32[]{:S(2)}, u32[]{:S(2)}) collective-permute-start(f32[112,128]{1,0:T(8,128)S(1)} %get-tuple-element.46), channel_id=1, source_target_pairs={{0,28},{4,24},{8,20},{12,16},{16,12},{20,8},{24,4},{28,0},{1,29},{... | collective-permute-start | bytes 172040 | tf_op jit(solution)/shard_map/ppermute | solution.py:273
  52.3 19.4 %all-to-all-start.1 = ((f32[32,28,128]{2,1,0:T(8,128)}), f32[32,28,128]{2,1,0:T(8,128)S(1)}, u32[]{:S(2)}, u32[]{:S(2)}) async-start(f32[32,28,128]{2,1,0:T(8,128)} %shard_map.77), calls=%async_computation.1 | async-start | bytes 1048576 | tf_op jit(solution)/shard_map/all_to_all | solution.py:374
  72.3 2.0 %collective-permute-start.18 = (f32[224,128]{1,0:T(8,128)S(1)}, f32[224,128]{1,0:T(8,128)S(1)}, u32[]{:S(2)}, u32[]{:S(2)}) collective-permute-start(f32[224,128]{1,0:T(8,128)S(1)} %get-tuple-element.51), channel_id=1, source_target_pairs={{0,1},{1,0},{2,3},{3,2},{4,5},{5,4},{6,7},{7,6},{8,9},{9,8},{10,11... | collective-permute-start | bytes 344072 | tf_op jit(solution)/shard_map/ppermute | solution.py:273
  72.4 6.0 %collective-permute-start.19 = (f32[224,128]{1,0:T(8,128)S(1)}, f32[224,128]{1,0:T(8,128)S(1)}, u32[]{:S(2)}, u32[]{:S(2)}) collective-permute-start(f32[224,128]{1,0:T(8,128)S(1)} %get-tuple-element.50), channel_id=1, source_target_pairs={{0,2},{1,3},{2,0},{3,1},{4,6},{5,7},{6,4},{7,5},{8,10},{9,11},{10,... | collective-permute-start | bytes 344072 | tf_op jit(solution)/shard_map/ppermute | solution.py:273
  73.7 6.3 %collective-permute-start.20 = (f32[224,128]{1,0:T(8,128)S(1)}, f32[224,128]{1,0:T(8,128)S(1)}, u32[]{:S(2)}, u32[]{:S(2)}) collective-permute-start(f32[224,128]{1,0:T(8,128)S(1)} %get-tuple-element.49), channel_id=1, source_target_pairs={{0,3},{1,2},{2,1},{3,0},{4,7},{5,6},{6,5},{7,4},{8,11},{9,10},{10,... | collective-permute-start | bytes 344072 | tf_op jit(solution)/shard_map/ppermute | solution.py:273
  80.0 0.8 copy-start.4

commit v6 on v5

--- a/solution.py
+++ b/solution.py
@@ -18,12 +18,24 @@
     return high, low
 
 
+def thirds(value):
+    high = value.astype(jnp.bfloat16)
+    rest = value - high.astype(jnp.float32)
+    middle = rest.astype(jnp.bfloat16)
+    return high, middle, (rest - middle.astype(jnp.float32)).astype(jnp.bfloat16)
+
+
 def product(a, b):
     return jnp.dot(a, b, preferred_element_type=jnp.float32)
 
 
 def product3(a, b):
     return product(a[0], b[0]) + product(a[1], b[0]) + product(a[0], b[1])
+
+
+def product6(a, b):
+    small = product(a[2], b[0]) + product(a[0], b[2]) + product(a[1], b[1])
+    return small + product(a[1], b[0]) + product(a[0], b[1]) + product(a[0], b[0])
 
 
 def three_parts(value):
@@ -43,7 +55,7 @@
     return [min(b, slab - ROWS) for b in range(0, slab, ROWS)]
 
 
-def mixer(projection, channel_of, height, rep_index, rep_count, share, group):
+def mixer(projection, channel_of, height, rep_index, rep_count, share, group, split=halves):
     channels = projection.shape[0]
     width = rep_count * group * share
     place = iota((height, channels), 0) // group
@@ -53,7 +65,7 @@
     pick = one_where(iota((channels, width), 0) == j)
     keep = iota((height, width), 0) % group == (iota((height, width), 1) // share) % group
     out = []
-    for part in halves(projection):
+    for part in split(projection):
         wide = product(product(spread, part).astype(jnp.bfloat16), pick)
         out.append(jnp.where(keep, wide, 0.0).astype(jnp.bfloat16))
     return out
@@ -69,7 +81,7 @@
 def state_mixer_kernel(rep_count, share, places_ref, table_ref, mix_ref):
     channels = table_ref.shape[0] - ROWS
     projection = table_ref[ROWS:, 0:channels]
-    parts = mixer(projection, lambda i: i, mix_ref.shape[1], places_ref[1], rep_count, share, ROWS)
+    parts = mixer(projection, lambda i: i, mix_ref.shape[1], places_ref[1], rep_count, share, ROWS, thirds)
     for at, part in enumerate(parts):
         mix_ref[at] = part
 
@@ -77,10 +89,10 @@
 def project_state_kernel(share, slab, places_ref, mix_ref, table_ref, *refs):
     slab_refs, out_ref = refs[:-1], refs[-1]
     channels, length, faces = out_ref.shape
-    mix = mix_ref[0], mix_ref[1]
+    mix = mix_ref[0], mix_ref[1], mix_ref[2]
     for b in starts(slab):
         pieces = [ref[pl.ds(b * share, ROWS * share), :] for ref in slab_refs]
-        out = product3(mix, halves(jnp.concatenate(pieces, axis=0))).reshape(channels, ROWS, faces)
+        out = product6(mix, thirds(jnp.concatenate(pieces, axis=0))).reshape(channels, ROWS, faces)
         out_ref[:, pl.ds(b, ROWS), :] = out
     tail = table_ref[pl.ds(places_ref[1] * (length - slab), length - slab), :]
     out_ref[:, slab:length, :] = jnp.broadcast_to(tail[None], (channels,) + tail.shape)
@@ -147,7 +159,7 @@
         then(*tile, made.pop(at))
 
 
-def slope_kernel(rep_count, slab, packed_ref, mortar_ref, info_ref, state_ref, maps_ref, mapped_ref, labels_ref, arrived):
+def slope_kernel(rep_count, slab, packed_ref, mortar_ref, info_ref, state_ref, maps_ref, mapped_ref, extra_ref, labels_ref, arrived):
     planes, total, faces = info_ref.shape
     partner_count = planes - 2
     devices = packed_ref.shape[0]
@@ -169,17 +181,29 @@
     owners = jnp.broadcast_to(owner_column, (total, faces))
     small_owners = owners.astype(jnp.bfloat16)
     copy.wait()
-    map_parts(state_ref[...], partner_count, faces, info_ref, maps_ref, mapped_ref)
+    for k in range(partner_count):
+        high, middle, low = thirds(info_ref[partner_count + 1, k * faces : (k + 1) * faces, :])
+        for at, part in enumerate((high, high, middle, high, low, middle)):
+            maps_ref[at * faces : (at + 1) * faces, k * faces : (k + 1) * faces] = part
+    high, middle, low = thirds(state_ref[...])
+    mapped = product(jnp.concatenate([high, middle, high, low, high, middle], axis=1), maps_ref[...])
+    for k in range(partner_count):
+        high, middle, low = thirds(mapped[:, k * faces : (k + 1) * faces])
+        mapped_ref[k, :, :faces] = high
+        mapped_ref[k, :, faces:] = middle
+        extra_ref[k, :, :faces] = low
+        extra_ref[k, :, faces:] = small_owners
     rows = total // 2
 
     def first(k, r):
         hot = one_hot(k, r, rows, partner_count, info_ref)
-        return gather(hot, mapped_ref[k]), product(hot, small_owners)
+        return gather(hot, mapped_ref[k]), product(hot, extra_ref[k])
 
     def then(k, r, made):
-        gathered, partner_owner = made
+        gathered, extra = made
+        gathered = gathered + extra[:, :faces]
         span = pl.ds(r, rows)
-        agree = partner_owner == info_ref[partner_count, span, partner_count : partner_count + 1]
+        agree = extra[:, faces:] == info_ref[partner_count, span, partner_count : partner_count + 1]
         small = jnp.exp(-sharpness * jnp.abs(state_ref[span, :] - gathered))
         slope = sharpness * small / ((1.0 + small) * (1.0 + small))
         info_ref[k, span, :] = jnp.where(agree, slope, 0.0)
@@ -301,7 +325,7 @@
     table = jnp.concatenate([labels, jnp.pad(projection, ((0, 0), (0, faces - channels)))], axis=0)
     state_mix = pl.pallas_call(
         functools.partial(state_mixer_kernel, rep_count, share),
-        out_shape=array(2, size, size, dtype=jnp.bfloat16),
+        out_shape=array(3, size, size, dtype=jnp.bfloat16),
         in_specs=[smem, vmem],
         out_specs=vmem,
         compiler_params=params,
@@ -336,7 +360,8 @@
         out_specs=vmem,
         scratch_shapes=[
             scratch(total, faces),
-            scratch(3 * faces, partner_count * faces, dtype=jnp.bfloat16),
+            scratch(6 * faces, partner_count * faces, dtype=jnp.bfloat16),
+            scratch(partner_count, total, 2 * faces, dtype=jnp.bfloat16),
             scratch(partner_count, total, 2 * faces, dtype=jnp.bfloat16),
             scratch(LANES, LANES),
             pltpu.SemaphoreType.DMA,

time: 81.2 us -> 82.5 us (1.016)
  Pallas kernels: 17.6 us -> 18.9 us
  starting transfers between devices: 31.3 us -> 32.5 us
  waiting for transfers between devices: 27.2 us -> 26 us
    ppermute x21, waiting for transfers between devices: 10.4 us -> 9.12 us  [swap(): return lax.ppermute(value, axis, [(i, i ^ d) for i in range(count)])]
    all_to_all x1, starting transfers between devices: 3.8 us -> 4.82 us  [spread_local(): returned = lax.all_to_all(summed, ('vol', 'rep'), 0, 0, tiled=True)]
  transfers between devices with their start and end apart: 23 -> 23, of which waited for: 9 -> 8; matrix products, arithmetic and copies ran while one was open for 3% -> 3% of each run, Pallas kernels for 12% -> 14%
where the time goes in v6:
time: 82.5 us; the launch traced here: 82.1 us
  starting transfers between devices  32.5 us (39%)
  waiting for transfers between devices  26 us (32%)
  Pallas kernels  18.9 us (23%)
  local copies, waits for them, and re-layouts  2.82 us (3%)
  other arithmetic  1.54 us (2%)
    ppermute x21, starting transfers between devices, swap(): return lax.ppermute(value, axis, [(i, i ^ d) for i in range(count)])  24.6 us
    all_to_all x1, waiting for transfers between devices, spread_local(): returned = lax.all_to_all(summed, ('vol', 'rep'), 0, 0, tiled=True)  14.5 us
    ppermute x21, waiting for transfers between devices, swap(): return lax.ppermute(value, axis, [(i, i ^ d) for i in range(count)])  9.12 us
    pallas_call x1, Pallas kernels, spread_local(): pl.pallas_call(functools.partial(contact_kernel, tuple(order), tuple(turn...  6.99 us
    pallas_call x1, Pallas kernels, spread_local(): pl.pallas_call(functools.partial(slope_kernel, rep_count, slab), out_shap...  5.6 us
    all_to_all x1, starting transfers between devices, spread_local(): returned = lax.all_to_all(summed, ('vol', 'rep'), 0, 0, tiled=True)  4.82 us
    all_to_all x1, starting transfers between devices, spread_local(): packed = lax.all_to_all(sent, ('vol', 'rep'), 0, 0, tiled=True)  3.04 us
    all_to_all x1, waiting for transfers between devices, spread_local(): packed = lax.all_to_all(sent, ('vol', 'rep'), 0, 0, tiled=True)  2.38 us
  transfers between devices with their start and end apart: 23, of which 8 were waited for; matrix products, arithmetic and copies ran while one was open for 3% of the time, Pallas kernels for 14%

profile of v6, /device:TPU:0, one launch (start us, length us, event | category | flops | bytes accessed | tf_op | source)
XLA Modules:
  0.0 82.1 jit_solution(15075470615185963587)
XLA Ops:
  0.0 0.8 copy-done
  0.8 3.0 %collective-permute-start.3 = (f32[56,128]{1,0:T(8,128)S(1)}, f32[56,128]{1,0:T(8,128)S(1)}, u32[]{:S(2)}, u32[]{:S(2)}) collective-permute-start(f32[56,128]{1,0:T(8,128)S(1)} %constant_dynamic-slice_fusion), channel_id=1, source_target_pairs={{0,4},{4,0},{8,12},{12,8},{16,20},{20,16},{24,28},{28,24},{1,5},{5... | collective-permute-start | bytes 86024 | tf_op jit(solution)/shard_map/ppermute | solution.py:297
  3.8 1.1 %dynamic-slice_bitcast_fusion = (f32[224,128]{1,0:T(8,128)S(1)}, f32[224,128]{1,0:T(8,128)S(1)}, f32[224,128]{1,0:T(8,128)S(1)}, f32[224,128]{1,0:T(8,128)S(1)}) fusion(f32[112,8,128]{2,1,0:T(8,128)} %param.7, s32[]{:T(128)S(6)} %select_n.39, s32[]{:T(128)S(6)} %select_n.37, s32[]{:T(128)S(6)} %select_n.36, s32[]{:T(128)S(6)} %select_n.38), kind=kLoop, calls=%fused_computation.6 | loop fusion | bytes 917520 | tf_op jit(solution)/shard_map/reshape | solution.py:303
  5.0 1.6 %collective-permute-start.5 = (f32[224,128]{1,0:T(8,128)S(1)}, f32[224,128]{1,0:T(8,128)S(1)}, u32[]{:S(2)}, u32[]{:S(2)}) collective-permute-start(f32[224,128]{1,0:T(8,128)S(1)} %get-tuple-element.55), channel_id=1, source_target_pairs={{0,2},{1,3},{2,0},{3,1},{4,6},{5,7},{6,4},{7,5},{8,10},{9,11},{10,... | collective-permute-start | bytes 344072 | tf_op jit(solution)/shard_map/ppermute | solution.py:297
  6.8 1.5 %collective-permute-start.1 = (f32[896,128]{1,0:T(8,128)}, f32[896,128]{1,0:T(8,128)S(1)}, u32[]{:S(2)}, u32[]{:S(2)}) collective-permute-start(f32[896,128]{1,0:T(8,128)} %bitcast.30), channel_id=1, source_target_pairs={{0,2},{1,3},{2,0},{3,1},{4,6},{5,7},{6,4},{7,5},{8,10},{9,11},{10,... | collective-permute-start | bytes 1376264 | tf_op jit(solution)/shard_map/ppermute | solution.py:297
  8.3 0.7 add_convert_fusion
  9.0 0.7 select_maximum_fusion.table_ref
  9.8 3.7 %collective-permute-start.7 = (f32[2,56,128]{2,1,0:T(8,128)S(1)}, f32[2,56,128]{2,1,0:T(8,128)S(1)}, u32[]{:S(2)}, u32[]{:S(2)}) collective-permute-start(f32[2,56,128]{2,1,0:T(8,128)S(1)} %pad_maximum_fusion.1), channel_id=1, source_target_pairs={{0,24},{4,28},{8,16},{12,20},{16,8},{20,12},{24,0},{28,4},{1,25},{... | collective-permute-start | bytes 172040 | tf_op jit(solution)/shard_map/ppermute | solution.py:297
  13.4 0.8 collective-permute-start.9
  14.3 1.0 %shard_map.73.mix_ref = bf16[3,256,256]{2,1,0:T(8,128)(2,1)S(1)} custom-call(s32[2]{0:T(128)S(1)} %pad_add_fusion.places_ref.after_ref, f32[40,128]{1,0:T(8,128)S(1)} %select_maximum_fusion.table_ref), custom_call_target="tpu_custom_call" | custom-call | tf_op jit(solution)/shard_map/pallas_call | solution.py:326
  15.4 2.4 %shard_map.74 = f32[32,30,128]{2,1,0:T(8,128)} custom-call(s32[2]{0:T(128)S(1)} %pad_add_fusion.places_ref.after_ref, bf16[3,256,256]{2,1,0:T(8,128)(2,1)S(1)} %shard_map.73.mix_ref, f32[40,128]{1,0:T(8,128)S(1)} %select_maximum_fusion.table_ref, f32[224,128]{1,0:T(8,128)S(1)} %get-tuple-element.27.refs_0_, f32[224,128]{1,0:T(8,128)S(1)} %collective-permute-done.4.refs_1_, ...), custom_call_target="tpu_custom_call" | custom-call | tf_op jit(solution)/shard_map/pallas_call | solution.py:334
  17.7 1.0 %collective-permute-done.8 = f32[2,56,128]{2,1,0:T(8,128)S(1)} collective-permute-done((f32[2,56,128]{2,1,0:T(8,128)S(1)}, f32[2,56,128]{2,1,0:T(8,128)S(1)}, u32[]{:S(2)}, u32[]{:S(2)}) %collective-permute-start.8) | collective-permute-done | bytes 57376 | tf_op jit(solution)/shard_map/ppermute | solution.py:297
  18.8 3.0 %all-to-all-start = ((f32[32,30,128]{2,1,0:T(8,128)}), f32[32,30,128]{2,1,0:T(8,128)S(1)}, u32[]{:S(2)}, u32[]{:S(2)}) async-start(f32[32,30,128]{2,1,0:T(8,128)} %shard_map.74), calls=%async_computation | async-start | bytes 1048576 | tf_op jit(solution)/shard_map/all_to_all | solution.py:342
  22.1 0.7 collective-permute-done.1.refs_2_
  23.3 1.6 %collective-permute-done.10 = f32[8,56,128]{2,1,0:T(8,128)S(1)} collective-permute-done((f32[8,56,128]{2,1,0:T(8,128)S(1)}, f32[8,56,128]{2,1,0:T(8,128)S(1)}, u32[]{:S(2)}, u32[]{:S(2)}) %collective-permute-start.10) | collective-permute-done | bytes 229408 | tf_op jit(solution)/shard_map/ppermute | solution.py:297
  25.0 1.4 %shard_map.76 = (f32[112,128]{1,0:T(8,128)S(1)}, f32[112,128]{1,0:T(8,128)S(1)}, f32[112,128]{1,0:T(8,128)S(1)}, f32[112,128]{1,0:T(8,128)S(1)}, f32[112,128]{1,...) custom-call(s32[2]{0:T(128)S(1)} %pad_add_fusion.places_ref.after_ref, ...), custom_call_target="tpu_custom_call" | custom-call | tf_op jit(solution)/shard_map/pallas_call | solution.py:347
  26.4 1.5 %collective-permute-start.11 = (f32[112,128]{1,0:T(8,128)S(1)}, f32[112,128]{1,0:T(8,128)S(1)}, u32[]{:S(2)}, u32[]{:S(2)}) collective-permute-start(f32[112,128]{1,0:T(8,128)S(1)} %get-tuple-element.40), channel_id=1, source_target_pairs={{0,4},{4,0},{8,12},{12,8},{16,20},{20,16},{24,28},{28,24},{1,5},{5... | collective-permute-start | bytes 172040 | tf_op jit(solution)/shard_map/ppermute | solution.py:297
  27.9 1.5 %collective-permute-start.12 = (f32[112,128]{1,0:T(8,128)S(1)}, f32[112,128]{1,0:T(8,128)S(1)}, u32[]{:S(2)}, u32[]{:S(2)}) collective-permute-start(f32[112,128]{1,0:T(8,128)S(1)} %get-tuple-element.41), channel_id=1, source_target_pairs={{0,8},{4,12},{8,0},{12,4},{16,24},{20,28},{24,16},{28,20},{1,9},{5... | collective-permute-start | bytes 172040 | tf_op jit(solution)/shard_map/ppermute | solution.py:297
  29.3 2.4 %collective-permute-start.13 = (f32[112,128]{1,0:T(8,128)S(1)}, f32[112,128]{1,0:T(8,128)S(1)}, u32[]{:S(2)}, u32[]{:S(2)}) collective-permute-start(f32[112,128]{1,0:T(8,128)S(1)} %get-tuple-element.42), channel_id=1, source_target_pairs={{0,16},{4,20},{8,24},{12,28},{16,0},{20,4},{24,8},{28,12},{1,17},{... | collective-permute-start | bytes 172040 | tf_op jit(solution)/shard_map/ppermute | solution.py:297
  31.8 0.7 collective-permute-start.14
  32.4 1.3 %collective-permute-start.15 = (f32[112,128]{1,0:T(8,128)S(1)}, f32[112,128]{1,0:T(8,128)S(1)}, u32[]{:S(2)}, u32[]{:S(2)}) collective-permute-start(f32[112,128]{1,0:T(8,128)S(1)} %get-tuple-element.44), channel_id=1, source_target_pairs={{0,12},{4,8},{8,4},{12,0},{16,28},{20,24},{24,20},{28,16},{1,13},{... | collective-permute-start | bytes 172040 | tf_op jit(solution)/shard_map/ppermute | solution.py:297
  33.7 3.3 %collective-permute-start.16 = (f32[112,128]{1,0:T(8,128)S(1)}, f32[112,128]{1,0:T(8,128)S(1)}, u32[]{:S(2)}, u32[]{:S(2)}) collective-permute-start(f32[112,128]{1,0:T(8,128)S(1)} %get-tuple-element.45), channel_id=1, source_target_pairs={{0,24},{4,28},{8,16},{12,20},{16,8},{20,12},{24,0},{28,4},{1,25},{... | collective-permute-start | bytes 172040 | tf_op jit(solution)/shard_map/ppermute | solution.py:297
  37.6 2.4 %all-to-all-done.packed_ref = f32[32,30,128]{2,1,0:T(8,128)S(1)} async-done(((f32[32,30,128]{2,1,0:T(8,128)}), f32[32,30,128]{2,1,0:T(8,128)S(1)}, u32[]{:S(2)}, u32[]{:S(2)}) %all-to-all-start) | async-done | bytes 491552 | tf_op jit(solution)/shard_map/all_to_all | solution.py:342
  40.0 5.6 %shard_map.75.info_ref = f32[6,896,128]{2,1,0:T(8,128)S(1)} custom-call(f32[32,30,128]{2,1,0:T(8,128)S(1)} %all-to-all-done.packed_ref, f32[512,128]{1,0:T(8,128)S(1)} %bitcast.33), custom_call_target="tpu_custom_call" | custom-call | tf_op jit(solution)/shard_map/pallas_call | solution.py:356
  45.6 7.0 %shard_map.77 = f32[32,28,128]{2,1,0:T(8,128)} custom-call(s32[2]{0:T(128)S(1)} %pad_add_fusion.places_ref.after_ref, f32[2,8,56,128]{3,2,1,0:T(8,128)S(1)} %pad_maximum_fusion.stiffness_ref, f32[6,896,128]{2,1,0:T(8,128)S(1)} %shard_map.75.info_ref, f32[112,128]{1,0:T(8,128)S(1)} %get-tuple-element.39.refs_0_, ...), custom_call_target="tpu_custom_call" | custom-call | tf_op jit(solution)/shard_map/pallas_call | solution.py:374
  52.6 4.8 %all-to-all-start.1 = ((f32[32,28,128]{2,1,0:T(8,128)}), f32[32,28,128]{2,1,0:T(8,128)S(1)}, u32[]{:S(2)}, u32[]{:S(2)}) async-start(f32[32,28,128]{2,1,0:T(8,128)} %shard_map.77), calls=%async_computation.1 | async-start | bytes 1048576 | tf_op jit(solution)/shard_map/all_to_all | solution.py:399
  57.5 1.0 %shard_map.78.mix_ref = bf16[2,256,256]{2,1,0:T(8,128)(2,1)S(1)} custom-call(s32[2]{0:T(128)S(1)} %pad_add_fusion.places_ref.after_ref, f32[32,32]{1,0:T(8,128)S(1)} %copy-done.3, s32[2]{0:T(128)S(1)} %pad_add_fusion.places_ref.after_ref), custom_call_target="tpu_custom_call" | custom-call | tf_op jit(solution)/shard_map/pallas_call | solution.py:392
  58.5 14.5 %all-to-all-done.1.summed_ref = f32[32,28,128]{2,1,0:T(8,128)S(1)} async-done(((f32[32,28,128]{2,1,0:T(8,128)}), f32[32,28,128]{2,1,0:T(8,128)S(1)}, u32[]{:S(2)}, u32[]{:S(2)}) %all-to-all-start.1) | async-done | bytes 458784 | tf_op jit(solution)/shard_map/all_to_all | solution.py:399
  73.7 1.3 %collective-permute-start.19 = (f32[224,128]{1,0:T(8,128)S(1)}, f32[224,128]{1,0:T(8,128)S(1)}, u32[]{:S(2)}, u32[]{:S(2)}) collective-permute-start(f32[224,128]{1,0:T(8,128)S(1)} %get-tuple-element.50), channel_id=1, source_target_pairs={{0,2},{1,3},{2,0},{3,1},{4,6},{5,7},{6,4},{7,5},{8,10},{9,11},{10,... | collective-permute-start | bytes 344072 | tf_op jit(solution)/shard_map/ppermute | solution.py:297
  75.7 4.1 %collective-permute-done.19 = f32[224,128]{1,0:T(8,128)S(1)} collective-permute-done((f32[224,128]{1,0:T(8,128)S(1)}, f32[224,128]{1,0:T(8,128)S(1)}, u32[]{:S(2)}, u32[]{:S(2)}) %collective-permute-start.19) | collective-permute-done | bytes 114720 | tf_op jit(solution)/shard_map/ppermute | solution.py:297
  79.7 1.5 %collective-permute-done.20 = f32[224,128]{1,0:T(8,128)S(1)} collective-permute-done((f32[224,128]{1,0:T(8,128)S(1)}, f32[224,128]{1,0:T(8,128)S(1)}, u32[]{:S(2)}, u32[]{:S(2)}) %collective-permute-start.20) | collective-permute-done | bytes 114720 | tf_op jit(solution)/shard_map/ppermute | solution.py:297
  81.3 0.8 copy-done.4
  (49 shorter events, 3.2 us)
Async XLA Ops:
  0.0 0.8 copy-start
  0.0 21.9 %copy-start.1 = (f32[112,8,128]{2,1,0:T(8,128)S(1)}, f32[112,8,128]{2,1,0:T(8,128)}, u32[]{:S(2)}) copy-start(f32[112,8,128]{2,1,0:T(8,128)} %param.8) | copy-start | bytes 1376260
  0.0 25.0 %copy-start.3 = (f32[32,32]{1,0:T(8,128)S(1)}, f32[32,32]{1,0:T(8,128)}, u32[]{:S(2)}) copy-start(f32[32,32]{1,0:T(8,128)} %projection_ref.3) | copy-start | bytes 12292
  0.8 8.9 %collective-permute-start.3 = (f32[56,128]{1,0:T(8,128)S(1)}, f32[56,128]{1,0:T(8,128)S(1)}, u32[]{:S(2)}, u32[]{:S(2)}) collective-permute-start(f32[56,128]{1,0:T(8,128)S(1)} %constant_dynamic-slice_fusion), channel_id=1, source_target_pairs={{0,4},{4,0},{8,12},{12,8},{16,20},{20,16},{24,28},{28,24},{1,5},{5... | collective-permute-start | bytes 86024 | tf_op jit(solution)/shard_map/ppermute | solution.py:297
  4.9 8.5 %collective-permute-start.4 = (f32[224,128]{1,0:T(8,128)S(1)}, f32[224,128]{1,0:T(8,128)S(1)}, u32[]{:S(2)}, u32[]{:S(2)}) collective-permute-start(f32[224,128]{1,0:T(8,128)S(1)} %get-tuple-element.53), channel_id=1, source_target_pairs={{0,1},{1,0},{2,3},{3,2},{4,5},{5,4},{6,7},{7,6},{8,9},{9,8},{10,11... | collective-permute-start | bytes 344072 | tf_op jit(solution)/shard_map/ppermute | solution.py:297
  5.0 8.5 %collective-permute-start.5 = (f32[224,128]{1,0:T(8,128)S(1)}, f32[224,128]{1,0:T(8,128)S(1)}, u32[]{:S(2)}, u32[]{:S(2)}) collective-permute-start(f32[224,128]{1,0:T(8,128)S(1)} %get-tuple-element.55), channel_id=1, source_target_pairs={{0,2},{1,3},{2,0},{3,1},{4,6},{5,7},{6,4},{7,5},{8,10},{9,11},{10,... | collective-permute-start | bytes 344072 | tf_op jit(solution)/shard_map/ppermute | solution.py:297
  6.5 8.8 %collective-permute-start.6 = (f32[224,128]{1,0:T(8,128)S(1)}, f32[224,128]{1,0:T(8,128)S(1)}, u32[]{:S(2)}, u32[]{:S(2)}) collective-permute-start(f32[224,128]{1,0:T(8,128)S(1)} %get-tuple-element.52), channel_id=1, source_target_pairs={{0,3},{1,2},{2,1},{3,0},{4,7},{5,6},{6,5},{7,4},{8,11},{9,10},{10,... | collective-permute-start | bytes 344072 | tf_op jit(solution)/shard_map/ppermute | solution.py:297
  6.8 16.0 %collective-permute-start.1 = (f32[896,128]{1,0:T(8,128)}, f32[896,128]{1,0:T(8,128)S(1)}, u32[]{:S(2)}, u32[]{:S(2)}) collective-permute-start(f32[896,128]{1,0:T(8,128)} %bitcast.30), channel_id=1, source_target_pairs={{0,2},{1,3},{2,0},{3,1},{4,6},{5,7},{6,4},{7,5},{8,10},{9,11},{10,... | collective-permute-start | bytes 1376264 | tf_op jit(solution)/shard_map/ppermute | solution.py:297
  9.8 8.0 %collective-permute-start.7 = (f32[2,56,128]{2,1,0:T(8,128)S(1)}, f32[2,56,128]{2,1,0:T(8,128)S(1)}, u32[]{:S(2)}, u32[]{:S(2)}) collective-permute-start(f32[2,56,128]{2,1,0:T(8,128)S(1)} %pad_maximum_fusion.1), channel_id=1, source_target_pairs={{0,24},{4,28},{8,16},{12,20},{16,8},{20,12},{24,0},{28,4},{1,25},{... | collective-permute-start | bytes 172040 | tf_op jit(solution)/shard_map/ppermute | solution.py:297
  13.4 5.3 %collective-permute-start.8 = (f32[2,56,128]{2,1,0:T(8,128)S(1)}, f32[2,56,128]{2,1,0:T(8,128)S(1)}, u32[]{:S(2)}, u32[]{:S(2)}) collective-permute-start(f32[2,56,128]{2,1,0:T(8,128)S(1)} %pad_maximum_fusion.1), channel_id=1, source_target_pairs={{0,16},{4,20},{8,24},{12,28},{16,0},{20,4},{24,8},{28,12},{1,17},{... | collective-permute-start | bytes 172040 | tf_op jit(solution)/shard_map/ppermute | solution.py:297
  13.4 5.4 %collective-permute-start.9 = (f32[2,56,128]{2,1,0:T(8,128)S(1)}, f32[2,56,128]{2,1,0:T(8,128)S(1)}, u32[]{:S(2)}, u32[]{:S(2)}) collective-permute-start(f32[2,56,128]{2,1,0:T(8,128)S(1)} %pad_maximum_fusion.1), channel_id=1, source_target_pairs={{0,8},{4,12},{8,0},{12,4},{16,24},{20,28},{24,16},{28,20},{1,9},{5... | collective-permute-start | bytes 172040 | tf_op jit(solution)/shard_map/ppermute | solution.py:297
  15.3 24.6 %copy-start.2 = (f32[4,128,128]{2,1,0:T(8,128)S(1)}, f32[4,128,128]{2,1,0:T(8,128)}, u32[]{:S(2)}) copy-start(f32[4,128,128]{2,1,0:T(8,128)} %param.13) | copy-start | bytes 786436
  18.8 21.1 %all-to-all-start = ((f32[32,30,128]{2,1,0:T(8,128)}), f32[32,30,128]{2,1,0:T(8,128)S(1)}, u32[]{:S(2)}, u32[]{:S(2)}) async-start(f32[32,30,128]{2,1,0:T(8,128)} %shard_map.74), calls=%async_computation | async-start | bytes 1048576 | tf_op jit(solution)/shard_map/all_to_all | solution.py:342
  21.9 3.1 %collective-permute-start = (f32[896,128]{1,0:T(8,128)S(1)}, f32[896,128]{1,0:T(8,128)S(1)}, u32[]{:S(2)}, u32[]{:S(2)}) collective-permute-start(f32[896,128]{1,0:T(8,128)S(1)} %bitcast.31), channel_id=1, source_target_pairs={{0,1},{1,0},{2,3},{3,2},{4,5},{5,4},{6,7},{7,6},{8,9},{9,8},{10,11... | collective-permute-start | bytes 1376264 | tf_op jit(solution)/shard_map/ppermute | solution.py:297
  22.8 2.2 %collective-permute-start.2 = (f32[896,128]{1,0:T(8,128)S(1)}, f32[896,128]{1,0:T(8,128)S(1)}, u32[]{:S(2)}, u32[]{:S(2)}) collective-permute-start(f32[896,128]{1,0:T(8,128)S(1)} %collective-permute-done.1.refs_2_), channel_id=1, source_target_pairs={{0,1},{1,0},{2,3},{3,2},{4,5},{5,4},{6,7},{7,6},{8,9},{9,8},{10,11... | collective-permute-start | bytes 1376264 | tf_op jit(solution)/shard_map/ppermute | solution.py:297
  22.8 2.1 %collective-permute-start.10 = (f32[8,56,128]{2,1,0:T(8,128)S(1)}, f32[8,56,128]{2,1,0:T(8,128)S(1)}, u32[]{:S(2)}, u32[]{:S(2)}) collective-permute-start(f32[8,56,128]{2,1,0:T(8,128)S(1)} %constant_dynamic-update-slice_fusion), channel_id=1, source_target_pairs={{0,1},{1,0},{2,3},{3,2},{4,5},{5,4},{6,7},{7,6},{8,9},{9,8},{10,11... | collective-permute-start | bytes 688136 | tf_op jit(solution)/shard_map/ppermute | solution.py:297
  26.4 7.3 %collective-permute-start.11 = (f32[112,128]{1,0:T(8,128)S(1)}, f32[112,128]{1,0:T(8,128)S(1)}, u32[]{:S(2)}, u32[]{:S(2)}) collective-permute-start(f32[112,128]{1,0:T(8,128)S(1)} %get-tuple-element.40), channel_id=1, source_target_pairs={{0,4},{4,0},{8,12},{12,8},{16,20},{20,16},{24,28},{28,24},{1,5},{5... | collective-permute-start | bytes 172040 | tf_op jit(solution)/shard_map/ppermute | solution.py:297
  27.9 9.2 %collective-permute-start.12 = (f32[112,128]{1,0:T(8,128)S(1)}, f32[112,128]{1,0:T(8,128)S(1)}, u32[]{:S(2)}, u32[]{:S(2)}) collective-permute-start(f32[112,128]{1,0:T(8,128)S(1)} %get-tuple-element.41), channel_id=1, source_target_pairs={{0,8},{4,12},{8,0},{12,4},{16,24},{20,28},{24,16},{28,20},{1,9},{5... | collective-permute-start | bytes 172040 | tf_op jit(solution)/shard_map/ppermute | solution.py:297
  29.3 16.3 %collective-permute-start.13 = (f32[112,128]{1,0:T(8,128)S(1)}, f32[112,128]{1,0:T(8,128)S(1)}, u32[]{:S(2)}, u32[]{:S(2)}) collective-permute-start(f32[112,128]{1,0:T(8,128)S(1)} %get-tuple-element.42), channel_id=1, source_target_pairs={{0,16},{4,20},{8,24},{12,28},{16,0},{20,4},{24,8},{28,12},{1,17},{... | collective-permute-start | bytes 172040 | tf_op jit(solution)/shard_map/ppermute | solution.py:297
  31.8 13.8 %collective-permute-start.14 = (f32[112,128]{1,0:T(8,128)S(1)}, f32[112,128]{1,0:T(8,128)S(1)}, u32[]{:S(2)}, u32[]{:S(2)}) collective-permute-start(f32[112,128]{1,0:T(8,128)S(1)} %get-tuple-element.43), channel_id=1, source_target_pairs={{0,20},{4,16},{8,28},{12,24},{16,4},{20,0},{24,12},{28,8},{1,21},{... | collective-permute-start | bytes 172040 | tf_op jit(solution)/shard_map/ppermute | solution.py:297
  32.4 13.2 %collective-permute-start.15 = (f32[112,128]{1,0:T(8,128)S(1)}, f32[112,128]{1,0:T(8,128)S(1)}, u32[]{:S(2)}, u32[]{:S(2)}) collective-permute-start(f32[112,128]{1,0:T(8,128)S(1)} %get-tuple-element.44), channel_id=1, source_target_pairs={{0,12},{4,8},{8,4},{12,0},{16,28},{20,24},{24,20},{28,16},{1,13},{... | collective-permute-start | bytes 172040 | tf_op jit(solution)/shard_map/ppermute | solution.py:297
  33.7 11.9 %collective-permute-start.16 = (f32[112,128]{1,0:T(8,128)S(1)}, f32[112,128]{1,0:T(8,128)S(1)}, u32[]{:S(2)}, u32[]{:S(2)}) collective-permute-start(f32[112,128]{1,0:T(8,128)S(1)} %get-tuple-element.45), channel_id=1, source_target_pairs={{0,24},{4,28},{8,16},{12,20},{16,8},{20,12},{24,0},{28,4},{1,25},{... | collective-permute-start | bytes 172040 | tf_op jit(solution)/shard_map/ppermute | solution.py:297
  37.1 8.6 %collective-permute-start.17 = (f32[112,128]{1,0:T(8,128)S(1)}, f32[112,128]{1,0:T(8,128)S(1)}, u32[]{:S(2)}, u32[]{:S(2)}) collective-permute-start(f32[112,128]{1,0:T(8,128)S(1)} %get-tuple-element.46), channel_id=1, source_target_pairs={{0,28},{4,24},{8,20},{12,16},{16,12},{20,8},{24,4},{28,0},{1,29},{... | collective-permute-start | bytes 172040 | tf_op jit(solution)/shard_map/ppermute | solution.py:297
  52.6 20.4 %all-to-all-start.1 = ((f32[32,28,128]{2,1,0:T(8,128)}), f32[32,28,128]{2,1,0:T(8,128)S(1)}, u32[]{:S(2)}, u32[]{:S(2)}) async-start(f32[32,28,128]{2,1,0:T(8,128)} %shard_map.77), calls=%async_computation.1 | async-start | bytes 1048576 | tf_op jit(solution)/shard_map/all_to_all | solution.py:399
  73.6 2.0 %collective-permute-start.18 = (f32[224,128]{1,0:T(8,128)S(1)}, f32[224,128]{1,0:T(8,128)S(1)}, u32[]{:S(2)}, u32[]{:S(2)}) collective-permute-start(f32[224,128]{1,0:T(8,128)S(1)} %get-tuple-element.51), channel_id=1, source_target_pairs={{0,1},{1,0},{2,3},{3,2},{4,5},{5,4},{6,7},{7,6},{8,9},{9,8},{10,11... | collective-permute-start | bytes 344072 | tf_op jit(solution)/shard_map/ppermute | solution.py:297
  73.7 6.0 %collective-permute-start.19 = (f32[224,128]{1,0:T(8,128)S(1)}, f32[224,128]{1,0:T(8,128)S(1)}, u32[]{:S(2)}, u32[]{:S(2)}) collective-permute-start(f32[224,128]{1,0:T(8,128)S(1)} %get-tuple-element.50), channel_id=1, source_target_pairs={{0,2},{1,3},{2,0},{3,1},{4,6},{5,7},{6,4},{7,5},{8,10},{9,11},{10,... | collective-permute-start | bytes 344072 | tf_op jit(solution)/shard_map/ppermute | solution.py:297
  75.0 6.3 %collective-permute-start.20 = (f32[224,128]{1,0:T(8,128)S(1)}, f32[224,128]{1,0:T(8,128)S(1)}, u32[]{:S(2)}, u32[]{:S(2)}) collective-permute-start(f32[224,128]{1,0:T(8,128)S(1)} %get-tuple-element.49), channel_id=1, source_target_pairs={{0,3},{1,2},{2,1},{3,0},{4,7},{5,6},{6,5},{7,4},{8,11},{9,10},{10,... | collective-permute-start | bytes 344072 | tf_op jit(solution)/shard_map/ppermute | solution.py:297
  81.3 0.8 copy-start.4

commit v7 on v6

--- a/solution.py
+++ b/solution.py
@@ -90,10 +90,16 @@
     slab_refs, out_ref = refs[:-1], refs[-1]
     channels, length, faces = out_ref.shape
     mix = mix_ref[0], mix_ref[1], mix_ref[2]
-    for b in starts(slab):
-        pieces = [ref[pl.ds(b * share, ROWS * share), :] for ref in slab_refs]
-        out = product6(mix, thirds(jnp.concatenate(pieces, axis=0))).reshape(channels, ROWS, faces)
-        out_ref[:, pl.ds(b, ROWS), :] = out
+    groups = starts(slab)
+    for at in range(0, len(groups), 2):
+        pair = groups[at : at + 2]
+        wide = [
+            jnp.concatenate([ref[pl.ds(b * share, ROWS * share), :] for ref in slab_refs], axis=0) for b in pair
+        ]
+        out = product6(mix, thirds(jnp.concatenate(wide, axis=1)))
+        for which, b in enumerate(pair):
+            part = out[:, which * faces : (which + 1) * faces]
+            out_ref[:, pl.ds(b, ROWS), :] = part.reshape(channels, ROWS, faces)
     tail = table_ref[pl.ds(places_ref[1] * (length - slab), length - slab), :]
     out_ref[:, slab:length, :] = jnp.broadcast_to(tail[None], (channels,) + tail.shape)
 

time: 82.5 us -> 81.8 us (level)
  transfers between devices with their start and end apart: 23 -> 23, of which waited for: 8 -> 8; matrix products, arithmetic and copies ran while one was open for 3% -> 3% of each run, Pallas kernels for 14% -> 13%
where the time goes in v7:
time: 81.8 us; the launch traced here: 81.3 us
  starting transfers between devices  31.7 us (39%)
  waiting for transfers between devices  26.4 us (32%)
  Pallas kernels  18.5 us (23%)
  local copies, waits for them, and re-layouts  2.82 us (3%)
  other arithmetic  1.54 us (2%)
    ppermute x21, starting transfers between devices, swap(): return lax.ppermute(value, axis, [(i, i ^ d) for i in range(count)])  24.8 us
    all_to_all x1, waiting for transfers between devices, spread_local(): returned = lax.all_to_all(summed, ('vol', 'rep'), 0, 0, tiled=True)  14.5 us
    ppermute x21, waiting for transfers between devices, swap(): return lax.ppermute(value, axis, [(i, i ^ d) for i in range(count)])  9.64 us
    pallas_call x1, Pallas kernels, spread_local(): pl.pallas_call(functools.partial(contact_kernel, tuple(order), tuple(turn...  6.99 us
    pallas_call x1, Pallas kernels, spread_local(): pl.pallas_call(functools.partial(slope_kernel, rep_count, slab), out_shap...  5.61 us
    all_to_all x1, starting transfers between devices, spread_local(): returned = lax.all_to_all(summed, ('vol', 'rep'), 0, 0, tiled=True)  4.2 us
    all_to_all x1, starting transfers between devices, spread_local(): packed = lax.all_to_all(sent, ('vol', 'rep'), 0, 0, tiled=True)  2.72 us
    all_to_all x1, waiting for transfers between devices, spread_local(): packed = lax.all_to_all(sent, ('vol', 'rep'), 0, 0, tiled=True)  2.24 us
  transfers between devices with their start and end apart: 23, of which 8 were waited for; matrix products, arithmetic and copies ran while one was open for 3% of the time, Pallas kernels for 13%

profile of v7, /device:TPU:0, one launch (start us, length us, event | category | flops | bytes accessed | tf_op | source)
XLA Modules:
  0.0 81.3 jit_solution(13918907921693689437)
XLA Ops:
  0.0 0.8 copy-done
  0.8 3.0 %collective-permute-start.3 = (f32[56,128]{1,0:T(8,128)S(1)}, f32[56,128]{1,0:T(8,128)S(1)}, u32[]{:S(2)}, u32[]{:S(2)}) collective-permute-start(f32[56,128]{1,0:T(8,128)S(1)} %constant_dynamic-slice_fusion), channel_id=1, source_target_pairs={{0,4},{4,0},{8,12},{12,8},{16,20},{20,16},{24,28},{28,24},{1,5},{5... | collective-permute-start | bytes 86024 | tf_op jit(solution)/shard_map/ppermute | solution.py:303
  3.8 1.1 %dynamic-slice_bitcast_fusion = (f32[224,128]{1,0:T(8,128)S(1)}, f32[224,128]{1,0:T(8,128)S(1)}, f32[224,128]{1,0:T(8,128)S(1)}, f32[224,128]{1,0:T(8,128)S(1)}) fusion(f32[112,8,128]{2,1,0:T(8,128)} %param.7, s32[]{:T(128)S(6)} %select_n.39, s32[]{:T(128)S(6)} %select_n.37, s32[]{:T(128)S(6)} %select_n.36, s32[]{:T(128)S(6)} %select_n.38), kind=kLoop, calls=%fused_computation.6 | loop fusion | bytes 917520 | tf_op jit(solution)/shard_map/reshape | solution.py:309
  5.0 1.6 %collective-permute-start.5 = (f32[224,128]{1,0:T(8,128)S(1)}, f32[224,128]{1,0:T(8,128)S(1)}, u32[]{:S(2)}, u32[]{:S(2)}) collective-permute-start(f32[224,128]{1,0:T(8,128)S(1)} %get-tuple-element.55), channel_id=1, source_target_pairs={{0,2},{1,3},{2,0},{3,1},{4,6},{5,7},{6,4},{7,5},{8,10},{9,11},{10,... | collective-permute-start | bytes 344072 | tf_op jit(solution)/shard_map/ppermute | solution.py:303
  6.8 1.5 %collective-permute-start.1 = (f32[896,128]{1,0:T(8,128)}, f32[896,128]{1,0:T(8,128)S(1)}, u32[]{:S(2)}, u32[]{:S(2)}) collective-permute-start(f32[896,128]{1,0:T(8,128)} %bitcast.30), channel_id=1, source_target_pairs={{0,2},{1,3},{2,0},{3,1},{4,6},{5,7},{6,4},{7,5},{8,10},{9,11},{10,... | collective-permute-start | bytes 1376264 | tf_op jit(solution)/shard_map/ppermute | solution.py:303
  8.3 0.7 add_convert_fusion
  9.0 0.7 select_maximum_fusion.table_ref
  9.8 3.7 %collective-permute-start.7 = (f32[2,56,128]{2,1,0:T(8,128)S(1)}, f32[2,56,128]{2,1,0:T(8,128)S(1)}, u32[]{:S(2)}, u32[]{:S(2)}) collective-permute-start(f32[2,56,128]{2,1,0:T(8,128)S(1)} %pad_maximum_fusion.1), channel_id=1, source_target_pairs={{0,24},{4,28},{8,16},{12,20},{16,8},{20,12},{24,0},{28,4},{1,25},{... | collective-permute-start | bytes 172040 | tf_op jit(solution)/shard_map/ppermute | solution.py:303
  13.4 0.8 collective-permute-start.9
  14.3 1.0 %shard_map.73.mix_ref = bf16[3,256,256]{2,1,0:T(8,128)(2,1)S(1)} custom-call(s32[2]{0:T(128)S(1)} %pad_add_fusion.places_ref.after_ref, f32[40,128]{1,0:T(8,128)S(1)} %select_maximum_fusion.table_ref), custom_call_target="tpu_custom_call" | custom-call | tf_op jit(solution)/shard_map/pallas_call | solution.py:332
  15.4 2.0 %shard_map.74 = f32[32,30,128]{2,1,0:T(8,128)} custom-call(s32[2]{0:T(128)S(1)} %pad_add_fusion.places_ref.after_ref, bf16[3,256,256]{2,1,0:T(8,128)(2,1)S(1)} %shard_map.73.mix_ref, f32[40,128]{1,0:T(8,128)S(1)} %select_maximum_fusion.table_ref, f32[224,128]{1,0:T(8,128)S(1)} %get-tuple-element.27.refs_0_, f32[224,128]{1,0:T(8,128)S(1)} %collective-permute-done.4.refs_1_, ...), custom_call_target="tpu_custom_call" | custom-call | tf_op jit(solution)/shard_map/pallas_call | solution.py:340
  17.4 1.4 %collective-permute-done.8 = f32[2,56,128]{2,1,0:T(8,128)S(1)} collective-permute-done((f32[2,56,128]{2,1,0:T(8,128)S(1)}, f32[2,56,128]{2,1,0:T(8,128)S(1)}, u32[]{:S(2)}, u32[]{:S(2)}) %collective-permute-start.8) | collective-permute-done | bytes 57376 | tf_op jit(solution)/shard_map/ppermute | solution.py:303
  18.8 2.7 %all-to-all-start = ((f32[32,30,128]{2,1,0:T(8,128)}), f32[32,30,128]{2,1,0:T(8,128)S(1)}, u32[]{:S(2)}, u32[]{:S(2)}) async-start(f32[32,30,128]{2,1,0:T(8,128)} %shard_map.74), calls=%async_computation | async-start | bytes 1048576 | tf_op jit(solution)/shard_map/all_to_all | solution.py:348
  21.9 0.9 %collective-permute-done.1.refs_2_ = f32[896,128]{1,0:T(8,128)S(1)} collective-permute-done((f32[896,128]{1,0:T(8,128)}, f32[896,128]{1,0:T(8,128)S(1)}, u32[]{:S(2)}, u32[]{:S(2)}) %collective-permute-start.1) | collective-permute-done | bytes 458784 | tf_op jit(solution)/shard_map/ppermute | solution.py:303
  23.3 1.6 %collective-permute-done.10 = f32[8,56,128]{2,1,0:T(8,128)S(1)} collective-permute-done((f32[8,56,128]{2,1,0:T(8,128)S(1)}, f32[8,56,128]{2,1,0:T(8,128)S(1)}, u32[]{:S(2)}, u32[]{:S(2)}) %collective-permute-start.10) | collective-permute-done | bytes 229408 | tf_op jit(solution)/shard_map/ppermute | solution.py:303
  25.0 1.4 %shard_map.76 = (f32[112,128]{1,0:T(8,128)S(1)}, f32[112,128]{1,0:T(8,128)S(1)}, f32[112,128]{1,0:T(8,128)S(1)}, f32[112,128]{1,0:T(8,128)S(1)}, f32[112,128]{1,...) custom-call(s32[2]{0:T(128)S(1)} %pad_add_fusion.places_ref.after_ref, ...), custom_call_target="tpu_custom_call" | custom-call | tf_op jit(solution)/shard_map/pallas_call | solution.py:353
  26.4 1.3 %collective-permute-start.11 = (f32[112,128]{1,0:T(8,128)S(1)}, f32[112,128]{1,0:T(8,128)S(1)}, u32[]{:S(2)}, u32[]{:S(2)}) collective-permute-start(f32[112,128]{1,0:T(8,128)S(1)} %get-tuple-element.40), channel_id=1, source_target_pairs={{0,4},{4,0},{8,12},{12,8},{16,20},{20,16},{24,28},{28,24},{1,5},{5... | collective-permute-start | bytes 172040 | tf_op jit(solution)/shard_map/ppermute | solution.py:303
  27.7 1.5 %collective-permute-start.12 = (f32[112,128]{1,0:T(8,128)S(1)}, f32[112,128]{1,0:T(8,128)S(1)}, u32[]{:S(2)}, u32[]{:S(2)}) collective-permute-start(f32[112,128]{1,0:T(8,128)S(1)} %get-tuple-element.41), channel_id=1, source_target_pairs={{0,8},{4,12},{8,0},{12,4},{16,24},{20,28},{24,16},{28,20},{1,9},{5... | collective-permute-start | bytes 172040 | tf_op jit(solution)/shard_map/ppermute | solution.py:303
  29.2 2.4 %collective-permute-start.13 = (f32[112,128]{1,0:T(8,128)S(1)}, f32[112,128]{1,0:T(8,128)S(1)}, u32[]{:S(2)}, u32[]{:S(2)}) collective-permute-start(f32[112,128]{1,0:T(8,128)S(1)} %get-tuple-element.42), channel_id=1, source_target_pairs={{0,16},{4,20},{8,24},{12,28},{16,0},{20,4},{24,8},{28,12},{1,17},{... | collective-permute-start | bytes 172040 | tf_op jit(solution)/shard_map/ppermute | solution.py:303
  31.6 0.8 collective-permute-start.14
  32.4 1.1 %collective-permute-start.15 = (f32[112,128]{1,0:T(8,128)S(1)}, f32[112,128]{1,0:T(8,128)S(1)}, u32[]{:S(2)}, u32[]{:S(2)}) collective-permute-start(f32[112,128]{1,0:T(8,128)S(1)} %get-tuple-element.44), channel_id=1, source_target_pairs={{0,12},{4,8},{8,4},{12,0},{16,28},{20,24},{24,20},{28,16},{1,13},{... | collective-permute-start | bytes 172040 | tf_op jit(solution)/shard_map/ppermute | solution.py:303
  33.6 3.3 %collective-permute-start.16 = (f32[112,128]{1,0:T(8,128)S(1)}, f32[112,128]{1,0:T(8,128)S(1)}, u32[]{:S(2)}, u32[]{:S(2)}) collective-permute-start(f32[112,128]{1,0:T(8,128)S(1)} %get-tuple-element.45), channel_id=1, source_target_pairs={{0,24},{4,28},{8,16},{12,20},{16,8},{20,12},{24,0},{28,4},{1,25},{... | collective-permute-start | bytes 172040 | tf_op jit(solution)/shard_map/ppermute | solution.py:303
  37.6 2.2 %all-to-all-done.packed_ref = f32[32,30,128]{2,1,0:T(8,128)S(1)} async-done(((f32[32,30,128]{2,1,0:T(8,128)}), f32[32,30,128]{2,1,0:T(8,128)S(1)}, u32[]{:S(2)}, u32[]{:S(2)}) %all-to-all-start) | async-done | bytes 491552 | tf_op jit(solution)/shard_map/all_to_all | solution.py:348
  39.8 5.6 %shard_map.75.info_ref = f32[6,896,128]{2,1,0:T(8,128)S(1)} custom-call(f32[32,30,128]{2,1,0:T(8,128)S(1)} %all-to-all-done.packed_ref, f32[512,128]{1,0:T(8,128)S(1)} %bitcast.33), custom_call_target="tpu_custom_call" | custom-call | tf_op jit(solution)/shard_map/pallas_call | solution.py:362
  45.5 7.0 %shard_map.77 = f32[32,28,128]{2,1,0:T(8,128)} custom-call(s32[2]{0:T(128)S(1)} %pad_add_fusion.places_ref.after_ref, f32[2,8,56,128]{3,2,1,0:T(8,128)S(1)} %pad_maximum_fusion.stiffness_ref, f32[6,896,128]{2,1,0:T(8,128)S(1)} %shard_map.75.info_ref, f32[112,128]{1,0:T(8,128)S(1)} %get-tuple-element.39.refs_0_, ...), custom_call_target="tpu_custom_call" | custom-call | tf_op jit(solution)/shard_map/pallas_call | solution.py:380
  52.5 4.2 %all-to-all-start.1 = ((f32[32,28,128]{2,1,0:T(8,128)}), f32[32,28,128]{2,1,0:T(8,128)S(1)}, u32[]{:S(2)}, u32[]{:S(2)}) async-start(f32[32,28,128]{2,1,0:T(8,128)} %shard_map.77), calls=%async_computation.1 | async-start | bytes 1048576 | tf_op jit(solution)/shard_map/all_to_all | solution.py:405
  56.7 1.0 %shard_map.78.mix_ref = bf16[2,256,256]{2,1,0:T(8,128)(2,1)S(1)} custom-call(s32[2]{0:T(128)S(1)} %pad_add_fusion.places_ref.after_ref, f32[32,32]{1,0:T(8,128)S(1)} %copy-done.3, s32[2]{0:T(128)S(1)} %pad_add_fusion.places_ref.after_ref), custom_call_target="tpu_custom_call" | custom-call | tf_op jit(solution)/shard_map/pallas_call | solution.py:398
  57.7 14.5 %all-to-all-done.1.summed_ref = f32[32,28,128]{2,1,0:T(8,128)S(1)} async-done(((f32[32,28,128]{2,1,0:T(8,128)}), f32[32,28,128]{2,1,0:T(8,128)S(1)}, u32[]{:S(2)}, u32[]{:S(2)}) %all-to-all-start.1) | async-done | bytes 458784 | tf_op jit(solution)/shard_map/all_to_all | solution.py:405
  73.0 1.3 %collective-permute-start.19 = (f32[224,128]{1,0:T(8,128)S(1)}, f32[224,128]{1,0:T(8,128)S(1)}, u32[]{:S(2)}, u32[]{:S(2)}) collective-permute-start(f32[224,128]{1,0:T(8,128)S(1)} %get-tuple-element.50), channel_id=1, source_target_pairs={{0,2},{1,3},{2,0},{3,1},{4,6},{5,7},{6,4},{7,5},{8,10},{9,11},{10,... | collective-permute-start | bytes 344072 | tf_op jit(solution)/shard_map/ppermute | solution.py:303
  74.9 4.1 %collective-permute-done.19 = f32[224,128]{1,0:T(8,128)S(1)} collective-permute-done((f32[224,128]{1,0:T(8,128)S(1)}, f32[224,128]{1,0:T(8,128)S(1)}, u32[]{:S(2)}, u32[]{:S(2)}) %collective-permute-start.19) | collective-permute-done | bytes 114720 | tf_op jit(solution)/shard_map/ppermute | solution.py:303
  79.0 1.5 %collective-permute-done.20 = f32[224,128]{1,0:T(8,128)S(1)} collective-permute-done((f32[224,128]{1,0:T(8,128)S(1)}, f32[224,128]{1,0:T(8,128)S(1)}, u32[]{:S(2)}, u32[]{:S(2)}) %collective-permute-start.20) | collective-permute-done | bytes 114720 | tf_op jit(solution)/shard_map/ppermute | solution.py:303
  80.5 0.8 copy-done.4
  (49 shorter events, 3.5 us)
Async XLA Ops:
  0.0 0.8 %copy-start = (f32[112,128]{1,0:T(8,128)S(1)}, f32[112,128]{1,0:T(8,128)}, u32[]{:S(2)}) copy-start(f32[112,128]{1,0:T(8,128)} %param.9) | copy-start | bytes 172036
  0.0 21.6 %copy-start.1 = (f32[112,8,128]{2,1,0:T(8,128)S(1)}, f32[112,8,128]{2,1,0:T(8,128)}, u32[]{:S(2)}) copy-start(f32[112,8,128]{2,1,0:T(8,128)} %param.8) | copy-start | bytes 1376260
  0.0 25.0 %copy-start.3 = (f32[32,32]{1,0:T(8,128)S(1)}, f32[32,32]{1,0:T(8,128)}, u32[]{:S(2)}) copy-start(f32[32,32]{1,0:T(8,128)} %projection_ref.3) | copy-start | bytes 12292
  0.8 8.9 %collective-permute-start.3 = (f32[56,128]{1,0:T(8,128)S(1)}, f32[56,128]{1,0:T(8,128)S(1)}, u32[]{:S(2)}, u32[]{:S(2)}) collective-permute-start(f32[56,128]{1,0:T(8,128)S(1)} %constant_dynamic-slice_fusion), channel_id=1, source_target_pairs={{0,4},{4,0},{8,12},{12,8},{16,20},{20,16},{24,28},{28,24},{1,5},{5... | collective-permute-start | bytes 86024 | tf_op jit(solution)/shard_map/ppermute | solution.py:303
  4.9 8.5 %collective-permute-start.4 = (f32[224,128]{1,0:T(8,128)S(1)}, f32[224,128]{1,0:T(8,128)S(1)}, u32[]{:S(2)}, u32[]{:S(2)}) collective-permute-start(f32[224,128]{1,0:T(8,128)S(1)} %get-tuple-element.53), channel_id=1, source_target_pairs={{0,1},{1,0},{2,3},{3,2},{4,5},{5,4},{6,7},{7,6},{8,9},{9,8},{10,11... | collective-permute-start | bytes 344072 | tf_op jit(solution)/shard_map/ppermute | solution.py:303
  5.0 8.5 %collective-permute-start.5 = (f32[224,128]{1,0:T(8,128)S(1)}, f32[224,128]{1,0:T(8,128)S(1)}, u32[]{:S(2)}, u32[]{:S(2)}) collective-permute-start(f32[224,128]{1,0:T(8,128)S(1)} %get-tuple-element.55), channel_id=1, source_target_pairs={{0,2},{1,3},{2,0},{3,1},{4,6},{5,7},{6,4},{7,5},{8,10},{9,11},{10,... | collective-permute-start | bytes 344072 | tf_op jit(solution)/shard_map/ppermute | solution.py:303
  6.5 8.8 %collective-permute-start.6 = (f32[224,128]{1,0:T(8,128)S(1)}, f32[224,128]{1,0:T(8,128)S(1)}, u32[]{:S(2)}, u32[]{:S(2)}) collective-permute-start(f32[224,128]{1,0:T(8,128)S(1)} %get-tuple-element.52), channel_id=1, source_target_pairs={{0,3},{1,2},{2,1},{3,0},{4,7},{5,6},{6,5},{7,4},{8,11},{9,10},{10,... | collective-permute-start | bytes 344072 | tf_op jit(solution)/shard_map/ppermute | solution.py:303
  6.8 16.0 %collective-permute-start.1 = (f32[896,128]{1,0:T(8,128)}, f32[896,128]{1,0:T(8,128)S(1)}, u32[]{:S(2)}, u32[]{:S(2)}) collective-permute-start(f32[896,128]{1,0:T(8,128)} %bitcast.30), channel_id=1, source_target_pairs={{0,2},{1,3},{2,0},{3,1},{4,6},{5,7},{6,4},{7,5},{8,10},{9,11},{10,... | collective-permute-start | bytes 1376264 | tf_op jit(solution)/shard_map/ppermute | solution.py:303
  9.8 7.6 %collective-permute-start.7 = (f32[2,56,128]{2,1,0:T(8,128)S(1)}, f32[2,56,128]{2,1,0:T(8,128)S(1)}, u32[]{:S(2)}, u32[]{:S(2)}) collective-permute-start(f32[2,56,128]{2,1,0:T(8,128)S(1)} %pad_maximum_fusion.1), channel_id=1, source_target_pairs={{0,24},{4,28},{8,16},{12,20},{16,8},{20,12},{24,0},{28,4},{1,25},{... | collective-permute-start | bytes 172040 | tf_op jit(solution)/shard_map/ppermute | solution.py:303
  13.4 5.3 %collective-permute-start.8 = (f32[2,56,128]{2,1,0:T(8,128)S(1)}, f32[2,56,128]{2,1,0:T(8,128)S(1)}, u32[]{:S(2)}, u32[]{:S(2)}) collective-permute-start(f32[2,56,128]{2,1,0:T(8,128)S(1)} %pad_maximum_fusion.1), channel_id=1, source_target_pairs={{0,16},{4,20},{8,24},{12,28},{16,0},{20,4},{24,8},{28,12},{1,17},{... | collective-permute-start | bytes 172040 | tf_op jit(solution)/shard_map/ppermute | solution.py:303
  13.4 5.4 %collective-permute-start.9 = (f32[2,56,128]{2,1,0:T(8,128)S(1)}, f32[2,56,128]{2,1,0:T(8,128)S(1)}, u32[]{:S(2)}, u32[]{:S(2)}) collective-permute-start(f32[2,56,128]{2,1,0:T(8,128)S(1)} %pad_maximum_fusion.1), channel_id=1, source_target_pairs={{0,8},{4,12},{8,0},{12,4},{16,24},{20,28},{24,16},{28,20},{1,9},{5... | collective-permute-start | bytes 172040 | tf_op jit(solution)/shard_map/ppermute | solution.py:303
  15.3 24.5 %copy-start.2 = (f32[4,128,128]{2,1,0:T(8,128)S(1)}, f32[4,128,128]{2,1,0:T(8,128)}, u32[]{:S(2)}) copy-start(f32[4,128,128]{2,1,0:T(8,128)} %param.13) | copy-start | bytes 786436
  18.8 21.0 %all-to-all-start = ((f32[32,30,128]{2,1,0:T(8,128)}), f32[32,30,128]{2,1,0:T(8,128)S(1)}, u32[]{:S(2)}, u32[]{:S(2)}) async-start(f32[32,30,128]{2,1,0:T(8,128)} %shard_map.74), calls=%async_computation | async-start | bytes 1048576 | tf_op jit(solution)/shard_map/all_to_all | solution.py:348
  21.6 3.4 %collective-permute-start = (f32[896,128]{1,0:T(8,128)S(1)}, f32[896,128]{1,0:T(8,128)S(1)}, u32[]{:S(2)}, u32[]{:S(2)}) collective-permute-start(f32[896,128]{1,0:T(8,128)S(1)} %bitcast.31), channel_id=1, source_target_pairs={{0,1},{1,0},{2,3},{3,2},{4,5},{5,4},{6,7},{7,6},{8,9},{9,8},{10,11... | collective-permute-start | bytes 1376264 | tf_op jit(solution)/shard_map/ppermute | solution.py:303
  22.8 2.2 %collective-permute-start.2 = (f32[896,128]{1,0:T(8,128)S(1)}, f32[896,128]{1,0:T(8,128)S(1)}, u32[]{:S(2)}, u32[]{:S(2)}) collective-permute-start(f32[896,128]{1,0:T(8,128)S(1)} %collective-permute-done.1.refs_2_), channel_id=1, source_target_pairs={{0,1},{1,0},{2,3},{3,2},{4,5},{5,4},{6,7},{7,6},{8,9},{9,8},{10,11... | collective-permute-start | bytes 1376264 | tf_op jit(solution)/shard_map/ppermute | solution.py:303
  22.8 2.1 %collective-permute-start.10 = (f32[8,56,128]{2,1,0:T(8,128)S(1)}, f32[8,56,128]{2,1,0:T(8,128)S(1)}, u32[]{:S(2)}, u32[]{:S(2)}) collective-permute-start(f32[8,56,128]{2,1,0:T(8,128)S(1)} %constant_dynamic-update-slice_fusion), channel_id=1, source_target_pairs={{0,1},{1,0},{2,3},{3,2},{4,5},{5,4},{6,7},{7,6},{8,9},{9,8},{10,11... | collective-permute-start | bytes 688136 | tf_op jit(solution)/shard_map/ppermute | solution.py:303
  26.4 7.2 %collective-permute-start.11 = (f32[112,128]{1,0:T(8,128)S(1)}, f32[112,128]{1,0:T(8,128)S(1)}, u32[]{:S(2)}, u32[]{:S(2)}) collective-permute-start(f32[112,128]{1,0:T(8,128)S(1)} %get-tuple-element.40), channel_id=1, source_target_pairs={{0,4},{4,0},{8,12},{12,8},{16,20},{20,16},{24,28},{28,24},{1,5},{5... | collective-permute-start | bytes 172040 | tf_op jit(solution)/shard_map/ppermute | solution.py:303
  27.7 9.2 %collective-permute-start.12 = (f32[112,128]{1,0:T(8,128)S(1)}, f32[112,128]{1,0:T(8,128)S(1)}, u32[]{:S(2)}, u32[]{:S(2)}) collective-permute-start(f32[112,128]{1,0:T(8,128)S(1)} %get-tuple-element.41), channel_id=1, source_target_pairs={{0,8},{4,12},{8,0},{12,4},{16,24},{20,28},{24,16},{28,20},{1,9},{5... | collective-permute-start | bytes 172040 | tf_op jit(solution)/shard_map/ppermute | solution.py:303
  29.2 16.3 %collective-permute-start.13 = (f32[112,128]{1,0:T(8,128)S(1)}, f32[112,128]{1,0:T(8,128)S(1)}, u32[]{:S(2)}, u32[]{:S(2)}) collective-permute-start(f32[112,128]{1,0:T(8,128)S(1)} %get-tuple-element.42), channel_id=1, source_target_pairs={{0,16},{4,20},{8,24},{12,28},{16,0},{20,4},{24,8},{28,12},{1,17},{... | collective-permute-start | bytes 172040 | tf_op jit(solution)/shard_map/ppermute | solution.py:303
  31.6 13.9 %collective-permute-start.14 = (f32[112,128]{1,0:T(8,128)S(1)}, f32[112,128]{1,0:T(8,128)S(1)}, u32[]{:S(2)}, u32[]{:S(2)}) collective-permute-start(f32[112,128]{1,0:T(8,128)S(1)} %get-tuple-element.43), channel_id=1, source_target_pairs={{0,20},{4,16},{8,28},{12,24},{16,4},{20,0},{24,12},{28,8},{1,21},{... | collective-permute-start | bytes 172040 | tf_op jit(solution)/shard_map/ppermute | solution.py:303
  32.4 13.1 %collective-permute-start.15 = (f32[112,128]{1,0:T(8,128)S(1)}, f32[112,128]{1,0:T(8,128)S(1)}, u32[]{:S(2)}, u32[]{:S(2)}) collective-permute-start(f32[112,128]{1,0:T(8,128)S(1)} %get-tuple-element.44), channel_id=1, source_target_pairs={{0,12},{4,8},{8,4},{12,0},{16,28},{20,24},{24,20},{28,16},{1,13},{... | collective-permute-start | bytes 172040 | tf_op jit(solution)/shard_map/ppermute | solution.py:303
  33.6 11.9 %collective-permute-start.16 = (f32[112,128]{1,0:T(8,128)S(1)}, f32[112,128]{1,0:T(8,128)S(1)}, u32[]{:S(2)}, u32[]{:S(2)}) collective-permute-start(f32[112,128]{1,0:T(8,128)S(1)} %get-tuple-element.45), channel_id=1, source_target_pairs={{0,24},{4,28},{8,16},{12,20},{16,8},{20,12},{24,0},{28,4},{1,25},{... | collective-permute-start | bytes 172040 | tf_op jit(solution)/shard_map/ppermute | solution.py:303
  36.9 8.6 %collective-permute-start.17 = (f32[112,128]{1,0:T(8,128)S(1)}, f32[112,128]{1,0:T(8,128)S(1)}, u32[]{:S(2)}, u32[]{:S(2)}) collective-permute-start(f32[112,128]{1,0:T(8,128)S(1)} %get-tuple-element.46), channel_id=1, source_target_pairs={{0,28},{4,24},{8,20},{12,16},{16,12},{20,8},{24,4},{28,0},{1,29},{... | collective-permute-start | bytes 172040 | tf_op jit(solution)/shard_map/ppermute | solution.py:303
  52.5 19.8 %all-to-all-start.1 = ((f32[32,28,128]{2,1,0:T(8,128)}), f32[32,28,128]{2,1,0:T(8,128)S(1)}, u32[]{:S(2)}, u32[]{:S(2)}) async-start(f32[32,28,128]{2,1,0:T(8,128)} %shard_map.77), calls=%async_computation.1 | async-start | bytes 1048576 | tf_op jit(solution)/shard_map/all_to_all | solution.py:405
  72.9 2.0 %collective-permute-start.18 = (f32[224,128]{1,0:T(8,128)S(1)}, f32[224,128]{1,0:T(8,128)S(1)}, u32[]{:S(2)}, u32[]{:S(2)}) collective-permute-start(f32[224,128]{1,0:T(8,128)S(1)} %get-tuple-element.51), channel_id=1, source_target_pairs={{0,1},{1,0},{2,3},{3,2},{4,5},{5,4},{6,7},{7,6},{8,9},{9,8},{10,11... | collective-permute-start | bytes 344072 | tf_op jit(solution)/shard_map/ppermute | solution.py:303
  73.0 6.0 %collective-permute-start.19 = (f32[224,128]{1,0:T(8,128)S(1)}, f32[224,128]{1,0:T(8,128)S(1)}, u32[]{:S(2)}, u32[]{:S(2)}) collective-permute-start(f32[224,128]{1,0:T(8,128)S(1)} %get-tuple-element.50), channel_id=1, source_target_pairs={{0,2},{1,3},{2,0},{3,1},{4,6},{5,7},{6,4},{7,5},{8,10},{9,11},{10,... | collective-permute-start | bytes 344072 | tf_op jit(solution)/shard_map/ppermute | solution.py:303
  74.3 6.3 %collective-permute-start.20 = (f32[224,128]{1,0:T(8,128)S(1)}, f32[224,128]{1,0:T(8,128)S(1)}, u32[]{:S(2)}, u32[]{:S(2)}) collective-permute-start(f32[224,128]{1,0:T(8,128)S(1)} %get-tuple-element.49), channel_id=1, source_target_pairs={{0,3},{1,2},{2,1},{3,0},{4,7},{5,6},{6,5},{7,4},{8,11},{9,10},{10,... | collective-permute-start | bytes 344072 | tf_op jit(solution)/shard_map/ppermute | solution.py:303
  80.5 0.8 copy-start.4
